TPU v7x, 32 devices: a whole 2x2x4 slice. The times are simulated.
32 devices in a mesh: section: 2 (over core), dp: 8 (over z, x), tensor: 2 (over y).
Axes of the slice: x: 2, y: 2, z: 4, core: 2. Of those that a mesh axis runs over, the one named last changes fastest.
Arguments:
- hidden: bfloat16 [2, 8, 128, 2048], P(None, 'dp', 'tensor'), may hold values from -6 to 6
- layer_inputs: bfloat16 [2, 2, 8, 128, 256], P('section', None, 'dp', 'tensor'), may hold values from -6 to 6
- span_starts: int32 [2, 8], P(None, 'dp'), may hold values from 0 to 64, as said below
- cotangent: bfloat16 [2, 8, 128, 2048], P(None, 'dp', 'tensor'), may hold values from -6 to 6
- input_gain: bfloat16 [2, 2048], P('section', 'dp'), may hold values from 0.5 to 1.5
- query_weight: bfloat16 [2, 2048, 2048], P('section', 'dp', 'tensor'), may hold values from -0.125 to 0.125
- key_projection: bfloat16 [2, 2048, 512], P('section', 'dp', 'tensor'), may hold values from -0.125 to 0.125
- value_projection: bfloat16 [2, 2048, 512], P('section', 'dp', 'tensor'), may hold values from -0.125 to 0.125
- query_gain: bfloat16 [2, 256], P('section', 'dp'), may hold values from 0.5 to 1.5
- key_norm_gain: bfloat16 [2, 256], P('section', 'dp'), may hold values from 0.5 to 1.5
- output_weight: bfloat16 [2, 2048, 2048], P('section', 'tensor', 'dp'), may hold values from -0.125 to 0.125
- attention_gain: bfloat16 [2, 2048], P('section', 'dp'), may hold values from 0.5 to 1.5
- laurel_left: bfloat16 [2, 2048, 64], P('section', 'dp'), may hold values from -0.125 to 0.125
- laurel_right: bfloat16 [2, 64, 2048], P('section', None, 'dp'), may hold values from -0.75 to 0.75
- laurel_gain: bfloat16 [2, 2048], P('section', 'dp'), may hold values from 0.5 to 1.5
- prefeed_gain: bfloat16 [2, 2048], P('section', 'dp'), may hold values from 0.5 to 1.5
- gate_weight: bfloat16 [2, 2048, 8192], P('section', 'dp', 'tensor'), may hold values from -0.125 to 0.125
- up_weight: bfloat16 [2, 2048, 8192], P('section', 'dp', 'tensor'), may hold values from -0.125 to 0.125
- down_weight: bfloat16 [2, 8192, 2048], P('section', 'tensor', 'dp'), may hold values from -0.0625 to 0.0625
- postfeed_gain: bfloat16 [2, 2048], P('section', 'dp'), may hold values from 0.5 to 1.5
- layer_gate: bfloat16 [2, 2048, 256], P('section', 'dp'), may hold values from -0.125 to 0.125
- layer_project: bfloat16 [2, 256, 2048], P('section', None, 'dp'), may hold values from -0.375 to 0.375
- layer_gain: bfloat16 [2, 2048], P('section', 'dp'), may hold values from 0.5 to 1.5
Outputs:
- activation: bfloat16 [2, 2, 8, 128, 2048], P('section', None, 'dp', 'tensor')
- input_grad: float32 [2, 2, 8, 128, 2048], P('section', None, 'dp', 'tensor')
- layer_input_grad: float32 [2, 2, 8, 128, 256], P('section', None, 'dp', 'tensor')
- grad_input_gain: float32 [2, 2048], P('section', 'dp')
- grad_query_weight: float32 [2, 2048, 2048], P('section', 'dp', 'tensor')
- grad_key_weight: float32 [2, 2048, 512], P('section', 'dp', 'tensor')
- grad_value_weight: float32 [2, 2048, 512], P('section', 'dp', 'tensor')
- grad_query_gain: float32 [2, 256], P('section', 'dp')
- grad_key_gain: float32 [2, 256], P('section', 'dp')
- grad_output_weight: float32 [2, 2048, 2048], P('section', 'tensor', 'dp')
- grad_attention_gain: float32 [2, 2048], P('section', 'dp')
- grad_laurel_left: float32 [2, 2048, 64], P('section', 'dp')
- grad_laurel_right: float32 [2, 64, 2048], P('section', None, 'dp')
- grad_laurel_gain: float32 [2, 2048], P('section', 'dp')
- grad_prefeed_gain: float32 [2, 2048], P('section', 'dp')
- grad_gate_weight: float32 [2, 2048, 8192], P('section', 'dp', 'tensor')
- grad_up_weight: float32 [2, 2048, 8192], P('section', 'dp', 'tensor')
- grad_down_weight: float32 [2, 8192, 2048], P('section', 'tensor', 'dp')
- grad_postfeed_gain: float32 [2, 2048], P('section', 'dp')
- grad_layer_gate: float32 [2, 2048, 256], P('section', 'dp')
- grad_layer_project: float32 [2, 256, 2048], P('section', None, 'dp')
- grad_layer_gain: float32 [2, 2048], P('section', 'dp')
Inputs may be any that keep to these rules, and one draw needn't show every extreme that they name: `span_starts`: each sequence has one image span of 64 positions starting here.
All inputs are finite; a program needn't handle non-finite values.
Results may differ from a plain program's by a relative error of at most 0.033.
Values may be sent and summed in bfloat16 or wider, within the bound.
A program may use at most 320 MiB of HBM per device.

v0:
```python
import math
from types import SimpleNamespace

import jax
import jax.numpy as jnp
from jax import lax
from jax.experimental import pallas as pl
from jax.experimental.pallas import tpu as pltpu
from jax.sharding import PartitionSpec as P

S, D, T = "section", "dp", "tensor"
MESH = pl.DeviceIdType.MESH
BF, F32 = jnp.bfloat16, jnp.float32
HEAD = 256
IMG = 64
EPS = 1e-06
RH = 0.5**0.5
NEG = -1e30
LANES = 128
GELU_C = math.sqrt(2.0 / math.pi)
GELU_K = 0.044715
VMEM_LIMIT = 60 << 20
HALVES = 2


def rms_of(v):
    return lax.rsqrt(jnp.mean(v * v, axis=-1, keepdims=True) + EPS)


def rms_back(v, gain, grad):
    r = rms_of(v)
    unit = v * r
    inner = grad * gain
    back = r * (inner - unit * jnp.mean(inner * unit, axis=-1, keepdims=True))
    return back, jnp.sum(grad * unit, axis=0, keepdims=True)


def plain_back(v, grad):
    r = rms_of(v)
    unit = v * r
    return r * (grad - unit * jnp.mean(grad * unit, axis=-1, keepdims=True))


def gelu(v):
    return 0.5 * v * (1.0 + jnp.tanh(GELU_C * (v + GELU_K * v * v * v)))


def gelu_both(v):
    square = v * v
    th = jnp.tanh(GELU_C * v * (1.0 + GELU_K * square))
    value = 0.5 * v * (1.0 + th)
    slope = 0.5 * (1.0 + th) + 0.5 * v * (1.0 - th * th) * GELU_C * (1.0 + 3.0 * GELU_K * square)
    return value, slope


def rotate(v, cos, sin):
    half = HEAD // 2
    front, back = v[:, :half], v[:, half:]
    return jnp.concatenate([front * cos - back * sin, back * cos + front * sin], axis=-1)


def rotate_back(g, cos, sin):
    half = HEAD // 2
    front, back = g[:, :half], g[:, half:]
    return jnp.concatenate([front * cos + back * sin, back * cos - front * sin], axis=-1)


def nn(x, w):
    return jnp.dot(x, w, preferred_element_type=F32)


def nt(x, w):
    return lax.dot_general(x, w, (((1,), (1,)), ((), ())), preferred_element_type=F32)


def tn(x, w):
    return lax.dot_general(x, w, (((0,), (0,)), ((), ())), preferred_element_type=F32)


def tiles(count, step):
    def wrap(fn):
        def one(j, carry):
            fn(pl.ds(pl.multiple_of(j * step, step), step))
            return carry

        lax.fori_loop(0, count // step, one, 0)

    return wrap


def place(n):
    s, d, t = lax.axis_index(S), lax.axis_index(D), lax.axis_index(T)
    return SimpleNamespace(s=s, d=d, t=t, a=lax.div(d, 2), b=lax.rem(d, 2), n=n, A=n // 2)


def rcopy(src, dst, send, recv, device):
    return pltpu.make_async_remote_copy(
        src_ref=src, dst_ref=dst, send_sem=send, recv_sem=recv, device_id=device, device_id_type=MESH
    )


def rows_of(index, size):
    return pl.ds(pl.multiple_of(index * size, size), size)


class Local:
    def __init__(self, sems):
        self.sems, self.used = sems, 0

    def __call__(self, src, dst):
        copy = pltpu.make_async_copy(src, dst, self.sems.at[self.used])
        self.used += 1
        copy.start()
        return copy


def greet(p, active, partner):
    barrier = pltpu.get_barrier_semaphore()

    def signal(device):
        pl.semaphore_signal(barrier, inc=1, device_id=device, device_id_type=MESH)

    if partner:
        signal((1 - p.s, p.d, p.t))

    @pl.when(active)
    def _():
        signal((p.s, p.d, 1 - p.t))
        signal((p.s, p.a * 2 + 1 - p.b, p.t))

        @pl.when(p.a > 0)
        def _():
            signal((p.s, (p.a - 1) * 2 + p.b, p.t))

        @pl.when(p.a < p.A - 1)
        def _():
            signal((p.s, (p.a + 1) * 2 + p.b, p.t))

    line = 2 + (p.a > 0).astype(jnp.int32) + (p.a < p.A - 1).astype(jnp.int32)
    pl.when(active)(lambda: pl.semaphore_wait(barrier, line + (1 if partner else 0)))
    if partner:
        pl.when(jnp.logical_not(active))(lambda: pl.semaphore_wait(barrier, 1))


def line_gather(p, buf, size, sems, cols=None):
    up_s, up_r, dn_s, dn_r, xs, xr = sems
    A = p.A
    above = (p.s, (p.a + 1) * 2 + p.b, p.t)
    below = (p.s, (p.a - 1) * 2 + p.b, p.t)
    side = (p.s, p.a * 2 + 1 - p.b, p.t)

    def at(col, row):
        return buf.at[col, rows_of(row, size)]

    def up(i, row):
        return rcopy(at(p.b, row), at(p.b, row), up_s.at[i], up_r.at[i], above)

    def down(i, row):
        return rcopy(at(p.b, row), at(p.b, row), dn_s.at[i], dn_r.at[i], below)

    def across(col, row):
        return rcopy(at(col, row), at(col, row), xs.at[row], xr.at[row], side)

    def when(cond, fn):
        pl.when(cond)(fn)

    when(p.a < A - 1, lambda: up(0, p.a).start())
    when(p.a > 0, lambda: down(0, p.a).start())
    across(p.b, p.a).start()
    for i in range(A - 1):

        @pl.when(p.a - 1 - i >= 0)
        def _():
            row = p.a - 1 - i
            up(i, row).wait_recv()
            if i + 1 < A - 1:
                when(p.a < A - 1, lambda: up(i + 1, row).start())
            across(p.b, row).start()

        @pl.when(p.a + 1 + i <= A - 1)
        def _():
            row = p.a + 1 + i
            down(i, row).wait_recv()
            if i + 1 < A - 1:
                when(p.a > 0, lambda: down(i + 1, row).start())
            across(p.b, row).start()

    def arrive():
        for row in range(A):
            across(1 - p.b, row).wait_recv()

    def finish():
        for i in range(A - 1):
            when((p.a < A - 1) & (p.a - i >= 0), lambda: up(i, p.a - i).wait_send())
            when((p.a > 0) & (p.a + i <= A - 1), lambda: down(i, p.a + i).wait_send())
        for row in range(A):
            across(p.b, row).wait_send()

    return arrive, finish


def line_scatter(p, acc, other, got, step_got, size, cuts, sems, out):
    xs, xr, us, ur, ds_, dr = sems
    A = p.A
    above = (p.s, (p.a + 1) * 2 + p.b, p.t)
    below = (p.s, (p.a - 1) * 2 + p.b, p.t)
    side = (p.s, p.a * 2 + 1 - p.b, p.t)

    def cols(h):
        return pl.ds(cuts[h][0], cuts[h][1])

    def across(h):
        return rcopy(other.at[:, cols(h)], got.at[:, cols(h)], xs.at[h], xr.at[h], side)

    def up(h, dest):
        return rcopy(
            other.at[pl.ds(dest * size, size), cols(h)],
            step_got.at[pl.ds(dest * size, size), cols(h)],
            us.at[h, dest],
            ur.at[h, dest],
            above,
        )

    def down(h, dest):
        slot = jnp.where(p.a - 1 == dest, A, dest)
        return rcopy(
            other.at[pl.ds(dest * size, size), cols(h)],
            step_got.at[rows_of(slot, size), cols(h)],
            ds_.at[h, dest],
            dr.at[h, dest],
            below,
        )

    def up_here(h, dest):
        rows = rows_of(dest, size) if not isinstance(dest, int) else pl.ds(dest * size, size)
        return rcopy(other.at[pl.ds(0, size), cols(h)], step_got.at[rows, cols(h)], us.at[h, dest], ur.at[h, dest], above)

    def down_here(h, dest, slot):
        rows = pl.ds(slot * size, size)
        return rcopy(other.at[pl.ds(0, size), cols(h)], step_got.at[rows, cols(h)], ds_.at[h, dest], dr.at[h, dest], below)

    def start(h):
        across(h).start()

    def carry(h):
        across(h).wait()
        for i in range(A - 1):
            hi, lo = A - 1 - i, i

            @pl.when(p.a < hi)
            def _():
                here = (pl.ds(hi * size, size), cols(h))
                total = acc[here] + got[here].astype(F32)
                other[here] = total.astype(BF)

                @pl.when(p.a > 0)
                def _():
                    up_here(h, hi).wait_recv()
                    other[here] = (acc[here] + got[here].astype(F32) + step_got[here].astype(F32)).astype(BF)

                up(h, hi).start()

            @pl.when(p.a > lo)
            def _():
                here = (pl.ds(lo * size, size), cols(h))
                total = acc[here] + got[here].astype(F32)
                other[here] = total.astype(BF)

                @pl.when(p.a < A - 1)
                def _():
                    down_here(h, lo, lo).wait_recv()
                    other[here] = (acc[here] + got[here].astype(F32) + step_got[here].astype(F32)).astype(BF)

                down(h, lo).start()

        mine = (rows_of(p.a, size), cols(h))
        out[:, cols(h)] = acc[mine] + got[mine].astype(F32)

        @pl.when(p.a > 0)
        def _():
            up_here(h, p.a).wait_recv()
            out[:, cols(h)] += step_got[mine].astype(F32)

        @pl.when(p.a < A - 1)
        def _():
            rcopy(
                other.at[pl.ds(0, size), cols(h)],
                step_got.at[pl.ds(A * size, size), cols(h)],
                ds_.at[h, p.a],
                dr.at[h, p.a],
                below,
            ).wait_recv()
            out[:, cols(h)] += step_got[pl.ds(A * size, size), cols(h)].astype(F32)

    def finish(h):
        for dest in range(A):
            pl.when(p.a < dest)(lambda: up(h, dest).wait_send())
            pl.when(p.a > dest)(lambda: down(h, dest).wait_send())

    return start, carry, finish


def dma(*shape):
    return pltpu.SemaphoreType.DMA(shape)


def gather_sems(A):
    return dict(gus=dma(A), gur=dma(A), gds=dma(A), gdr=dma(A), gxs=dma(A), gxr=dma(A))


def scatter_sems(A, parts):
    return dict(
        rxs=dma(parts), rxr=dma(parts), rus=dma(parts, A), rur=dma(parts, A), rds=dma(parts, A), rdr=dma(parts, A)
    )


HBM = pl.BlockSpec(memory_space=pltpu.HBM)
VM = pl.BlockSpec(memory_space=pltpu.VMEM)


def launch(kernel, cid, hbm_in, vmem_in, outs, scratch, kept=None, cost=None):
    kept = kept or {}
    names = [*hbm_in, *vmem_in]
    taken = [name for name in outs if name in kept]
    everything = names + [None] * len(taken) + [*outs, *scratch]

    def run(*refs):
        kernel(SimpleNamespace(**{k: v for k, v in zip(everything, refs) if k}))

    order = list(outs)
    results = pl.pallas_call(
        run,
        out_shape=[jax.ShapeDtypeStruct(*spec) for spec in outs.values()],
        in_specs=[HBM] * len(hbm_in) + [VM] * len(vmem_in) + [HBM] * len(taken),
        out_specs=[HBM] * len(outs),
        scratch_shapes=list(scratch.values()),
        input_output_aliases={len(names) + i: order.index(name) for i, name in enumerate(taken)},
        compiler_params=pltpu.CompilerParams(
            collective_id=cid, has_side_effects=True, vmem_limit_bytes=VMEM_LIMIT
        ),
    )(*hbm_in.values(), *vmem_in.values(), *[kept[name] for name in taken])
    return dict(zip(order, results))


def fetch_kernel(c, o):
    p = place(c.n)
    n, A, R, hb = c.n, c.n // 2, c.R, c.hb
    barrier = pltpu.get_barrier_semaphore()

    def signal(device):
        pl.semaphore_signal(barrier, inc=1, device_id=device, device_id_type=MESH)

    for k in range(1, n):
        signal((p.s, lax.rem(p.d + k, n), p.t))
    signal((p.s, p.d, 1 - p.t))
    signal((1 - p.s, p.d, p.t))
    pl.semaphore_wait(barrier, n + 1)

    @pl.when(p.s == 1)
    def _():
        pl.semaphore_wait(o.go, 1)

    above = (p.s, (p.a + 1) * 2 + p.b, p.t)
    below = (p.s, (p.a - 1) * 2 + p.b, p.t)
    side = (p.s, p.a * 2 + 1 - p.b, p.t)
    pair = (p.s, p.d, 1 - p.t)
    cuts = c.cuts
    local = Local(o.lsem)
    waits = []

    def shard(row, col):
        return rows_of(row * 2 + col, R)

    def piece(row, q, own):
        cs = pl.ds(*cuts[q])
        return o.pack.at[:, cs] if own else o.pk.at[shard(row, p.b), cs]

    def up(i, q, row):
        return rcopy(
            piece(row, q, i == 0), o.pk.at[shard(row, p.b), pl.ds(*cuts[q])], o.gus.at[i, q], o.gur.at[i, q], above
        )

    def down(i, q, row):
        return rcopy(
            piece(row, q, i == 0), o.pk.at[shard(row, p.b), pl.ds(*cuts[q])], o.gds.at[i, q], o.gdr.at[i, q], below
        )

    def across(q, row, own, col):
        return rcopy(
            o.pack.at[:, pl.ds(*cuts[q])] if own else o.pk.at[shard(row, col), pl.ds(*cuts[q])],
            o.pk.at[shard(row, col), pl.ds(*cuts[q])],
            o.gxs.at[row, q],
            o.gxr.at[row, q],
            side,
        )

    ffn = ((o.gate, o.gw), (o.up, o.uw), (o.down, o.dw))

    def block(m, source, half):
        return ffn[m][1].at[rows_of(source, R), rows_of(half, hb)]

    def trade(m, k):
        dest = lax.rem(p.d + k, n)
        return rcopy(
            ffn[m][0].at[:, rows_of(dest, hb)], block(m, p.d, p.t), o.ts.at[k, m], o.tr.at[k, m], (p.s, dest, p.t)
        )

    def came(m, k):
        source = lax.rem(p.d + n - k, n)
        return rcopy(
            ffn[m][0].at[:, rows_of(p.d, hb)], block(m, source, p.t), o.ts.at[k, m], o.tr.at[k, m], side
        )

    def share(m, k, half):
        source = lax.rem(p.d + n - k, n)
        src = ffn[m][0].at[:, rows_of(p.d, hb)] if k == 0 else block(m, source, half)
        return rcopy(src, block(m, source, half), o.ys.at[k, m], o.yr.at[k, m], pair)

    waits.append(local(o.pack, o.pk.at[shard(p.a, p.b)]))
    for m in range(3):
        waits.append(local(ffn[m][0].at[:, rows_of(p.d, hb)], block(m, p.d, p.t)))
        share(m, 0, p.t).start()
    for q in range(len(cuts)):
        pl.when(p.a < A - 1)(lambda: up(0, q, p.a).start())
        pl.when(p.a > 0)(lambda: down(0, q, p.a).start())
        across(q, p.a, True, p.b).start()
    for k in range(1, n):
        for m in range(3):
            trade(m, k).start()
    todo = [(m, k) for k in range(1, n) for m in range(3)]
    steps = [(i, q) for i in range(A - 1) for q in range(len(cuts))]
    share_each = -(-len(todo) // len(steps))
    for i, q in steps:

        @pl.when(p.a - 1 - i >= 0)
        def _():
            row = p.a - 1 - i
            up(i, q, row).wait_recv()
            if i + 1 < A - 1:
                pl.when(p.a < A - 1)(lambda: up(i + 1, q, row).start())
            across(q, row, False, p.b).start()

        @pl.when(p.a + 1 + i <= A - 1)
        def _():
            row = p.a + 1 + i
            down(i, q, row).wait_recv()
            if i + 1 < A - 1:
                pl.when(p.a > 0)(lambda: down(i + 1, q, row).start())
            across(q, row, False, p.b).start()

        for _ in range(min(share_each, len(todo))):
            m, k = todo.pop(0)
            came(m, k).wait_recv()
            share(m, k, p.t).start()
    for m, k in todo:
        came(m, k).wait_recv()
        share(m, k, p.t).start()

    @pl.when(p.s == 0)
    def _():
        pl.semaphore_signal(o.go, inc=1, device_id=(1 - p.s, p.d, p.t), device_id_type=MESH)

    for row in range(A):
        for q in range(len(cuts)):
            across(q, row, False, 1 - p.b).wait_recv()
    for k in range(n):
        for m in range(3):
            share(m, k, 1 - p.t).wait_recv()
    for i, q in steps:
        pl.when((p.a < A - 1) & (p.a - i >= 0))(lambda: up(i, q, p.a - i).wait_send())
        pl.when((p.a > 0) & (p.a + i <= A - 1))(lambda: down(i, q, p.a + i).wait_send())
    for row in range(A):
        for q in range(len(cuts)):
            across(q, row, False, p.b).wait_send()
    for k in range(n):
        for m in range(3):
            if k:
                trade(m, k).wait_send()
            share(m, k, p.t).wait_send()
    for copy in waits:
        copy.wait()
    last = local(o.pk.at[:, pl.ds(c.qkv + c.heads, LANES)], o.gcol)
    last.wait()
    o.grow_v[...] = o.gcol[...].astype(F32).T[c.rank : c.rank + 8]
    last = local(o.grow_v, o.grow)
    last.wait()


def load_weights(c, o, local):
    qn, on = c.qkv, c.heads
    got = [
        local(o.pk.at[:, pl.ds(qn + on, c.small)], o.sm_v),
        local(o.pk.at[:, pl.ds(0, qn)], o.qkv_v),
        local(o.pk.at[:, pl.ds(qn, on)], o.ot_v),
        local(o.gw, o.gw_v),
        local(o.uw, o.uw_v),
        local(o.dw, o.dw_v),
    ]
    return SimpleNamespace(sm=got[0], qkv=got[1], ot=got[2], gw=got[3], uw=got[4], dw=got[5])


def weight_scratch(c):
    return dict(
        sm_v=pltpu.VMEM((c.width, c.small), BF),
        qkv_v=pltpu.VMEM((c.width, c.qkv), BF),
        ot_v=pltpu.VMEM((c.width, c.heads), BF),
        gw_v=pltpu.VMEM((c.width, 2 * c.hb), BF),
        uw_v=pltpu.VMEM((c.width, 2 * c.hb), BF),
        dw_v=pltpu.VMEM((c.width, 2 * c.hb), BF),
    )


LL, LR, LG, LP = (0, 128), (128, 128), (256, 256), (512, 256)


def cols_of(cut):
    return (slice(None), pl.ds(*cut))


def forward_kernel(c, k, o):
    p = place(c.n)
    r, width, hb2 = c.r, c.width, 2 * c.hb
    A = p.A
    m = jnp.clip(k - p.s, 0, 1)
    active = (k - p.s >= 0) & (k - p.s <= 1)
    local = Local(o.lsem)
    pair = (p.s, p.d, 1 - p.t)

    greet(p, active, k >= 1)
    hand = k and rcopy(o.act.at[min(max(k - 1, 0), 1)], o.hid, o.hs.at[0], o.hr.at[0], (1 - p.s, p.d, p.t))
    if k >= 1:
        pl.when(p.s == 0)(hand.start)

    @pl.when(active)
    def _():
        w = load_weights(c, o, local)
        lv_copy = local(o.lin.at[m], o.lv)
        first = pltpu.make_async_copy(o.hidden.at[m], o.hid, o.fsem.at[0])

        @pl.when(p.s == 0)
        def _():
            first.start()
            first.wait()

        if k >= 1:
            pl.when(p.s == 1)(hand.wait_recv)
        mine, theirs = rows_of(p.t, r), rows_of(1 - p.t, r)
        gain = lambda i: o.gains[i : i + 1, :]

        def normed_of():
            x = o.hid[...].astype(F32)
            return x, x * rms_of(x) * gain(0)

        o.nbuf[mine, :] = normed_of()[1].astype(BF)
        send = rcopy(o.nbuf.at[mine], o.nbuf.at[mine], o.ys.at[0], o.yr.at[0], pair)
        send.start()
        w.sm.wait()
        lane = lax.broadcasted_iota(jnp.int32, (r, LANES), 1)
        mid = jnp.where(lane < c.rank, nn(o.nbuf[mine, :], o.sm_v[cols_of(LL)]), 0.0)
        o.lmid_v[...] = mid.astype(BF)
        o.lraw_v[...] = nt(o.lmid_v[...], o.sm_v[cols_of(LR)])
        w.qkv.wait()
        rcopy(o.nbuf.at[theirs], o.nbuf.at[theirs], o.ys.at[0], o.yr.at[0], pair).wait_recv()

        @tiles(c.qkv, 256)
        def _(at):
            o.qraw_v[:, at] = nn(o.nbuf[...], o.qkv_v[:, at])

        cos, sin = o.cos[...], o.sin[...]
        q_gain, k_gain = o.gains[6:7, 0:HEAD], o.gains[7:8, 0:HEAD]
        allowed = o.allowed[m] > 0.5
        kraw = o.qraw_v[:, pl.ds(c.heads, HEAD)]
        vraw = o.qraw_v[:, pl.ds(c.heads + HEAD, HEAD)]
        key = rotate(kraw * rms_of(kraw) * k_gain, cos, sin).astype(BF)
        value = (vraw * rms_of(vraw)).astype(BF)
        for h in range(c.heads // HEAD):
            at = pl.ds(h * HEAD, HEAD)
            raw = o.qraw_v[:, at]
            query = rotate(raw * rms_of(raw) * q_gain, cos, sin).astype(BF)
            scores = jnp.where(allowed, nt(query, key) * HEAD**-0.5, NEG)
            shifted = jnp.exp(scores - jnp.max(scores, axis=-1, keepdims=True))
            prob = shifted / jnp.sum(shifted, axis=-1, keepdims=True)
            o.heads_v[:, at] = nn(prob.astype(BF), value).astype(BF)
        w.ot.wait()

        @tiles(width, 256)
        def _(at):
            o.acc[0 : 2 * r, at] = nt(o.heads_v[...], o.ot_v[at, :])

        o.ysend[...] = o.acc[theirs, :].astype(BF)
        swap = rcopy(o.ysend, o.ygot, o.ys.at[1], o.yr.at[1], pair)
        swap.start()
        swap.wait()
        x, normed = normed_of()
        att = o.acc[mine, :] + o.ygot[...].astype(F32)
        o.att_v[...] = att
        lraw = o.lraw_v[...]
        comb = (x + att * rms_of(att) * gain(1) + normed + lraw * rms_of(lraw) * gain(2)) * RH
        o.comb_v[...] = comb
        o.xbuf[p.b, rows_of(p.a, r), :] = (comb * rms_of(comb) * gain(3)).astype(BF)
        send.wait_send()

        arrive, gathered = line_gather(p, o.xbuf, r, (o.gus, o.gur, o.gds, o.gdr, o.gxs, o.gxr))
        w.gw.wait()
        w.uw.wait()

        def hidden_part(col):
            @tiles(hb2, min(256, hb2))
            def _(at):
                gate = nn(o.xbuf[col], o.gw_v[:, at])
                up = nn(o.xbuf[col], o.uw_v[:, at])
                o.gate_v[col, :, at] = gate
                o.up_v[col, :, at] = up
                o.geglu_v[col, :, at] = (gelu(gate) * up).astype(BF)

        def down_part(col, dest, h):
            start, size = c.halves[h]

            @tiles(size, 256)
            def _(at):
                at = pl.ds(pl.multiple_of(start + at.start, 256), 256)
                dest[:, at] = nt(o.geglu_v[col], o.dw_v[at, :]).astype(dest.dtype)

        hidden_part(p.b)
        arrive()
        hidden_part(1 - p.b)
        w.dw.wait()
        start, carry, finish = line_scatter(
            p, o.acc, o.other, o.got, o.step_got, r, c.halves, (o.rxs, o.rxr, o.rus, o.rur, o.rds, o.rdr), o.down_v
        )
        for h in range(HALVES):
            down_part(1 - p.b, o.other, h)
            start(h)
        for h in range(HALVES):
            down_part(p.b, o.acc, h)
        for h in range(HALVES):
            carry(h)
        down = o.down_v[...]
        resid = o.comb_v[...] + down * rms_of(down) * gain(4)
        o.resid_v[...] = resid
        graw = nn(resid.astype(BF), o.sm_v[cols_of(LG)])
        o.graw_v[...] = graw
        lv_copy.wait()
        o.llow_v[...] = (gelu(graw) * o.lv[...].astype(F32)).astype(BF)
        proj = nt(o.llow_v[...], o.sm_v[cols_of(LP)])
        o.proj_v[...] = proj
        o.act_v[...] = (o.resid_v[...] + proj * rms_of(proj) * gain(5)).astype(BF)
        out = [
            local(o.hid, o.xlow.at[m]),
            local(o.nbuf, o.nfull.at[m]),
            local(o.qraw_v, o.qraw.at[m]),
            local(o.heads_v, o.heads.at[m]),
            local(o.att_v, o.att.at[m]),
            local(o.lmid_v, o.lmid.at[m]),
            local(o.lraw_v, o.lraw.at[m]),
            local(o.comb_v, o.comb.at[m]),
            local(o.xbuf, o.pfull.at[m]),
            local(o.gate_v, o.gate.at[m]),
            local(o.up_v, o.up.at[m]),
            local(o.geglu_v, o.geglu.at[m]),
            local(o.down_v, o.down.at[m]),
            local(o.resid_v, o.resid.at[m]),
            local(o.graw_v, o.graw.at[m]),
            local(o.llow_v, o.llow.at[m]),
            local(o.proj_v, o.proj.at[m]),
            local(o.act_v, o.act.at[m]),
        ]
        gathered()
        for h in range(HALVES):
            finish(h)
        for copy in out:
            copy.wait()

    if k >= 1:
        pl.when(p.s == 0)(hand.wait_send)


def stash_shapes(c):
    m, r, w, q = 2, c.r, c.width, 2 * c.r
    ar, hb2 = c.n // 2 * c.r, 2 * c.hb
    return dict(
        act=((m, r, w), BF),
        xlow=((m, r, w), BF),
        nfull=((m, q, w), BF),
        qraw=((m, q, c.qkv), F32),
        heads=((m, q, c.heads), BF),
        att=((m, r, w), F32),
        lmid=((m, r, LANES), BF),
        lraw=((m, r, w), F32),
        comb=((m, r, w), F32),
        pfull=((m, 2, ar, w), BF),
        gate=((m, 2, ar, hb2), F32),
        up=((m, 2, ar, hb2), F32),
        geglu=((m, 2, ar, hb2), BF),
        down=((m, r, w), F32),
        resid=((m, r, w), F32),
        graw=((m, r, c.per), F32),
        llow=((m, r, c.per), BF),
        proj=((m, r, w), F32),
    )


def scratch_of(shapes):
    return {name + chr(95) + chr(118): pltpu.VMEM(shape[1:], kind) for name, (shape, kind) in shapes.items()}


def line_scratch(c):
    ar = c.n // 2 * c.r
    return dict(
        xbuf=pltpu.VMEM((2, ar, c.width), BF),
        acc=pltpu.VMEM((ar, c.width), F32),
        other=pltpu.VMEM((ar, c.width), BF),
        got=pltpu.VMEM((ar, c.width), BF),
        step_got=pltpu.VMEM((ar + c.r, c.width), BF),
        ysend=pltpu.VMEM((c.r, c.width), BF),
        ygot=pltpu.VMEM((c.r, c.width), BF),
        lsem=dma(40),
        fsem=dma(1),
        hs=dma(1),
        hr=dma(1),
        ys=dma(2),
        yr=dma(2),
        **gather_sems(c.n // 2),
        **scatter_sems(c.n // 2, HALVES),
    )


def forward_tick(c, k, weights, data, tables, stash):
    shapes = stash_shapes(c)
    own = {name: shapes[name] for name in shapes if name not in ("xlow", "nfull", "pfull")}
    scratch = dict(
        hid=pltpu.VMEM((c.r, c.width), BF),
        nbuf=pltpu.VMEM((2 * c.r, c.width), BF),
        lv=pltpu.VMEM((c.r, c.per), BF),
        **scratch_of(own),
        **weight_scratch(c),
        **line_scratch(c),
    )
    return launch(
        lambda o: forward_kernel(c, k, o),
        k,
        dict(**weights, hidden=data.hidden, lin=data.lin),
        tables,
        shapes,
        scratch,
        stash,
    )


def backward_kernel(c, k, o):
    p = place(c.n)
    r, width, hb2 = c.r, c.width, 2 * c.hb
    A = p.A
    m = jnp.clip(2 - k - p.s, 0, 1)
    active = (2 - k - p.s >= 0) & (2 - k - p.s <= 1)
    local = Local(o.lsem)
    pair = (p.s, p.d, 1 - p.t)

    greet(p, active, k >= 1)
    hand = k and rcopy(o.ilow.at[min(max(2 - k, 0), 1)], o.hid, o.hs.at[0], o.hr.at[0], (1 - p.s, p.d, p.t))
    if k >= 1:
        pl.when(p.s == 1)(hand.start)

    @pl.when(active)
    def _():
        mine, theirs = rows_of(p.t, r), rows_of(1 - p.t, r)
        gain = lambda i: o.gains[i : i + 1, :]
        first = pltpu.make_async_copy(o.cot.at[m], o.hid, o.fsem.at[0])
        pl.when(p.s == 1)(first.start)
        need = {}
        need[0] = [local(o.proj.at[m], o.proj_v), local(o.graw.at[m], o.graw_v), local(o.lin.at[m], o.lv)]
        need[1] = [local(o.down.at[m], o.down_v)]
        w = load_weights(c, o, local)
        need[2] = [local(o.gate.at[m], o.gate_v), local(o.up.at[m], o.up_v)]
        need[3] = [local(o.comb.at[m], o.comb_v), local(o.att.at[m], o.att_v), local(o.lraw.at[m], o.lraw_v)]
        need[4] = [local(o.xlow.at[m], o.xlow_v), local(o.qraw.at[m], o.qraw_v)]

        def have(i):
            for copy in need[i]:
                copy.wait()

        pl.when(p.s == 1)(first.wait)
        if k >= 1:
            pl.when(p.s == 0)(hand.wait_recv)
        have(0)
        o.ggr_v[...] = jnp.zeros_like(o.ggr_v)
        dres = o.hid[...].astype(F32)
        dproj, o.ggr_v[5:6, :] = rms_back(o.proj_v[...], gain(5), dres)
        o.plow_v[...] = dproj.astype(BF)
        w.sm.wait()
        dmid = nn(o.plow_v[...], o.sm_v[cols_of(LP)])
        value, slope = gelu_both(o.graw_v[...])
        o.lgrad_v[...] = value * dmid
        o.grlow_v[...] = (dmid * o.lv[...].astype(F32) * slope).astype(BF)
        dres = o.hid[...].astype(F32) + nt(o.grlow_v[...], o.sm_v[cols_of(LG)])
        o.dcomb_v[...] = dres
        have(1)
        ddown, o.ggr_v[4:5, :] = rms_back(o.down_v[...], gain(4), dres)
        o.xbuf[p.b, rows_of(p.a, r), :] = ddown.astype(BF)
        arrive, gathered = line_gather(p, o.xbuf, r, (o.gus, o.gur, o.gds, o.gdr, o.gxs, o.gxr))
        w.dw.wait()
        have(2)

        def hidden_part(col):
            @tiles(hb2, min(256, hb2))
            def _(at):
                dgeglu = nn(o.xbuf[col], o.dw_v[:, at])
                value, slope = gelu_both(o.gate_v[col, :, at])
                o.dul_v[col, :, at] = (dgeglu * value).astype(BF)
                o.dgl_v[col, :, at] = (dgeglu * o.up_v[col, :, at] * slope).astype(BF)

        def down_part(col, dest, h):
            start, size = c.halves[h]

            @tiles(size, 256)
            def _(at):
                at = pl.ds(pl.multiple_of(start + at.start, 256), 256)
                part = nt(o.dgl_v[col], o.gw_v[at, :]) + nt(o.dul_v[col], o.uw_v[at, :])
                dest[:, at] = part.astype(dest.dtype)

        hidden_part(p.b)
        arrive()
        hidden_part(1 - p.b)
        w.gw.wait()
        w.uw.wait()
        start, carry, finish = line_scatter(
            p, o.acc, o.other, o.got, o.step_got, r, c.halves, (o.rxs, o.rxr, o.rus, o.rur, o.rds, o.rdr), o.down_v
        )
        for h in range(HALVES):
            down_part(1 - p.b, o.other, h)
            start(h)
        for h in range(HALVES):
            down_part(p.b, o.acc, h)
        for h in range(HALVES):
            carry(h)
        have(3)
        dcomb, o.ggr_v[3:4, :] = rms_back(o.comb_v[...], gain(3), o.down_v[...])
        even = (o.dcomb_v[...] + dcomb) * RH
        o.dcomb_v[...] = even
        datt, o.ggr_v[1:2, :] = rms_back(o.att_v[...], gain(1), even)
        o.abuf[mine, :] = datt.astype(BF)
        send = rcopy(o.abuf.at[mine], o.abuf.at[mine], o.ys.at[0], o.yr.at[0], pair)
        send.start()
        dlraw, o.ggr_v[2:3, :] = rms_back(o.lraw_v[...], gain(2), o.dcomb_v[...])
        o.lrlow_v[...] = dlraw.astype(BF)
        o.lmg_v[...] = nn(o.lrlow_v[...], o.sm_v[cols_of(LR)]).astype(BF)
        o.proj_v[...] = o.dcomb_v[...] + nt(o.lmg_v[...], o.sm_v[cols_of(LL)])
        w.ot.wait()
        rcopy(o.abuf.at[theirs], o.abuf.at[theirs], o.ys.at[0], o.yr.at[0], pair).wait_recv()

        @tiles(c.heads, 256)
        def _(at):
            o.hgrad_v[:, at] = nn(o.abuf[...], o.ot_v[:, at]).astype(BF)

        have(4)
        cos, sin = o.cos[...], o.sin[...]
        q_gain, k_gain = o.gains[6:7, 0:HEAD], o.gains[7:8, 0:HEAD]
        allowed = o.allowed[m] > 0.5
        k_at, v_at = pl.ds(c.heads, HEAD), pl.ds(c.heads + HEAD, HEAD)
        kraw, vraw = o.qraw_v[:, k_at], o.qraw_v[:, v_at]
        key = rotate(kraw * rms_of(kraw) * k_gain, cos, sin).astype(BF)
        value = (vraw * rms_of(vraw)).astype(BF)
        dkey = jnp.zeros(kraw.shape, F32)
        dvalue = jnp.zeros(vraw.shape, F32)
        dq_gain = jnp.zeros((1, HEAD), F32)
        for h in range(c.heads // HEAD):
            at = pl.ds(h * HEAD, HEAD)
            raw = o.qraw_v[:, at]
            query = rotate(raw * rms_of(raw) * q_gain, cos, sin).astype(BF)
            scores = jnp.where(allowed, nt(query, key) * HEAD**-0.5, NEG)
            shifted = jnp.exp(scores - jnp.max(scores, axis=-1, keepdims=True))
            prob = shifted / jnp.sum(shifted, axis=-1, keepdims=True)
            hgrad = o.hgrad_v[:, at]
            dprob = nt(hgrad, value)
            dvalue = dvalue + tn(prob.astype(BF), hgrad)
            inner = jnp.sum(prob * dprob, axis=-1, keepdims=True)
            dscore = (prob * (dprob - inner)).astype(BF)
            dquery = nn(dscore, key) * HEAD**-0.5
            dkey = dkey + tn(dscore, query) * HEAD**-0.5
            draw, dg = rms_back(raw, q_gain, rotate_back(dquery, cos, sin))
            dq_gain = dq_gain + dg
            o.dqkv_v[:, at] = draw.astype(BF)
        draw, dk_gain = rms_back(kraw, k_gain, rotate_back(dkey, cos, sin))
        o.dqkv_v[:, k_at] = draw.astype(BF)
        o.dqkv_v[:, v_at] = plain_back(vraw, dvalue).astype(BF)
        o.ggr_v[6:7, 0:HEAD] = dq_gain
        o.ggr_v[7:8, 0:HEAD] = dk_gain
        w.qkv.wait()

        @tiles(width, 256)
        def _(at):
            o.acc[0 : 2 * r, at] = nt(o.dqkv_v[...], o.qkv_v[at, :])

        o.ysend[...] = o.acc[theirs, :].astype(BF)
        swap = rcopy(o.ysend, o.ygot, o.ys.at[1], o.yr.at[1], pair)
        swap.start()
        swap.wait()
        dnorm = o.proj_v[...] + o.acc[mine, :] + o.ygot[...].astype(F32)
        dx, o.ggr_v[0:1, :] = rms_back(o.xlow_v[...].astype(F32), gain(0), dnorm)
        dx = dx + o.dcomb_v[...]
        o.igrad_v[...] = dx
        o.ilow_v[...] = dx.astype(BF)
        send.wait_send()
        out = [
            local(o.igrad_v, o.igrad.at[m]),
            local(o.ilow_v, o.ilow.at[m]),
            local(o.lgrad_v, o.lgrad.at[m]),
            local(o.plow_v, o.plow.at[m]),
            local(o.grlow_v, o.grlow.at[m]),
            local(o.xbuf, o.dfull.at[m]),
            local(o.dgl_v, o.dgl.at[m]),
            local(o.dul_v, o.dul.at[m]),
            local(o.lrlow_v, o.lrlow.at[m]),
            local(o.lmg_v, o.lmg.at[m]),
            local(o.abuf, o.afull.at[m]),
            local(o.dqkv_v, o.dqkv.at[m]),
            local(o.ggr_v, o.ggr.at[m]),
        ]
        gathered()
        for h in range(HALVES):
            finish(h)
        for copy in out:
            copy.wait()

    if k >= 1:
        pl.when(p.s == 1)(hand.wait_send)


def grad_shapes(c):
    m, r, w, q = 2, c.r, c.width, 2 * c.r
    ar, hb2 = c.n // 2 * c.r, 2 * c.hb
    return dict(
        igrad=((m, r, w), F32),
        ilow=((m, r, w), BF),
        lgrad=((m, r, c.per), F32),
        plow=((m, r, w), BF),
        grlow=((m, r, c.per), BF),
        dfull=((m, 2, ar, w), BF),
        dgl=((m, 2, ar, hb2), BF),
        dul=((m, 2, ar, hb2), BF),
        lrlow=((m, r, w), BF),
        lmg=((m, r, LANES), BF),
        afull=((m, q, w), BF),
        dqkv=((m, q, c.qkv), BF),
        ggr=((m, 8, w), F32),
    )


READ = ("proj", "graw", "down", "gate", "up", "comb", "att", "lraw", "xlow", "qraw")


def backward_tick(c, k, weights, data, tables, stash, grads):
    shapes = grad_shapes(c)
    kept_shapes = stash_shapes(c)
    own = {name: shapes[name] for name in shapes if name not in ("dfull", "afull")}
    scratch = dict(
        hid=pltpu.VMEM((c.r, c.width), BF),
        abuf=pltpu.VMEM((2 * c.r, c.width), BF),
        lv=pltpu.VMEM((c.r, c.per), BF),
        dcomb_v=pltpu.VMEM((c.r, c.width), F32),
        hgrad_v=pltpu.VMEM((2 * c.r, c.heads), BF),
        **scratch_of(own),
        **scratch_of({name: kept_shapes[name] for name in READ}),
        **weight_scratch(c),
        **line_scratch(c),
    )
    return launch(
        lambda o: backward_kernel(c, k, o),
        3 + k,
        dict(**weights, cot=data.cot, lin=data.lin, **{name: stash[name] for name in READ}),
        tables,
        shapes,
        scratch,
        grads,
    )


def return_kernel(c, o):
    p = place(c.n)
    n, A, R, hb = c.n, c.n // 2, c.R, c.hb
    pair = (p.s, p.d, 1 - p.t)
    side = (p.s, p.a * 2 + 1 - p.b, p.t)
    barrier = pltpu.get_barrier_semaphore()

    def signal(device):
        pl.semaphore_signal(barrier, inc=1, device_id=device, device_id_type=MESH)

    for k in range(1, n):
        signal((p.s, lax.rem(p.d + k, n), p.t))
    signal(pair)
    pl.semaphore_wait(barrier, n)
    local = Local(o.lsem)
    ffn = (o.dg, o.du, o.dd)

    def swap(m, k):
        dest = lax.rem(p.d + k, n)
        return rcopy(
            ffn[m].at[rows_of(dest, R), rows_of(1 - p.t, hb)],
            o.fgot.at[m, rows_of(dest, R)],
            o.ys.at[m, k],
            o.yr.at[m, k],
            pair,
        )

    def trade(m, k):
        dest = lax.rem(p.d + k, n)
        return rcopy(
            o.fown.at[m, rows_of(dest, R)], o.gf.at[m, :, rows_of(p.d, hb)], o.ts.at[m, k], o.tr.at[m, k], (p.s, dest, p.t)
        )

    def came(m, k):
        source = lax.rem(p.d + n - k, n)
        return rcopy(
            o.fown.at[m, rows_of(p.d, R)], o.gf.at[m, :, rows_of(source, hb)], o.ts.at[m, k], o.tr.at[m, k], side
        )

    attn = (o.dqkv, o.dot, o.dsm)
    loads = []
    for row in range(A):
        for q, part in enumerate(attn):
            cs = pl.ds(*c.parts[q])
            loads.append(local(part.at[rows_of(row * 2 + 1 - p.b, R)], o.other.at[pl.ds(row * R, R), cs]))
            loads.append(local(part.at[rows_of(row * 2 + p.b, R)], o.acc.at[pl.ds(row * R, R), cs]))
    owns = [local(ffn[m].at[:, rows_of(p.t, hb)], o.fown.at[m]) for m in range(3)]
    for m in range(3):
        for k in [*range(1, n), 0]:
            swap(m, k).start()
    for copy in loads:
        copy.wait()
    start, carry, finish = line_scatter(
        p, o.acc, o.other, o.got, o.step_got, R, c.parts, (o.rxs, o.rxr, o.rus, o.rur, o.rds, o.rdr), o.gp_v
    )
    for q in range(len(c.parts)):
        start(q)
    mine_copies = []
    for q in range(max(len(c.parts), 3)):
        if q < 3:
            owns[q].wait()
            for k in [*range(1, n), 0]:
                rows = rows_of(lax.rem(p.d + k, n), R)
                swap(q, k).wait_recv()
                total = o.fown[q, rows, :].astype(F32) + o.fgot[q, rows, :].astype(F32)
                o.fown[q, rows, :] = total.astype(BF)
                if k:
                    trade(q, k).start()
                else:
                    mine_copies.append(local(o.fown.at[q, rows], o.gf.at[q, :, rows_of(p.d, hb)]))
        if q < len(c.parts):
            carry(q)
    shared = pl.ds(c.qkv + c.heads, c.small)
    o.ssend[...] = o.gp_v[:, shared].astype(BF)
    last = rcopy(o.ssend, o.sgot, o.ss.at[0], o.sr.at[0], pair)
    last.start()
    last.wait()
    o.gp_v[:, shared] += o.sgot[...].astype(F32)
    out = local(o.gp_v, o.gp)
    for m in range(3):
        for k in range(n):
            swap(m, k).wait_send()
            if k:
                came(m, k).wait_recv()
                trade(m, k).wait_send()
    for q in range(len(c.parts)):
        finish(q)
    for copy in [*mine_copies, out]:
        copy.wait()


def fetch_weights(c, pack, gate, up, down):
    n, A, q = c.n, c.n // 2, len(c.cuts)
    outs = dict(
        pk=((c.width, c.total), BF),
        gw=((c.width, 2 * c.hb), BF),
        uw=((c.width, 2 * c.hb), BF),
        dw=((c.width, 2 * c.hb), BF),
        grow=((8, c.width), F32),
    )
    scratch = dict(
        gcol=pltpu.VMEM((c.width, LANES), BF),
        grow_v=pltpu.VMEM((8, c.width), F32),
        gus=dma(A, q), gur=dma(A, q), gds=dma(A, q), gdr=dma(A, q), gxs=dma(A, q), gxr=dma(A, q),
        ts=dma(n, 3), tr=dma(n, 3), ys=dma(n, 3), yr=dma(n, 3), lsem=dma(6),
        go=pltpu.SemaphoreType.REGULAR,
    )
    return launch(
        lambda o: fetch_kernel(c, o), 6, dict(pack=pack, gate=gate, up=up, down=down), {}, outs, scratch
    )


def return_grads(c, dqkv, dot, dsm, dg, du, dd):
    n, A = c.n, c.n // 2
    R = c.R
    outs = dict(gp=((R, c.total), F32), gf=((3, R, n * c.hb), BF))
    scratch = dict(
        acc=pltpu.VMEM((A * R, c.total), BF),
        other=pltpu.VMEM((A * R, c.total), BF),
        got=pltpu.VMEM((A * R, c.total), BF),
        step_got=pltpu.VMEM((A * R + R, c.total), BF),
        gp_v=pltpu.VMEM((R, c.total), F32),
        fown=pltpu.VMEM((3, c.width, c.hb), BF),
        fgot=pltpu.VMEM((3, c.width, c.hb), BF),
        ssend=pltpu.VMEM((R, c.small), BF),
        sgot=pltpu.VMEM((R, c.small), BF),
        ys=dma(3, n), yr=dma(3, n), ts=dma(3, n), tr=dma(3, n), ss=dma(1), sr=dma(1), lsem=dma(6 * A + 8),
        **scatter_sems(A, len(c.parts)),
    )
    return launch(lambda o: return_kernel(c, o), 7, dict(dqkv=dqkv, dot=dot, dsm=dsm, dg=dg, du=du, dd=dd), {}, outs, scratch)


def spread(gain, n, rows):
    return jnp.pad(gain, (0, rows - gain.shape[0]))


def body(
    hidden, layer_inputs, span_starts, cotangent, input_gain, query_weight, key_projection, value_projection,
    query_gain, key_norm_gain, output_weight, attention_gain, laurel_left, laurel_right, laurel_gain, prefeed_gain,
    gate_weight, up_weight, down_weight, postfeed_gain, layer_gate, layer_project, layer_gain,
):
    n, nt_ = lax.axis_size(D), lax.axis_size(T)
    t = lax.axis_index(T)
    rank = laurel_left.shape[2]
    width = hidden.shape[3]
    R = width // n
    heads = query_weight.shape[2]
    qkv = heads + 2 * HEAD
    per = layer_gate.shape[2]
    small = 2 * LANES + 2 * per
    c = SimpleNamespace(
        n=n, R=R, r=hidden.shape[2], width=width, heads=heads, qkv=qkv, per=per, small=small, rank=rank,
        total=qkv + heads + small, hb=gate_weight.shape[2] // n,
        cuts=((0, qkv), (qkv, heads), (qkv + heads, small)),
        parts=((0, qkv), (qkv, heads), (qkv + heads, small)),
        halves=tuple((h * width // HALVES, width // HALVES) for h in range(HALVES)),
    )
    gains = jnp.stack(
        [
            input_gain[0], attention_gain[0], laurel_gain[0], prefeed_gain[0], postfeed_gain[0], layer_gain[0],
            spread(query_gain[0], n, R), spread(key_norm_gain[0], n, R),
        ],
        axis=1,
    )
    pad = lambda v, k: jnp.pad(v, ((0, 0), (0, LANES - k)))
    pack = jnp.concatenate(
        [
            query_weight[0], key_projection[0], value_projection[0], output_weight[0].T,
            pad(jnp.concatenate([laurel_left[0], gains], axis=1), rank + 8), pad(laurel_right[0].T, rank),
            layer_gate[0], layer_project[0].T,
        ],
        axis=1,
    )
    weights = fetch_weights(c, pack, gate_weight[0], up_weight[0], down_weight[0].T)
    columns = weights.pop("grow")
    short = HEAD // n
    head_gains = columns[6:].reshape(2, n, R)[:, :, :short].reshape(2, HEAD)
    gain_rows = jnp.concatenate([columns[:6], jnp.pad(head_gains, ((0, 0), (0, width - HEAD)))], axis=0)

    span = c.r * nt_
    position = jnp.arange(span, dtype=jnp.int32)
    begin = span_starts[:, 0][:, None]
    inside = (position[None] >= begin) & (position[None] < begin + IMG)
    allowed = (position[None, :] <= position[:, None])[None] | (inside[:, :, None] & inside[:, None, :])
    half = HEAD // 2
    frequency = jnp.exp(jnp.arange(half, dtype=F32) * (-2.0 * math.log(10000.0) / HEAD))
    angles = jnp.arange(span, dtype=F32)[:, None] * frequency[None, :]
    tables = dict(gains=gain_rows, cos=jnp.cos(angles), sin=jnp.sin(angles), allowed=allowed.astype(F32))
    data = SimpleNamespace(hidden=hidden[:, 0], lin=layer_inputs[0, :, 0], cot=cotangent[:, 0])

    stash, grads = None, None
    for k in range(3):
        stash = forward_tick(c, k, weights, data, tables, stash)
    for k in range(3):
        grads = backward_tick(c, k, weights, data, tables, stash, grads)
    f, g = SimpleNamespace(**stash), SimpleNamespace(**grads)

    def pair_grad(inputs, outs):
        inputs = inputs.reshape(-1, inputs.shape[-1])
        return tn(inputs, outs.reshape(-1, outs.shape[-1])).astype(BF)

    nlow = lax.dynamic_slice_in_dim(f.nfull, t * c.r, c.r, axis=1)
    sums = g.ggr[0] + g.ggr[1]
    head_sums = jnp.pad(sums[6:, :HEAD].reshape(2, n, short), ((0, 0), (0, 0), (0, R - short))).reshape(2, width)
    gain_cols = jnp.concatenate([sums[:6], head_sums], axis=0).T.astype(BF)
    left = pair_grad(nlow, g.lmg)
    left = jnp.concatenate([left[:, :rank], gain_cols, left[:, rank + 8 :]], axis=1)
    dsm = jnp.concatenate(
        [left, pair_grad(g.lrlow, f.lmid), pair_grad(f.resid.astype(BF), g.grlow), pair_grad(g.plow, f.llow)], axis=1
    )
    done = return_grads(
        c, pair_grad(f.nfull, g.dqkv), pair_grad(g.afull, f.heads), dsm,
        pair_grad(f.pfull, g.dgl), pair_grad(f.pfull, g.dul), pair_grad(g.dfull, f.geglu),
    )
    gp, gf = done["gp"], done["gf"].astype(F32)
    base = qkv + heads
    gain_out = gp[:, base + rank : base + rank + 8].T
    one = lambda i: gain_out[i][None]
    return (
        f.act[None, :, None],
        g.igrad[None, :, None],
        g.lgrad[None, :, None],
        one(0),
        gp[:, :heads][None],
        gp[:, heads : heads + HEAD][None],
        gp[:, heads + HEAD : qkv][None],
        gain_out[6, :short][None],
        gain_out[7, :short][None],
        gp[:, qkv:base].T[None],
        one(1),
        gp[:, base : base + rank][None],
        gp[:, base + LANES : base + LANES + rank].T[None],
        one(2),
        one(3),
        gf[0][None],
        gf[1][None],
        gf[2].T[None],
        one(4),
        gp[:, base + 2 * LANES : base + 2 * LANES + per][None],
        gp[:, base + 2 * LANES + per :].T[None],
        one(5),
    )


def solution(mesh):
    rows, cols = P(S, D, T), P(S, T, D)
    vec, tall, flat = P(S, D), P(S, D, None), P(S, None, D)
    seq, out = P(None, D, T, None), P(S, None, D, T, None)
    weights = (
        vec, rows, rows, rows, vec, vec, cols, vec, tall, flat, vec, vec, rows, rows, cols, vec, tall, flat, vec,
    )
    return jax.shard_map(
        body,
        mesh=mesh,
        in_specs=(seq, out, P(None, D), seq, *weights),
        out_specs=(out, out, out, *weights),
        check_vma=False,
    )
```

profile of v0, /device:TPU:0, one launch (start us, length us, event | category | flops | bytes accessed | tf_op | source)
XLA Modules:
  0.0 1093.5 jit_solution(17214352912195567638)
XLA Ops:
  0.8 1.2 bitcast_dynamic-update-slice_fusion.1
  3.8 1.2 copy.177
  7.0 4.6 copy.189
  11.6 154.5 %shard_map.393 = (bf16[2048,3328]{1,0:T(8,128)(2,1)}, bf16[2048,1024]{1,0:T(8,128)(2,1)}, bf16[2048,1024]{1,0:T(8,128)(2,1)}, bf16[2048,1024]{1,0:T(8,128)(2,1)}, f32[8,2048]{1,0:T(8,128)}) custom-call(bf16[256,3328]{1,0:T(8,128)(2,1)} %copy-done.14, bf16[256,4096]{1,0:T(8,128)(2,1)} %bitcast.157, bf16[256,4096]{1,0:T(8,128)(2,1)} %bitcast.158, ...), custom_call_target="tpu_custom_call" | custom-call | tf_op jit(solution)/shard_map/pallas_call | solution.py:331
  167.1 1.5 select_maximum_fusion.refs_6_.refs_16_
  170.4 132.1 %shard_map.394 = (bf16[2,64,2048]{2,1,0:T(8,128)(2,1)}, bf16[2,64,2048]{2,1,0:T(8,128)(2,1)}, bf16[2,128,2048]{2,1,0:T(8,128)(2,1)}, f32[2,128,1536]{2,1,0:T(8,1...) custom-call(bf16[2048,3328]{1,0:T(8,128)(2,1)} %get-tuple-element.12, ...), custom_call_target="tpu_custom_call" | custom-call | tf_op jit(solution)/shard_map/pallas_call | solution.py:331
  302.5 105.1 %shard_map.395 = (bf16[2,64,2048]{2,1,0:T(8,128)(2,1)}, bf16[2,64,2048]{2,1,0:T(8,128)(2,1)}, bf16[2,128,2048]{2,1,0:T(8,128)(2,1)}, f32[2,128,1536]{2,1,0:T(8,1...) custom-call(bf16[2048,3328]{1,0:T(8,128)(2,1)} %get-tuple-element.12, ...), custom_call_target="tpu_custom_call", output_to_operand_aliasing={{0}: (10, {}), {1}: (11, {}), {2}: (12, {}), {3}: (13, {}),... | custom-call | tf_op jit(solution)/shard_map/pallas_call | solution.py:331
  407.5 3.4 shard_map.396
  411.0 8.8 shard_map.397
  419.8 255.3 %shard_map.398 = (f32[2,64,2048]{2,1,0:T(8,128)}, bf16[2,64,2048]{2,1,0:T(8,128)(2,1)}, f32[2,64,256]{2,1,0:T(8,128)}, bf16[2,64,2048]{2,1,0:T(8,128)(2,1)}, bf1...) custom-call(bf16[2048,3328]{1,0:T(8,128)(2,1)} %get-tuple-element.12, ...), custom_call_target="tpu_custom_call", output_to_operand_aliasing={{0}: (20, {}), {1}: (21, {}), {2}: (22, {}), {3}: (23, {}),... | custom-call | tf_op jit(solution)/shard_map/pallas_call | solution.py:331
  675.1 116.9 %shard_map.399 = (f32[2,64,2048]{2,1,0:T(8,128)}, bf16[2,64,2048]{2,1,0:T(8,128)(2,1)}, f32[2,64,256]{2,1,0:T(8,128)}, bf16[2,64,2048]{2,1,0:T(8,128)(2,1)}, bf1...) custom-call(bf16[2048,3328]{1,0:T(8,128)(2,1)} %get-tuple-element.12, ...), custom_call_target="tpu_custom_call", output_to_operand_aliasing={{0}: (20, {}), {1}: (21, {}), {2}: (22, {}), {3}: (23, {}),... | custom-call | tf_op jit(solution)/shard_map/pallas_call | solution.py:331
  792.0 8.6 bitcast_convert_fusion.1.refs_5_
  800.6 6.2 bitcast_convert_fusion.2.refs_4_
  806.8 6.2 bitcast_convert_fusion.3.refs_3_
  813.1 1.4 fusion.1
  814.5 1.4 fusion
  816.0 1.1 fusion.3
  817.3 1.0 copy.193
  818.7 1.0 slice.126
  819.7 7.0 concatenate.20.refs_2_
  826.8 3.3 bitcast_convert_fusion.4.refs_1_
  830.1 4.5 bitcast_convert_fusion.refs_0_
  834.6 222.3 %shard_map.400 = (f32[256,3328]{1,0:T(8,128)}, bf16[3,256,4096]{2,1,0:T(8,128)(2,1)}) custom-call(bf16[2048,1536]{1,0:T(8,128)(2,1)} %bitcast_convert_fusion.refs_0_, bf16[2048,1024]{1,0:T(8,128)(2,1)} %bitcast_convert_fusion.4.refs_1_, bf16[2048,768]{1,0:T(8,128)(2,1)} %concatenate.20.refs_2_, bf16[2048,1024]{1,0:T(8,128)(2,1)} %bitcast_convert_fusion.3.refs_3_, ...), custom_call_target="tpu_custom_call" | custom-call | tf_op jit(solution)/shard_map/pallas_call | solution.py:331
  1056.9 4.5 convert_element_type.63
  1061.4 2.3 slice_bitcast_fusion
  1063.7 5.6 copy.212
  1069.3 6.9 fusion.9
  1076.2 1.3 slice_bitcast_fusion.1
  1077.4 1.3 copy.206
  1078.8 2.2 slice_bitcast_fusion.3
  1081.8 1.0 slice_bitcast_fusion.9
  1086.9 1.0 slice_bitcast_fusion.7
  (124 shorter events, 17.0 us)
Async XLA Ops:
  0.7 4.4 copy-start.31
  0.7 4.5 copy-start.32
  0.7 4.7 copy-start.23
  0.7 4.8 copy-start.25
  0.7 4.9 copy-start.26
  0.7 5.1 copy-start.27
  0.7 5.2 copy-start.28
  0.7 5.3 copy-start.29
  0.7 5.5 copy-start.30
  0.8 5.9 copy-start.24
  0.8 6.1 copy-start.21
  0.8 6.1 copy-start.22
  7.0 4.6 copy-start.14
  11.6 157.9 %copy-start.33 = (s32[2,1]{0,1:T(1,128)S(1)}, s32[2,1]{0,1:T(1,128)}, u32[]{:S(2)}) copy-start(s32[2,1]{0,1:T(1,128)} %param.25) | copy-start | bytes 28
  675.1 116.9 %copy-start.5 = (bf16[2,2,256,1024]{3,2,1,0:T(8,128)(2,1)S(1)}, bf16[2,2,256,1024]{3,2,1,0:T(8,128)(2,1)}, u32[]{:S(2)}) copy-start(bf16[2,2,256,1024]{3,2,1,0:T(8,128)(2,1)} %get-tuple-element.217) | copy-start | bytes 6291460
  792.0 8.6 copy-start
  792.0 8.6 copy-start.7
  800.6 6.2 copy-start.6
  806.8 6.3 copy-start.10
  806.8 6.3 copy-start.17
  806.8 7.7 copy-start.3
  806.8 7.7 copy-start.18
  813.1 4.1 copy-start.15
  813.1 5.3 copy-start.1
  813.1 5.3 copy-start.19
  819.7 7.1 copy-start.2
  819.7 7.1 copy-start.9
  826.8 3.3 copy-start.8
  1069.3 6.9 copy-start.13
  1078.8 11.8 %copy-start.11 = (bf16[2,64,2048]{2,1,0:T(8,128)(2,1)S(1)}, bf16[2,64,2048]{2,1,0:T(8,128)(2,1)}, u32[]{:S(2)}) copy-start(bf16[2,64,2048]{2,1,0:T(8,128)(2,1)} %get-tuple-element.162) | copy-start | bytes 1572868
  1078.8 12.6 %copy-start.4 = (f32[2,64,2048]{2,1,0:T(8,128)S(1)}, f32[2,64,2048]{2,1,0:T(8,128)}, u32[]{:S(2)}) copy-start(f32[2,64,2048]{2,1,0:T(8,128)} %get-tuple-element.199) | copy-start | bytes 3145732
  1081.8 10.6 copy-start.16
  (2 other events, 5.8 us)
where the time goes:
time: 1100 us; the launch traced here: 1090 us
  Pallas kernels  998 us (91%)
  local copies, waits for them, and re-layouts  52.4 us (5%)
  matrix products  33.2 us (3%)
    pallas_call x8, Pallas kernels, launch(): pl.pallas_call(run, out_shape=[jax.ShapeDtypeStruct(*spec) for spec in ou...  998 us
    dot_general x9, matrix products, tn(): lax.dot_general(x, w, (((0,), (0,)), ((), ())), preferred_element_type=F32)  33.2 us
    unnamed x99, local copies, waits for them, and re-layouts  26.1 us

commit v1 on v0

--- a/solution.py
+++ b/solution.py
@@ -21,6 +21,7 @@
 GELU_K = 0.044715
 VMEM_LIMIT = 60 << 20
 HALVES = 2
+GATHER_PARTS = 2
 
 
 def rms_of(v):
@@ -128,176 +129,179 @@
         signal((p.s, p.d, 1 - p.t))
         signal((p.s, p.a * 2 + 1 - p.b, p.t))
 
-        @pl.when(p.a > 0)
-        def _():
-            signal((p.s, (p.a - 1) * 2 + p.b, p.t))
-
-        @pl.when(p.a < p.A - 1)
-        def _():
-            signal((p.s, (p.a + 1) * 2 + p.b, p.t))
-
-    line = 2 + (p.a > 0).astype(jnp.int32) + (p.a < p.A - 1).astype(jnp.int32)
+        steps_of(p, lambda row: signal((p.s, row * 2 + p.b, p.t)))
+
+    line = 2 + p.A - 1
     pl.when(active)(lambda: pl.semaphore_wait(barrier, line + (1 if partner else 0)))
     if partner:
         pl.when(jnp.logical_not(active))(lambda: pl.semaphore_wait(barrier, 1))
 
 
-def line_gather(p, buf, size, sems, cols=None):
-    up_s, up_r, dn_s, dn_r, xs, xr = sems
-    A = p.A
-    above = (p.s, (p.a + 1) * 2 + p.b, p.t)
-    below = (p.s, (p.a - 1) * 2 + p.b, p.t)
+def steps_of(p, fn, far_first=False):
+    for delta in range(p.A - 1, 0, -1) if far_first else range(1, p.A):
+        pl.when(p.a - delta >= 0)(lambda: fn(p.a - delta))
+        pl.when(p.a + delta < p.A)(lambda: fn(p.a + delta))
+
+
+def line_gather(p, buf, size, sems):
+    zs, zr, xs, xr = sems
     side = (p.s, p.a * 2 + 1 - p.b, p.t)
-
-    def at(col, row):
-        return buf.at[col, rows_of(row, size)]
-
-    def up(i, row):
-        return rcopy(at(p.b, row), at(p.b, row), up_s.at[i], up_r.at[i], above)
-
-    def down(i, row):
-        return rcopy(at(p.b, row), at(p.b, row), dn_s.at[i], dn_r.at[i], below)
-
-    def across(col, row):
-        return rcopy(at(col, row), at(col, row), xs.at[row], xr.at[row], side)
-
-    def when(cond, fn):
-        pl.when(cond)(fn)
-
-    when(p.a < A - 1, lambda: up(0, p.a).start())
-    when(p.a > 0, lambda: down(0, p.a).start())
-    across(p.b, p.a).start()
-    for i in range(A - 1):
-
-        @pl.when(p.a - 1 - i >= 0)
-        def _():
-            row = p.a - 1 - i
-            up(i, row).wait_recv()
-            if i + 1 < A - 1:
-                when(p.a < A - 1, lambda: up(i + 1, row).start())
-            across(p.b, row).start()
-
-        @pl.when(p.a + 1 + i <= A - 1)
-        def _():
-            row = p.a + 1 + i
-            down(i, row).wait_recv()
-            if i + 1 < A - 1:
-                when(p.a > 0, lambda: down(i + 1, row).start())
-            across(p.b, row).start()
+    part = size // GATHER_PARTS
+
+    def at(col, row, g):
+        return buf.at[col, pl.ds(pl.multiple_of(row * size + g * part, part), part)]
+
+    def along(row, g):
+        return rcopy(at(p.b, p.a, g), at(p.b, p.a, g), zs.at[row, g], zr.at[p.a, g], (p.s, row * 2 + p.b, p.t))
+
+    def came(row, g):
+        return rcopy(at(p.b, row, g), at(p.b, row, g), zs.at[row, g], zr.at[row, g], side)
+
+    def across(col, row, g):
+        return rcopy(at(col, row, g), at(col, row, g), xs.at[row, g], xr.at[row, g], side)
+
+    def each(fn):
+        def run(row):
+            for g in range(GATHER_PARTS):
+                fn(row, g)
+
+        return run
+
+    for g in range(GATHER_PARTS):
+        steps_of(p, lambda row: along(row, g).start(), True)
+        across(p.b, p.a, g).start()
+
+    def forward(row, g):
+        came(row, g).wait_recv()
+        across(p.b, row, g).start()
+
+    steps_of(p, each(forward))
 
     def arrive():
-        for row in range(A):
-            across(1 - p.b, row).wait_recv()
+        for row in range(p.A):
+            each(lambda row, g: across(1 - p.b, row, g).wait_recv())(row)
 
     def finish():
-        for i in range(A - 1):
-            when((p.a < A - 1) & (p.a - i >= 0), lambda: up(i, p.a - i).wait_send())
-            when((p.a > 0) & (p.a + i <= A - 1), lambda: down(i, p.a + i).wait_send())
-        for row in range(A):
-            across(p.b, row).wait_send()
+        steps_of(p, each(lambda row, g: along(row, g).wait_send()))
+        for row in range(p.A):
+            each(lambda row, g: across(p.b, row, g).wait_send())(row)
 
     return arrive, finish
 
 
 def line_scatter(p, acc, other, got, step_got, size, cuts, sems, out):
-    xs, xr, us, ur, ds_, dr = sems
-    A = p.A
-    above = (p.s, (p.a + 1) * 2 + p.b, p.t)
-    below = (p.s, (p.a - 1) * 2 + p.b, p.t)
+    xs, xr, zs, zr = sems
     side = (p.s, p.a * 2 + 1 - p.b, p.t)
+
+    def part(row, h):
+        return (rows_of(row, size), pl.ds(cuts[h][0], cuts[h][1]))
+
+    def across(h, row):
+        at = part(row, h)
+        return rcopy(other.at[at], got.at[at], xs.at[h, row], xr.at[h, row], side)
+
+    def along(h, row):
+        return rcopy(
+            other.at[part(row, h)], step_got.at[part(p.a, h)], zs.at[h, row], zr.at[h, p.a], (p.s, row * 2 + p.b, p.t)
+        )
+
+    def came(h, row):
+        return rcopy(other.at[part(row, h)], step_got.at[part(row, h)], zs.at[h, row], zr.at[h, row], side)
+
+    def start(h):
+        steps_of(p, lambda row: across(h, row).start(), True)
+        across(h, p.a).start()
+
+    def carry(h):
+        def pass_on(row):
+            at = part(row, h)
+            across(h, row).wait()
+            other[at] = (acc[at] + got[at].astype(F32)).astype(BF)
+            along(h, row).start()
+
+        steps_of(p, pass_on, True)
+
+    def collect(h):
+        across(h, p.a).wait()
+        at = part(p.a, h)
+        cols = (slice(None), at[1])
+        out[cols] = acc[at] + got[at].astype(F32)
+
+        def add(row):
+            came(h, row).wait_recv()
+            out[cols] += step_got[part(row, h)].astype(F32)
+
+        steps_of(p, add)
+
+    def finish(h):
+        steps_of(p, lambda row: along(h, row).wait_send())
+
+    return start, carry, collect, finish
+
+
+def lowest(mask, n):
+    bit = 0
+    while (1 << bit) < n and not mask >> bit & 1:
+        bit += 1
+    return bit
+
+
+def flip(d, mask):
+    bit = 0
+    result = d
+    while 1 << bit <= mask:
+        if mask >> bit & 1:
+            result = result + (1 - 2 * lax.rem(lax.div(d, 1 << bit), 2)) * (1 << bit)
+        bit += 1
+    return result
+
+
+def cube_scatter(p, acc, got, size, cuts, sems, out):
+    send, recv = sems
+    n = p.n
 
     def cols(h):
         return pl.ds(cuts[h][0], cuts[h][1])
 
-    def across(h):
-        return rcopy(other.at[:, cols(h)], got.at[:, cols(h)], xs.at[h], xr.at[h], side)
-
-    def up(h, dest):
+    def block(mask):
+        return rows_of(flip(p.d, mask), size)
+
+    def message(h, mask):
+        bit = lowest(mask, n)
         return rcopy(
-            other.at[pl.ds(dest * size, size), cols(h)],
-            step_got.at[pl.ds(dest * size, size), cols(h)],
-            us.at[h, dest],
-            ur.at[h, dest],
-            above,
+            acc.at[block(mask), cols(h)],
+            got.at[pl.ds((mask - 1) * size, size), cols(h)],
+            send.at[h, mask],
+            recv.at[h, mask],
+            (p.s, flip(p.d, 1 << bit), p.t),
         )
 
-    def down(h, dest):
-        slot = jnp.where(p.a - 1 == dest, A, dest)
-        return rcopy(
-            other.at[pl.ds(dest * size, size), cols(h)],
-            step_got.at[rows_of(slot, size), cols(h)],
-            ds_.at[h, dest],
-            dr.at[h, dest],
-            below,
-        )
-
-    def up_here(h, dest):
-        rows = rows_of(dest, size) if not isinstance(dest, int) else pl.ds(dest * size, size)
-        return rcopy(other.at[pl.ds(0, size), cols(h)], step_got.at[rows, cols(h)], us.at[h, dest], ur.at[h, dest], above)
-
-    def down_here(h, dest, slot):
-        rows = pl.ds(slot * size, size)
-        return rcopy(other.at[pl.ds(0, size), cols(h)], step_got.at[rows, cols(h)], ds_.at[h, dest], dr.at[h, dest], below)
-
-    def start(h):
-        across(h).start()
-
-    def carry(h):
-        across(h).wait()
-        for i in range(A - 1):
-            hi, lo = A - 1 - i, i
-
-            @pl.when(p.a < hi)
-            def _():
-                here = (pl.ds(hi * size, size), cols(h))
-                total = acc[here] + got[here].astype(F32)
-                other[here] = total.astype(BF)
-
-                @pl.when(p.a > 0)
-                def _():
-                    up_here(h, hi).wait_recv()
-                    other[here] = (acc[here] + got[here].astype(F32) + step_got[here].astype(F32)).astype(BF)
-
-                up(h, hi).start()
-
-            @pl.when(p.a > lo)
-            def _():
-                here = (pl.ds(lo * size, size), cols(h))
-                total = acc[here] + got[here].astype(F32)
-                other[here] = total.astype(BF)
-
-                @pl.when(p.a < A - 1)
-                def _():
-                    down_here(h, lo, lo).wait_recv()
-                    other[here] = (acc[here] + got[here].astype(F32) + step_got[here].astype(F32)).astype(BF)
-
-                down(h, lo).start()
-
-        mine = (rows_of(p.a, size), cols(h))
-        out[:, cols(h)] = acc[mine] + got[mine].astype(F32)
-
-        @pl.when(p.a > 0)
-        def _():
-            up_here(h, p.a).wait_recv()
-            out[:, cols(h)] += step_got[mine].astype(F32)
-
-        @pl.when(p.a < A - 1)
-        def _():
-            rcopy(
-                other.at[pl.ds(0, size), cols(h)],
-                step_got.at[pl.ds(A * size, size), cols(h)],
-                ds_.at[h, p.a],
-                dr.at[h, p.a],
-                below,
-            ).wait_recv()
-            out[:, cols(h)] += step_got[pl.ds(A * size, size), cols(h)].astype(F32)
+    def stage(h, bit):
+        for mask in range(1, n):
+            if lowest(mask, n) == bit:
+                at = (block(mask), cols(h))
+                total = None
+                for below in range(bit):
+                    came = mask | 1 << below
+                    message(h, came).wait_recv()
+                    term = got[pl.ds((came - 1) * size, size), cols(h)].astype(F32)
+                    total = term if total is None else total + term
+                if total is not None:
+                    acc[at] = (acc[at].astype(F32) + total).astype(BF)
+                message(h, mask).start()
+
+    def last(h):
+        total = acc[block(0), cols(h)].astype(F32)
+        for below in range(lowest(0, n)):
+            message(h, 1 << below).wait_recv()
+            total = total + got[pl.ds(((1 << below) - 1) * size, size), cols(h)].astype(F32)
+        out[:, cols(h)] = total
 
     def finish(h):
-        for dest in range(A):
-            pl.when(p.a < dest)(lambda: up(h, dest).wait_send())
-            pl.when(p.a > dest)(lambda: down(h, dest).wait_send())
-
-    return start, carry, finish
+        for mask in range(1, n):
+            message(h, mask).wait_send()
+
+    return stage, last, finish
 
 
 def dma(*shape):
@@ -305,13 +309,12 @@
 
 
 def gather_sems(A):
-    return dict(gus=dma(A), gur=dma(A), gds=dma(A), gdr=dma(A), gxs=dma(A), gxr=dma(A))
+    g = GATHER_PARTS
+    return dict(gzs=dma(A, g), gzr=dma(A, g), gxs=dma(A, g), gxr=dma(A, g))
 
 
 def scatter_sems(A, parts):
-    return dict(
-        rxs=dma(parts), rxr=dma(parts), rus=dma(parts, A), rur=dma(parts, A), rds=dma(parts, A), rdr=dma(parts, A)
-    )
+    return dict(rxs=dma(parts, A), rxr=dma(parts, A), rzs=dma(parts, A), rzr=dma(parts, A))
 
 
 HBM = pl.BlockSpec(memory_space=pltpu.HBM)
@@ -336,7 +339,7 @@
         scratch_shapes=list(scratch.values()),
         input_output_aliases={len(names) + i: order.index(name) for i, name in enumerate(taken)},
         compiler_params=pltpu.CompilerParams(
-            collective_id=cid, has_side_effects=True, vmem_limit_bytes=VMEM_LIMIT
+            collective_id=cid, has_side_effects=cid is not None, vmem_limit_bytes=VMEM_LIMIT
         ),
     )(*hbm_in.values(), *vmem_in.values(), *[kept[name] for name in taken])
     return dict(zip(order, results))
@@ -360,39 +363,28 @@
     def _():
         pl.semaphore_wait(o.go, 1)
 
-    above = (p.s, (p.a + 1) * 2 + p.b, p.t)
-    below = (p.s, (p.a - 1) * 2 + p.b, p.t)
     side = (p.s, p.a * 2 + 1 - p.b, p.t)
     pair = (p.s, p.d, 1 - p.t)
     cuts = c.cuts
+    bits = lowest(0, n)
     local = Local(o.lsem)
     waits = []
 
-    def shard(row, col):
-        return rows_of(row * 2 + col, R)
-
-    def piece(row, q, own):
-        cs = pl.ds(*cuts[q])
-        return o.pack.at[:, cs] if own else o.pk.at[shard(row, p.b), cs]
-
-    def up(i, q, row):
-        return rcopy(
-            piece(row, q, i == 0), o.pk.at[shard(row, p.b), pl.ds(*cuts[q])], o.gus.at[i, q], o.gur.at[i, q], above
-        )
-
-    def down(i, q, row):
-        return rcopy(
-            piece(row, q, i == 0), o.pk.at[shard(row, p.b), pl.ds(*cuts[q])], o.gds.at[i, q], o.gdr.at[i, q], below
-        )
-
-    def across(q, row, own, col):
-        return rcopy(
-            o.pack.at[:, pl.ds(*cuts[q])] if own else o.pk.at[shard(row, col), pl.ds(*cuts[q])],
-            o.pk.at[shard(row, col), pl.ds(*cuts[q])],
-            o.gxs.at[row, q],
-            o.gxr.at[row, q],
-            side,
-        )
+    def give(mask, bit, q):
+        rows, cs = rows_of(flip(p.d, mask), R), pl.ds(*cuts[q])
+        src = o.pk.at[rows, cs] if mask else o.pack.at[:, cs]
+        far = mask | 1 << bit
+        return rcopy(src, o.pk.at[rows, cs], o.gs.at[far, q], o.gr.at[far, q], (p.s, flip(p.d, 1 << bit), p.t))
+
+    def taken(mask, q):
+        at = (rows_of(flip(p.d, mask), R), pl.ds(*cuts[q]))
+        return rcopy(o.pk.at[at], o.pk.at[at], o.gs.at[mask, q], o.gr.at[mask, q], side)
+
+    def pass_on(mask, q):
+        if mask:
+            taken(mask, q).wait_recv()
+        for bit in reversed(range(lowest(mask, n))):
+            give(mask, bit, q).start()
 
     ffn = ((o.gate, o.gw), (o.up, o.uw), (o.down, o.dw))
 
@@ -416,62 +408,45 @@
         src = ffn[m][0].at[:, rows_of(p.d, hb)] if k == 0 else block(m, source, half)
         return rcopy(src, block(m, source, half), o.ys.at[k, m], o.yr.at[k, m], pair)
 
-    waits.append(local(o.pack, o.pk.at[shard(p.a, p.b)]))
+    bounce = [local(o.pack, o.pack_v)]
     for m in range(3):
-        waits.append(local(ffn[m][0].at[:, rows_of(p.d, hb)], block(m, p.d, p.t)))
-        share(m, 0, p.t).start()
+        bounce.append(local(ffn[m][0].at[:, rows_of(p.d, hb)], o.block_v.at[m]))
+    events = []
+    inner = sorted((mask for mask in range(2, n, 2)), key=lambda mask: (-lowest(mask, n), mask))
     for q in range(len(cuts)):
-        pl.when(p.a < A - 1)(lambda: up(0, q, p.a).start())
-        pl.when(p.a > 0)(lambda: down(0, q, p.a).start())
-        across(q, p.a, True, p.b).start()
-    for k in range(1, n):
+        events.append((0.0 + 0.1 * q, lambda q=q: pass_on(0, q)))
+        for i, mask in enumerate(inner):
+            events.append((c.ag[0] + c.ag[1] * q + c.ag[2] * i, lambda q=q, mask=mask: pass_on(mask, q)))
+    for k in range(n):
         for m in range(3):
-            trade(m, k).start()
-    todo = [(m, k) for k in range(1, n) for m in range(3)]
-    steps = [(i, q) for i in range(A - 1) for q in range(len(cuts))]
-    share_each = -(-len(todo) // len(steps))
-    for i, q in steps:
-
-        @pl.when(p.a - 1 - i >= 0)
-        def _():
-            row = p.a - 1 - i
-            up(i, q, row).wait_recv()
-            if i + 1 < A - 1:
-                pl.when(p.a < A - 1)(lambda: up(i + 1, q, row).start())
-            across(q, row, False, p.b).start()
-
-        @pl.when(p.a + 1 + i <= A - 1)
-        def _():
-            row = p.a + 1 + i
-            down(i, q, row).wait_recv()
-            if i + 1 < A - 1:
-                pl.when(p.a > 0)(lambda: down(i + 1, q, row).start())
-            across(q, row, False, p.b).start()
-
-        for _ in range(min(share_each, len(todo))):
-            m, k = todo.pop(0)
-            came(m, k).wait_recv()
-            share(m, k, p.t).start()
-    for m, k in todo:
-        came(m, k).wait_recv()
-        share(m, k, p.t).start()
+            at = m * n + k if c.by_matrix else k * 3 + m
+            if k:
+                events.append((c.tr[0] + c.tr[1] * at, lambda m=m, k=k: trade(m, k).start()))
+                events.append((c.tr[2] + c.tr[3] * at, lambda m=m, k=k: (came(m, k).wait_recv(), share(m, k, p.t).start())))
+            else:
+                events.append((c.tr[0] + c.tr[1] * at, lambda m=m: share(m, 0, p.t).start()))
+    for _, run in sorted(events, key=lambda e: e[0]):
+        run()
+    for copy in bounce:
+        copy.wait()
+    waits.append(local(o.pack_v, o.pk.at[rows_of(p.d, R)]))
+    for m in range(3):
+        waits.append(local(o.block_v.at[m], block(m, p.d, p.t)))
 
     @pl.when(p.s == 0)
     def _():
         pl.semaphore_signal(o.go, inc=1, device_id=(1 - p.s, p.d, p.t), device_id_type=MESH)
 
-    for row in range(A):
-        for q in range(len(cuts)):
-            across(q, row, False, 1 - p.b).wait_recv()
+    for q in range(len(cuts)):
+        for mask in range(1, n, 2):
+            taken(mask, q).wait_recv()
     for k in range(n):
         for m in range(3):
             share(m, k, 1 - p.t).wait_recv()
-    for i, q in steps:
-        pl.when((p.a < A - 1) & (p.a - i >= 0))(lambda: up(i, q, p.a - i).wait_send())
-        pl.when((p.a > 0) & (p.a + i <= A - 1))(lambda: down(i, q, p.a + i).wait_send())
-    for row in range(A):
-        for q in range(len(cuts)):
-            across(q, row, False, p.b).wait_send()
+    for q in range(len(cuts)):
+        for mask in range(0, n, 2):
+            for bit in range(lowest(mask, n)):
+                give(mask, bit, q).wait_send()
     for k in range(n):
         for m in range(3):
             if k:
@@ -600,7 +575,7 @@
         o.xbuf[p.b, rows_of(p.a, r), :] = (comb * rms_of(comb) * gain(3)).astype(BF)
         send.wait_send()
 
-        arrive, gathered = line_gather(p, o.xbuf, r, (o.gus, o.gur, o.gds, o.gdr, o.gxs, o.gxr))
+        arrive, gathered = line_gather(p, o.xbuf, r, (o.gzs, o.gzr, o.gxs, o.gxr))
         w.gw.wait()
         w.uw.wait()
 
@@ -625,16 +600,17 @@
         arrive()
         hidden_part(1 - p.b)
         w.dw.wait()
-        start, carry, finish = line_scatter(
-            p, o.acc, o.other, o.got, o.step_got, r, c.halves, (o.rxs, o.rxr, o.rus, o.rur, o.rds, o.rdr), o.down_v
+        start, carry, collect, finish = line_scatter(
+            p, o.acc, o.other, o.got, o.step_got, r, c.halves, (o.rxs, o.rxr, o.rzs, o.rzr), o.down_v
         )
         for h in range(HALVES):
             down_part(1 - p.b, o.other, h)
             start(h)
         for h in range(HALVES):
             down_part(p.b, o.acc, h)
+            carry(h)
         for h in range(HALVES):
-            carry(h)
+            collect(h)
         down = o.down_v[...]
         resid = o.comb_v[...] + down * rms_of(down) * gain(4)
         o.resid_v[...] = resid
@@ -700,8 +676,11 @@
     )
 
 
+TAIL = "_v"
+
+
 def scratch_of(shapes):
-    return {name + chr(95) + chr(118): pltpu.VMEM(shape[1:], kind) for name, (shape, kind) in shapes.items()}
+    return {name + TAIL: pltpu.VMEM(shape[1:], kind) for name, (shape, kind) in shapes.items()}
 
 
 def line_scratch(c):
@@ -711,7 +690,7 @@
         acc=pltpu.VMEM((ar, c.width), F32),
         other=pltpu.VMEM((ar, c.width), BF),
         got=pltpu.VMEM((ar, c.width), BF),
-        step_got=pltpu.VMEM((ar + c.r, c.width), BF),
+        step_got=pltpu.VMEM((ar, c.width), BF),
         ysend=pltpu.VMEM((c.r, c.width), BF),
         ygot=pltpu.VMEM((c.r, c.width), BF),
         lsem=dma(40),
@@ -797,7 +776,7 @@
         have(1)
         ddown, o.ggr_v[4:5, :] = rms_back(o.down_v[...], gain(4), dres)
         o.xbuf[p.b, rows_of(p.a, r), :] = ddown.astype(BF)
-        arrive, gathered = line_gather(p, o.xbuf, r, (o.gus, o.gur, o.gds, o.gdr, o.gxs, o.gxr))
+        arrive, gathered = line_gather(p, o.xbuf, r, (o.gzs, o.gzr, o.gxs, o.gxr))
         w.dw.wait()
         have(2)
 
@@ -823,16 +802,17 @@
         hidden_part(1 - p.b)
         w.gw.wait()
         w.uw.wait()
-        start, carry, finish = line_scatter(
-            p, o.acc, o.other, o.got, o.step_got, r, c.halves, (o.rxs, o.rxr, o.rus, o.rur, o.rds, o.rdr), o.down_v
+        start, carry, collect, finish = line_scatter(
+            p, o.acc, o.other, o.got, o.step_got, r, c.halves, (o.rxs, o.rxr, o.rzs, o.rzr), o.down_v
         )
         for h in range(HALVES):
             down_part(1 - p.b, o.other, h)
             start(h)
         for h in range(HALVES):
             down_part(p.b, o.acc, h)
+            carry(h)
         for h in range(HALVES):
-            carry(h)
+            collect(h)
         have(3)
         dcomb, o.ggr_v[3:4, :] = rms_back(o.comb_v[...], gain(3), o.down_v[...])
         even = (o.dcomb_v[...] + dcomb) * RH
@@ -1002,56 +982,92 @@
             pair,
         )
 
+    def ffn_out(m, source):
+        return (o.gg, o.gu, o.gd)[m].at[:, rows_of(source, hb)]
+
     def trade(m, k):
         dest = lax.rem(p.d + k, n)
         return rcopy(
-            o.fown.at[m, rows_of(dest, R)], o.gf.at[m, :, rows_of(p.d, hb)], o.ts.at[m, k], o.tr.at[m, k], (p.s, dest, p.t)
+            o.fown.at[m, rows_of(dest, R)], ffn_out(m, p.d), o.ts.at[m, k], o.tr.at[m, k], (p.s, dest, p.t)
         )
 
     def came(m, k):
         source = lax.rem(p.d + n - k, n)
-        return rcopy(
-            o.fown.at[m, rows_of(p.d, R)], o.gf.at[m, :, rows_of(source, hb)], o.ts.at[m, k], o.tr.at[m, k], side
-        )
-
-    attn = (o.dqkv, o.dot, o.dsm)
-    loads = []
-    for row in range(A):
-        for q, part in enumerate(attn):
-            cs = pl.ds(*c.parts[q])
-            loads.append(local(part.at[rows_of(row * 2 + 1 - p.b, R)], o.other.at[pl.ds(row * R, R), cs]))
-            loads.append(local(part.at[rows_of(row * 2 + p.b, R)], o.acc.at[pl.ds(row * R, R), cs]))
+        return rcopy(o.fown.at[m, rows_of(p.d, R)], ffn_out(m, source), o.ts.at[m, k], o.tr.at[m, k], side)
+
     owns = [local(ffn[m].at[:, rows_of(p.t, hb)], o.fown.at[m]) for m in range(3)]
+    order = [*range(1, n), 0]
     for m in range(3):
-        for k in [*range(1, n), 0]:
+        for k in order:
             swap(m, k).start()
-    for copy in loads:
+    need = [
+        local(getattr(o, name), getattr(o, name + TAIL))
+        for name in ("nfull", "dqkv", "afull", "heads", "lrlow", "lmid", "resid", "grlow", "plow", "llow", "lmg", "gcol")
+    ]
+    stage, last, finish = cube_scatter(p, o.acc, o.got, R, c.parts, (o.rs, o.rr), o.gp_v)
+    mine_copies = []
+
+    def grad(x, y, at, block=512):
+        tokens = 2 * x.shape[1]
+
+        @tiles(c.width, block)
+        def _(rows):
+            left = x[:, :, rows].reshape(tokens, block)
+            o.acc[rows, at] = tn(left, y[...].reshape(tokens, y.shape[2])).astype(BF)
+
+    def ffn_block(m, k):
+        rows = rows_of(lax.rem(p.d + k, n), R)
+        if k == order[0]:
+            owns[m].wait()
+        swap(m, k).wait_recv()
+        total = o.fown[m, rows, :].astype(F32) + o.fgot[m, rows, :].astype(F32)
+        o.fown[m, rows, :] = total.astype(BF)
+        if k:
+            trade(m, k).start()
+        else:
+            mine_copies.append(local(o.fown.at[m, rows], ffn_out(m, p.d)))
+
+    def part_grad(h):
+        begin, size = c.parts[h]
+        base = c.qkv + c.heads
+        if begin < c.qkv:
+            grad(o.nfull_v, o.dqkv_v.at[:, :, pl.ds(begin, size)], pl.ds(begin, size))
+        elif begin < base:
+            grad(o.afull_v, o.heads_v.at[:, :, pl.ds(begin - c.qkv, size)], pl.ds(begin, size))
+        elif begin == base:
+            mine = rows_of(p.t, c.r)
+            lane = lax.broadcasted_iota(jnp.int32, (512, LANES), 1)
+
+            @tiles(c.width, 512)
+            def _(rows):
+                left = tn(o.nfull_v[0, mine, rows], o.lmg_v[0]) + tn(o.nfull_v[1, mine, rows], o.lmg_v[1])
+                gains = o.gcol_v[rows, :].astype(F32)
+                o.acc[rows, pl.ds(begin, LANES)] = jnp.where(lane < c.rank, left, gains).astype(BF)
+
+            grad(o.lrlow_v, o.lmid_v, pl.ds(begin + LANES, LANES))
+            o.rlow_v[...] = o.resid_v[...].astype(BF)
+            grad(o.rlow_v, o.grlow_v, pl.ds(begin + 2 * LANES, c.per))
+        else:
+            grad(o.plow_v, o.llow_v, pl.ds(begin, c.per))
+
+    for copy in need:
         copy.wait()
-    start, carry, finish = line_scatter(
-        p, o.acc, o.other, o.got, o.step_got, R, c.parts, (o.rxs, o.rxr, o.rus, o.rur, o.rds, o.rdr), o.gp_v
-    )
-    for q in range(len(c.parts)):
-        start(q)
-    mine_copies = []
-    for q in range(max(len(c.parts), 3)):
-        if q < 3:
-            owns[q].wait()
-            for k in [*range(1, n), 0]:
-                rows = rows_of(lax.rem(p.d + k, n), R)
-                swap(q, k).wait_recv()
-                total = o.fown[q, rows, :].astype(F32) + o.fgot[q, rows, :].astype(F32)
-                o.fown[q, rows, :] = total.astype(BF)
-                if k:
-                    trade(q, k).start()
-                else:
-                    mine_copies.append(local(o.fown.at[q, rows], o.gf.at[q, :, rows_of(p.d, hb)]))
-        if q < len(c.parts):
-            carry(q)
+    events = []
+    for m in range(3):
+        for i, k in enumerate(order):
+            events.append((c.kg[0] + c.kg[1] * (m * n + i), lambda m=m, k=k: ffn_block(m, k)))
+    for h in range(len(c.parts)):
+        events.append((c.kg[2] * h, lambda h=h: (part_grad(h), stage(h, 0))))
+        for bit in range(1, lowest(0, n)):
+            events.append((c.kg[3] + c.kg[4] * h + c.kg[5] * (bit - 1), lambda h=h, bit=bit: stage(h, bit)))
+        events.append((c.kg[3] + c.kg[4] * h + c.kg[5] * (lowest(0, n) - 1), lambda h=h: last(h)))
+    for _, run in sorted(events, key=lambda e: e[0]):
+        run()
     shared = pl.ds(c.qkv + c.heads, c.small)
     o.ssend[...] = o.gp_v[:, shared].astype(BF)
-    last = rcopy(o.ssend, o.sgot, o.ss.at[0], o.sr.at[0], pair)
-    last.start()
-    last.wait()
+    rest = rcopy(o.ssend, o.sgot, o.ss.at[0], o.sr.at[0], pair)
+    rest.start()
+    rest.wait()
     o.gp_v[:, shared] += o.sgot[...].astype(F32)
     out = local(o.gp_v, o.gp)
     for m in range(3):
@@ -1077,9 +1093,11 @@
     )
     scratch = dict(
         gcol=pltpu.VMEM((c.width, LANES), BF),
+        pack_v=pltpu.VMEM((c.R, c.total), BF),
+        block_v=pltpu.VMEM((3, c.R, c.hb), BF),
         grow_v=pltpu.VMEM((8, c.width), F32),
-        gus=dma(A, q), gur=dma(A, q), gds=dma(A, q), gdr=dma(A, q), gxs=dma(A, q), gxr=dma(A, q),
-        ts=dma(n, 3), tr=dma(n, 3), ys=dma(n, 3), yr=dma(n, 3), lsem=dma(6),
+        gs=dma(n, q), gr=dma(n, q),
+        ts=dma(n, 3), tr=dma(n, 3), ys=dma(n, 3), yr=dma(n, 3), lsem=dma(12),
         go=pltpu.SemaphoreType.REGULAR,
     )
     return launch(
@@ -1087,24 +1105,64 @@
     )
 
 
-def return_grads(c, dqkv, dot, dsm, dg, du, dd):
+def return_grads(c, f, g, gcol, dg, du, dd):
     n, A = c.n, c.n // 2
     R = c.R
-    outs = dict(gp=((R, c.total), F32), gf=((3, R, n * c.hb), BF))
+    flat = ((R, n * c.hb), BF)
+    outs = dict(gp=((R, c.total), F32), gg=flat, gu=flat, gd=flat)
+    arrays = dict(
+        nfull=f.nfull, dqkv=g.dqkv, afull=g.afull, heads=f.heads, lrlow=g.lrlow, lmid=f.lmid, resid=f.resid,
+        grlow=g.grlow, plow=g.plow, llow=f.llow, lmg=g.lmg, gcol=gcol,
+    )
     scratch = dict(
-        acc=pltpu.VMEM((A * R, c.total), BF),
-        other=pltpu.VMEM((A * R, c.total), BF),
-        got=pltpu.VMEM((A * R, c.total), BF),
-        step_got=pltpu.VMEM((A * R + R, c.total), BF),
+        acc=pltpu.VMEM((c.width, c.total), BF),
+        got=pltpu.VMEM(((n - 1) * R, c.total), BF),
         gp_v=pltpu.VMEM((R, c.total), F32),
         fown=pltpu.VMEM((3, c.width, c.hb), BF),
         fgot=pltpu.VMEM((3, c.width, c.hb), BF),
         ssend=pltpu.VMEM((R, c.small), BF),
         sgot=pltpu.VMEM((R, c.small), BF),
-        ys=dma(3, n), yr=dma(3, n), ts=dma(3, n), tr=dma(3, n), ss=dma(1), sr=dma(1), lsem=dma(6 * A + 8),
-        **scatter_sems(A, len(c.parts)),
-    )
-    return launch(lambda o: return_kernel(c, o), 7, dict(dqkv=dqkv, dot=dot, dsm=dsm, dg=dg, du=du, dd=dd), {}, outs, scratch)
+        rlow_v=pltpu.VMEM(f.resid.shape, BF),
+        ys=dma(3, n), yr=dma(3, n), ts=dma(3, n), tr=dma(3, n), ss=dma(1), sr=dma(1), lsem=dma(24),
+        **{name + TAIL: pltpu.VMEM(v.shape, v.dtype) for name, v in arrays.items()},
+        rs=dma(len(c.parts), n), rr=dma(len(c.parts), n),
+    )
+    return launch(lambda o: return_kernel(c, o), 7, dict(**arrays, dg=dg, du=du, dd=dd), {}, outs, scratch)
+
+
+def widen_kernel(c, o):
+    local = Local(o.lsem)
+    loads = [local(o.gp, o.gp_v), local(o.gg, o.g_v.at[0]), local(o.gu, o.g_v.at[1]), local(o.gd, o.g_v.at[2])]
+    base = c.qkv + c.heads
+    loads[0].wait()
+    out = [
+        local(o.gp_v.at[:, pl.ds(0, c.heads)], o.q),
+        local(o.gp_v.at[:, pl.ds(c.heads, HEAD)], o.k),
+        local(o.gp_v.at[:, pl.ds(c.heads + HEAD, HEAD)], o.v),
+        local(o.gp_v.at[:, pl.ds(base, LANES)], o.left),
+        local(o.gp_v.at[:, pl.ds(base + 2 * LANES, c.per)], o.lg),
+    ]
+    o.t_v[...] = o.gp_v[:, pl.ds(c.qkv, c.heads)].T
+    out.append(local(o.t_v, o.out))
+    for m in range(3):
+        loads[1 + m].wait()
+        o.w_v[m] = o.g_v[m].astype(F32)
+        out.append(local(o.w_v.at[m], (o.wg, o.wu, o.wd)[m]))
+    for copy in out:
+        copy.wait()
+
+
+def widen(c, done):
+    R, wide = c.R, c.n * c.hb
+    outs = dict(
+        q=((R, c.heads), F32), k=((R, HEAD), F32), v=((R, HEAD), F32), left=((R, LANES), F32), lg=((R, c.per), F32),
+        out=((c.heads, R), F32), wg=((R, wide), F32), wu=((R, wide), F32), wd=((R, wide), F32),
+    )
+    scratch = dict(
+        gp_v=pltpu.VMEM((R, c.total), F32), t_v=pltpu.VMEM((c.heads, R), F32),
+        g_v=pltpu.VMEM((3, R, wide), BF), w_v=pltpu.VMEM((3, R, wide), F32), lsem=dma(16),
+    )
+    return launch(lambda o: widen_kernel(c, o), None, done, {}, outs, scratch)
 
 
 def spread(gain, n, rows):
@@ -1125,11 +1183,13 @@
     qkv = heads + 2 * HEAD
     per = layer_gate.shape[2]
     small = 2 * LANES + 2 * per
+    base = qkv + heads
     c = SimpleNamespace(
         n=n, R=R, r=hidden.shape[2], width=width, heads=heads, qkv=qkv, per=per, small=small, rank=rank,
         total=qkv + heads + small, hb=gate_weight.shape[2] // n,
         cuts=((0, qkv), (qkv, heads), (qkv + heads, small)),
-        parts=((0, qkv), (qkv, heads), (qkv + heads, small)),
+        parts=(*((i, 512) for i in range(0, qkv + heads, 512)), (base, small - per), (base + small - per, per)),
+        ag=(12.0, 6.0, 12.0), tr=(1.0, 2.5, 30.0, 3.0), by_matrix=True, kg=(6.0, 2.9, 2.0, 20.0, 12.0, 12.0),
         halves=tuple((h * width // HALVES, width // HALVES) for h in range(HALVES)),
     )
     gains = jnp.stack(
@@ -1176,44 +1236,39 @@
         inputs = inputs.reshape(-1, inputs.shape[-1])
         return tn(inputs, outs.reshape(-1, outs.shape[-1])).astype(BF)
 
-    nlow = lax.dynamic_slice_in_dim(f.nfull, t * c.r, c.r, axis=1)
     sums = g.ggr[0] + g.ggr[1]
     head_sums = jnp.pad(sums[6:, :HEAD].reshape(2, n, short), ((0, 0), (0, 0), (0, R - short))).reshape(2, width)
-    gain_cols = jnp.concatenate([sums[:6], head_sums], axis=0).T.astype(BF)
-    left = pair_grad(nlow, g.lmg)
-    left = jnp.concatenate([left[:, :rank], gain_cols, left[:, rank + 8 :]], axis=1)
-    dsm = jnp.concatenate(
-        [left, pair_grad(g.lrlow, f.lmid), pair_grad(f.resid.astype(BF), g.grlow), pair_grad(g.plow, f.llow)], axis=1
-    )
+    gain_cols = jnp.concatenate([sums[:6], head_sums], axis=0).T
+    gcol = jnp.pad(gain_cols, ((0, 0), (rank, LANES - rank - 8))).astype(BF)
     done = return_grads(
-        c, pair_grad(f.nfull, g.dqkv), pair_grad(g.afull, f.heads), dsm,
-        pair_grad(f.pfull, g.dgl), pair_grad(f.pfull, g.dul), pair_grad(g.dfull, f.geglu),
-    )
-    gp, gf = done["gp"], done["gf"].astype(F32)
+        c, f, g, gcol, pair_grad(f.pfull, g.dgl), pair_grad(f.pfull, g.dul), pair_grad(g.dfull, f.geglu)
+    )
+    w = SimpleNamespace(**widen(c, done))
+    gp = done["gp"]
     base = qkv + heads
-    gain_out = gp[:, base + rank : base + rank + 8].T
+    gain_out = w.left[:, rank : rank + 8].T
     one = lambda i: gain_out[i][None]
     return (
         f.act[None, :, None],
         g.igrad[None, :, None],
         g.lgrad[None, :, None],
         one(0),
-        gp[:, :heads][None],
-        gp[:, heads : heads + HEAD][None],
-        gp[:, heads + HEAD : qkv][None],
+        w.q[None],
+        w.k[None],
+        w.v[None],
         gain_out[6, :short][None],
         gain_out[7, :short][None],
-        gp[:, qkv:base].T[None],
+        w.out[None],
         one(1),
-        gp[:, base : base + rank][None],
+        w.left[:, :rank][None],
         gp[:, base + LANES : base + LANES + rank].T[None],
         one(2),
         one(3),
-        gf[0][None],
-        gf[1][None],
-        gf[2].T[None],
+        w.wg[None],
+        w.wu[None],
+        w.wd.T[None],
         one(4),
-        gp[:, base + 2 * LANES : base + 2 * LANES + per][None],
+        w.lg[None],
         gp[:, base + 2 * LANES + per :].T[None],
         one(5),
     )

time: 1100 us -> 942 us (0.86)
  Pallas kernels: 998 us -> 869 us
  local copies, waits for them, and re-layouts: 52.4 us -> 36.4 us
  matrix products: 33.2 us -> 20.9 us
    pallas_call x8 -> x9, Pallas kernels: 998 us -> 869 us  [launch(): pl.pallas_call(run, out_shape=[jax.ShapeDtypeStruct(*spec) for spec in ou...]
    dot_general x9 -> x3, matrix products: 33.2 us -> 20.9 us  [tn(): lax.dot_general(x, w, (((0,), (0,)), ((), ())), preferred_element_type=F32)]
    unnamed x99 -> x56, local copies, waits for them, and re-layouts: 26.1 us -> 23.3 us
where the time goes in v1:
time: 942 us; the launch traced here: 934 us
  Pallas kernels  869 us (92%)
  local copies, waits for them, and re-layouts  36.4 us (4%)
  matrix products  20.9 us (2%)
    pallas_call x9, Pallas kernels, launch(): pl.pallas_call(run, out_shape=[jax.ShapeDtypeStruct(*spec) for spec in ou...  869 us
    unnamed x56, local copies, waits for them, and re-layouts  23.3 us
    dot_general x3, matrix products, tn(): lax.dot_general(x, w, (((0,), (0,)), ((), ())), preferred_element_type=F32)  20.9 us

profile of v1, /device:TPU:0, one launch (start us, length us, event | category | flops | bytes accessed | tf_op | source)
XLA Modules:
  0.0 934.0 jit_solution(16294880899371239143)
XLA Ops:
  3.7 0.8 copy.165
  5.4 0.9 copy.164
  6.3 0.9 copy.173
  7.1 0.8 copy.167
  8.8 0.8 copy.169
  11.4 0.9 fusion
  12.3 1.0 copy.174
  13.9 4.6 copy.175
  18.5 146.0 %shard_map.393 = (bf16[2048,3328]{1,0:T(8,128)(2,1)}, bf16[2048,1024]{1,0:T(8,128)(2,1)}, bf16[2048,1024]{1,0:T(8,128)(2,1)}, bf16[2048,1024]{1,0:T(8,128)(2,1)}, f32[8,2048]{1,0:T(8,128)}) custom-call(bf16[256,3328]{1,0:T(8,128)(2,1)} %copy-done.6, bf16[256,4096]{1,0:T(8,128)(2,1)} %bitcast.118, bf16[256,4096]{1,0:T(8,128)(2,1)} %bitcast.119, ...), custom_call_target="tpu_custom_call" | custom-call | tf_op jit(solution)/shard_map/pallas_call | solution.py:334
  164.5 0.8 slice.63
  165.4 1.5 select_maximum_fusion.refs_6_.refs_16_
  166.9 108.9 %shard_map.394 = (bf16[2,64,2048]{2,1,0:T(8,128)(2,1)}, bf16[2,64,2048]{2,1,0:T(8,128)(2,1)}, bf16[2,128,2048]{2,1,0:T(8,128)(2,1)}, f32[2,128,1536]{2,1,0:T(8,1...) custom-call(bf16[2048,3328]{1,0:T(8,128)(2,1)} %get-tuple-element.13, ...), custom_call_target="tpu_custom_call" | custom-call | tf_op jit(solution)/shard_map/pallas_call | solution.py:334
  275.9 101.9 %shard_map.395 = (bf16[2,64,2048]{2,1,0:T(8,128)(2,1)}, bf16[2,64,2048]{2,1,0:T(8,128)(2,1)}, bf16[2,128,2048]{2,1,0:T(8,128)(2,1)}, f32[2,128,1536]{2,1,0:T(8,1...) custom-call(bf16[2048,3328]{1,0:T(8,128)(2,1)} %get-tuple-element.13, ...), custom_call_target="tpu_custom_call", output_to_operand_aliasing={{0}: (10, {}), {1}: (11, {}), {2}: (12, {}), {3}: (13, {}),... | custom-call | tf_op jit(solution)/shard_map/pallas_call | solution.py:334
  377.8 3.5 shard_map.396
  381.2 8.8 shard_map.397
  390.0 224.6 %shard_map.398 = (f32[2,64,2048]{2,1,0:T(8,128)}, bf16[2,64,2048]{2,1,0:T(8,128)(2,1)}, f32[2,64,256]{2,1,0:T(8,128)}, bf16[2,64,2048]{2,1,0:T(8,128)(2,1)}, bf1...) custom-call(bf16[2048,3328]{1,0:T(8,128)(2,1)} %get-tuple-element.13, ...), custom_call_target="tpu_custom_call", output_to_operand_aliasing={{0}: (20, {}), {1}: (21, {}), {2}: (22, {}), {3}: (23, {}),... | custom-call | tf_op jit(solution)/shard_map/pallas_call | solution.py:334
  614.6 81.1 %shard_map.399 = (f32[2,64,2048]{2,1,0:T(8,128)}, bf16[2,64,2048]{2,1,0:T(8,128)(2,1)}, f32[2,64,256]{2,1,0:T(8,128)}, bf16[2,64,2048]{2,1,0:T(8,128)(2,1)}, bf1...) custom-call(bf16[2048,3328]{1,0:T(8,128)(2,1)} %get-tuple-element.13, ...), custom_call_target="tpu_custom_call", output_to_operand_aliasing={{0}: (20, {}), {1}: (21, {}), {2}: (22, {}), {3}: (23, {}),... | custom-call | tf_op jit(solution)/shard_map/pallas_call | solution.py:334
  695.7 1.0 fusion.10
  696.7 0.9 add_convert_fusion
  698.1 1.0 pad.35.refs_11_
  699.1 8.5 bitcast_convert_fusion.refs_14_
  707.6 6.2 bitcast_convert_fusion.2.refs_12_
  713.8 6.2 bitcast_convert_fusion.1.refs_13_
  720.0 185.5 %shard_map.400 = (f32[256,3328]{1,0:T(8,128)}, bf16[256,4096]{1,0:T(8,128)(2,1)}, bf16[256,4096]{1,0:T(8,128)(2,1)}, bf16[256,4096]{1,0:T(8,128)(2,1)}) custom-call(bf16[2,128,2048]{2,1,0:T(8,128)(2,1)} %get-tuple-element.212.refs_0_, bf16[2,128,1536]{2,1,0:T(8,128)(2,1)} %get-tuple-element.213.refs_1_, bf16[2,128,2048]{2,1,0:T(8,128)(2,1)} %get-tuple-element.214.refs_2_, ...), custom_call_target="tpu_custom_call" | custom-call | tf_op jit(solution)/shard_map/pallas_call | solution.py:334
  905.6 0.9 slice_bitcast_fusion.1
  907.2 1.0 slice_bitcast_fusion
  908.2 0.8 copy.193
  909.0 8.3 shard_map.401
  917.4 1.0 slice_bitcast_fusion.3
  918.4 0.9 slice_bitcast_fusion.2
  925.3 5.7 copy.191
  931.8 1.0 copy.278
  (72 shorter events, 15.6 us)
Async XLA Ops:
  0.7 12.7 %copy-start.8 = (bf16[1,1024,256]{2,1,0:T(8,128)(2,1)S(1)}, bf16[1,1024,256]{2,1,0:T(8,128)(2,1)}, u32[]{:S(2)}) copy-start(bf16[1,1024,256]{2,1,0:T(8,128)(2,1)} %param.33) | copy-start | bytes 1572868
  0.7 13.0 %copy-start.10 = (bf16[1,256,256]{2,1,0:T(8,128)(2,1)S(1)}, bf16[1,256,256]{2,1,0:T(8,128)(2,1)}, u32[]{:S(2)}) copy-start(bf16[1,256,256]{2,1,0:T(8,128)(2,1)} %param.29) | copy-start | bytes 393220
  0.7 12.9 %copy-start.9 = (bf16[1,256,1024]{2,1,0:T(8,128)(2,1)S(1)}, bf16[1,256,1024]{2,1,0:T(8,128)(2,1)}, u32[]{:S(2)}) copy-start(bf16[1,256,1024]{2,1,0:T(8,128)(2,1)} %param.28) | copy-start | bytes 1572868
  3.6 10.0 %copy-start.11 = (bf16[1,256,256]{2,1,0:T(8,128)(2,1)S(1)}, bf16[1,256,256]{2,1,0:T(8,128)(2,1)}, u32[]{:S(2)}) copy-start(bf16[1,256,256]{2,1,0:T(8,128)(2,1)} %param.30) | copy-start | bytes 393220
  12.3 1.5 copy-start.12
  13.9 4.6 copy-start.6
  695.7 3.4 copy-start.2
  699.1 8.5 copy-start
  699.1 8.5 copy-start.3
  707.6 6.2 copy-start.4
  925.3 5.7 copy-start.5
  925.3 6.5 copy-start.1
  931.1 1.8 copy-start.7

commit v2 on v1

--- a/solution.py
+++ b/solution.py
@@ -115,28 +115,6 @@
         return copy
 
 
-def greet(p, active, partner):
-    barrier = pltpu.get_barrier_semaphore()
-
-    def signal(device):
-        pl.semaphore_signal(barrier, inc=1, device_id=device, device_id_type=MESH)
-
-    if partner:
-        signal((1 - p.s, p.d, p.t))
-
-    @pl.when(active)
-    def _():
-        signal((p.s, p.d, 1 - p.t))
-        signal((p.s, p.a * 2 + 1 - p.b, p.t))
-
-        steps_of(p, lambda row: signal((p.s, row * 2 + p.b, p.t)))
-
-    line = 2 + p.A - 1
-    pl.when(active)(lambda: pl.semaphore_wait(barrier, line + (1 if partner else 0)))
-    if partner:
-        pl.when(jnp.logical_not(active))(lambda: pl.semaphore_wait(barrier, 1))
-
-
 def steps_of(p, fn, far_first=False):
     for delta in range(p.A - 1, 0, -1) if far_first else range(1, p.A):
         pl.when(p.a - delta >= 0)(lambda: fn(p.a - delta))
@@ -175,8 +153,6 @@
         came(row, g).wait_recv()
         across(p.b, row, g).start()
 
-    steps_of(p, each(forward))
-
     def arrive():
         for row in range(p.A):
             each(lambda row, g: across(1 - p.b, row, g).wait_recv())(row)
@@ -186,7 +162,7 @@
         for row in range(p.A):
             each(lambda row, g: across(p.b, row, g).wait_send())(row)
 
-    return arrive, finish
+    return lambda: steps_of(p, each(forward)), arrive, finish
 
 
 def line_scatter(p, acc, other, got, step_got, size, cuts, sems, out):
@@ -321,28 +297,23 @@
 VM = pl.BlockSpec(memory_space=pltpu.VMEM)
 
 
-def launch(kernel, cid, hbm_in, vmem_in, outs, scratch, kept=None, cost=None):
-    kept = kept or {}
-    names = [*hbm_in, *vmem_in]
-    taken = [name for name in outs if name in kept]
-    everything = names + [None] * len(taken) + [*outs, *scratch]
+def launch(kernel, cid, hbm_in, vmem_in, outs, scratch):
+    everything = [*hbm_in, *vmem_in, *outs, *scratch]
 
     def run(*refs):
-        kernel(SimpleNamespace(**{k: v for k, v in zip(everything, refs) if k}))
-
-    order = list(outs)
+        kernel(SimpleNamespace(**dict(zip(everything, refs))))
+
     results = pl.pallas_call(
         run,
         out_shape=[jax.ShapeDtypeStruct(*spec) for spec in outs.values()],
-        in_specs=[HBM] * len(hbm_in) + [VM] * len(vmem_in) + [HBM] * len(taken),
+        in_specs=[HBM] * len(hbm_in) + [VM] * len(vmem_in),
         out_specs=[HBM] * len(outs),
         scratch_shapes=list(scratch.values()),
-        input_output_aliases={len(names) + i: order.index(name) for i, name in enumerate(taken)},
         compiler_params=pltpu.CompilerParams(
             collective_id=cid, has_side_effects=cid is not None, vmem_limit_bytes=VMEM_LIMIT
         ),
-    )(*hbm_in.values(), *vmem_in.values(), *[kept[name] for name in taken])
-    return dict(zip(order, results))
+    )(*hbm_in.values(), *vmem_in.values())
+    return dict(zip(outs, results))
 
 
 def fetch_kernel(c, o):
@@ -492,163 +463,283 @@
     return (slice(None), pl.ds(*cut))
 
 
-def forward_kernel(c, k, o):
-    p = place(c.n)
+def enter(p, o, sender):
+    barrier = pltpu.get_barrier_semaphore()
+
+    def signal(device):
+        pl.semaphore_signal(barrier, inc=1, device_id=device, device_id_type=MESH)
+
+    partner = (1 - p.s, p.d, p.t)
+    pl.when(p.s == sender)(lambda: signal(partner))
+    line_greet(p, signal)
+    line = p.A + 1
+    pl.semaphore_wait(barrier, jnp.where(p.s == sender, line, line + 1))
+
+    @pl.when(p.s == 1 - sender)
+    def _():
+        pl.semaphore_signal(o.ready, inc=1, device_id=partner, device_id_type=MESH)
+
+
+def line_greet(p, signal):
+    signal((p.s, p.d, 1 - p.t))
+    signal((p.s, p.a * 2 + 1 - p.b, p.t))
+    steps_of(p, lambda row: signal((p.s, row * 2 + p.b, p.t)))
+
+
+def again(p):
+    barrier = pltpu.get_barrier_semaphore()
+    line_greet(p, lambda device: pl.semaphore_signal(barrier, inc=1, device_id=device, device_id_type=MESH))
+    pl.semaphore_wait(barrier, p.A + 1)
+
+
+def view(c, o, m, buffers, sems):
+    slot = m if c.slots == 2 else 0
+    names = {name: getattr(o, name + str(slot)) for name in buffers}
+    names.update({name: getattr(o, name + str(m)) for name in sems})
+    return SimpleNamespace(**names)
+
+
+def twice(c, buffers, sems):
+    out = {}
+    for slot in range(c.slots):
+        out.update({name + str(slot): spec for name, spec in buffers.items()})
+    for m in range(2):
+        out.update({name + str(m): spec for name, spec in sems.items()})
+    return out
+
+
+def run_stages(c, p, order, stages):
+    if c.slots == 1:
+        order = [item for m in range(2) for item in order if item[1] == m]
+    for name, m in order:
+        if c.slots == 1 and name == FIRST and m == 1:
+            stages[0][LAST]()
+            again(p)
+        stages[m][name]()
+    for m in range(2) if c.slots == 2 else (1,):
+        stages[m][LAST]()
+
+
+FIRST, GIVE, OWN, REST, SUMS, PASS, LAST = range(7)
+BEGIN, PROJ, JOIN, TAIL_STAGE, MIDDLE, HEADS_STAGE, ENTRY = range(10, 17)
+
+
+def line_stages(c, p, v, hidden_part, down_part, ready):
+    start, carry, collect, finish = line_scatter(
+        p, v.acc, v.other, v.got, v.step_got, c.r, c.halves, (v.rxs, v.rxr, v.rzs, v.rzr), v.down_v
+    )
+    link = SimpleNamespace()
+
+    def begin():
+        link.forward, link.arrive, link.gathered = line_gather(p, v.xbuf, c.r, (v.gzs, v.gzr, v.gxs, v.gxr))
+
+    def own():
+        ready(0)
+        hidden_part(p.b)
+
+    def rest():
+        link.arrive()
+        hidden_part(1 - p.b)
+        ready(1)
+        for h in range(HALVES):
+            down_part(1 - p.b, v.other, h)
+            start(h)
+        for h in range(HALVES):
+            down_part(p.b, v.acc, h)
+
+    def sums():
+        for h in range(HALVES):
+            carry(h)
+
+    def total():
+        for h in range(HALVES):
+            collect(h)
+
+    def end():
+        link.gathered()
+        for h in range(HALVES):
+            finish(h)
+
+    return SimpleNamespace(begin=begin, give=lambda: link.forward(), own=own, rest=rest, sums=sums, total=total, end=end)
+
+
+def once(*copies):
+    state = [False]
+
+    def run():
+        if not state[0]:
+            state[0] = True
+            for copy in copies:
+                copy.wait()
+
+    return run
+
+
+def forward_stages(c, p, o, v, m, w, local):
     r, width, hb2 = c.r, c.width, 2 * c.hb
-    A = p.A
-    m = jnp.clip(k - p.s, 0, 1)
-    active = (k - p.s >= 0) & (k - p.s <= 1)
-    local = Local(o.lsem)
     pair = (p.s, p.d, 1 - p.t)
-
-    greet(p, active, k >= 1)
-    hand = k and rcopy(o.act.at[min(max(k - 1, 0), 1)], o.hid, o.hs.at[0], o.hr.at[0], (1 - p.s, p.d, p.t))
-    if k >= 1:
-        pl.when(p.s == 0)(hand.start)
-
-    @pl.when(active)
-    def _():
-        w = load_weights(c, o, local)
-        lv_copy = local(o.lin.at[m], o.lv)
-        first = pltpu.make_async_copy(o.hidden.at[m], o.hid, o.fsem.at[0])
+    mine, theirs = rows_of(p.t, r), rows_of(1 - p.t, r)
+    gain = lambda i: o.gains[i : i + 1, :]
+    hand = rcopy(v.act_v, v.hid, v.hs.at[0], v.hr.at[0], (1 - p.s, p.d, p.t))
+    first = pltpu.make_async_copy(o.hidden.at[m], v.hid, v.fsem.at[0])
+    send = rcopy(v.nbuf.at[mine], v.nbuf.at[mine], v.ys.at[0], v.yr.at[0], pair)
+    swap = rcopy(v.ysend, v.ygot, v.ys.at[1], v.yr.at[1], pair)
+    keep = []
+
+    def stash(*pairs):
+        keep.extend(local(src, dst.at[m]) for src, dst in pairs)
+
+    def normed_of():
+        x = v.hid[...].astype(F32)
+        return x, x * rms_of(x) * gain(0)
+
+    def begin():
+        lv = local(o.lin.at[m], v.lv)
+        v.lv_wait = lv.wait
 
         @pl.when(p.s == 0)
         def _():
             first.start()
             first.wait()
 
-        if k >= 1:
-            pl.when(p.s == 1)(hand.wait_recv)
-        mine, theirs = rows_of(p.t, r), rows_of(1 - p.t, r)
-        gain = lambda i: o.gains[i : i + 1, :]
-
-        def normed_of():
-            x = o.hid[...].astype(F32)
-            return x, x * rms_of(x) * gain(0)
-
-        o.nbuf[mine, :] = normed_of()[1].astype(BF)
-        send = rcopy(o.nbuf.at[mine], o.nbuf.at[mine], o.ys.at[0], o.yr.at[0], pair)
+        pl.when(p.s == 1)(hand.wait_recv)
+        v.nbuf[mine, :] = normed_of()[1].astype(BF)
         send.start()
-        w.sm.wait()
+        w.sm()
         lane = lax.broadcasted_iota(jnp.int32, (r, LANES), 1)
-        mid = jnp.where(lane < c.rank, nn(o.nbuf[mine, :], o.sm_v[cols_of(LL)]), 0.0)
-        o.lmid_v[...] = mid.astype(BF)
-        o.lraw_v[...] = nt(o.lmid_v[...], o.sm_v[cols_of(LR)])
-        w.qkv.wait()
-        rcopy(o.nbuf.at[theirs], o.nbuf.at[theirs], o.ys.at[0], o.yr.at[0], pair).wait_recv()
+        mid = jnp.where(lane < c.rank, nn(v.nbuf[mine, :], o.sm_v[cols_of(LL)]), 0.0)
+        v.lmid_v[...] = mid.astype(BF)
+        v.lraw_v[...] = nt(v.lmid_v[...], o.sm_v[cols_of(LR)])
+        stash((v.hid, o.xlow), (v.lmid_v, o.lmid), (v.lraw_v, o.lraw))
+
+    def proj():
+        w.qkv()
+        rcopy(v.nbuf.at[theirs], v.nbuf.at[theirs], v.ys.at[0], v.yr.at[0], pair).wait_recv()
 
         @tiles(c.qkv, 256)
         def _(at):
-            o.qraw_v[:, at] = nn(o.nbuf[...], o.qkv_v[:, at])
+            v.qraw_v[:, at] = nn(v.nbuf[...], o.qkv_v[:, at])
 
         cos, sin = o.cos[...], o.sin[...]
         q_gain, k_gain = o.gains[6:7, 0:HEAD], o.gains[7:8, 0:HEAD]
         allowed = o.allowed[m] > 0.5
-        kraw = o.qraw_v[:, pl.ds(c.heads, HEAD)]
-        vraw = o.qraw_v[:, pl.ds(c.heads + HEAD, HEAD)]
+        kraw = v.qraw_v[:, pl.ds(c.heads, HEAD)]
+        vraw = v.qraw_v[:, pl.ds(c.heads + HEAD, HEAD)]
         key = rotate(kraw * rms_of(kraw) * k_gain, cos, sin).astype(BF)
         value = (vraw * rms_of(vraw)).astype(BF)
         for h in range(c.heads // HEAD):
             at = pl.ds(h * HEAD, HEAD)
-            raw = o.qraw_v[:, at]
+            raw = v.qraw_v[:, at]
             query = rotate(raw * rms_of(raw) * q_gain, cos, sin).astype(BF)
             scores = jnp.where(allowed, nt(query, key) * HEAD**-0.5, NEG)
             shifted = jnp.exp(scores - jnp.max(scores, axis=-1, keepdims=True))
             prob = shifted / jnp.sum(shifted, axis=-1, keepdims=True)
-            o.heads_v[:, at] = nn(prob.astype(BF), value).astype(BF)
-        w.ot.wait()
+            v.heads_v[:, at] = nn(prob.astype(BF), value).astype(BF)
+        w.ot()
 
         @tiles(width, 256)
         def _(at):
-            o.acc[0 : 2 * r, at] = nt(o.heads_v[...], o.ot_v[at, :])
-
-        o.ysend[...] = o.acc[theirs, :].astype(BF)
-        swap = rcopy(o.ysend, o.ygot, o.ys.at[1], o.yr.at[1], pair)
+            v.acc[0 : 2 * r, at] = nt(v.heads_v[...], o.ot_v[at, :])
+
+        v.ysend[...] = v.acc[theirs, :].astype(BF)
         swap.start()
+        stash((v.nbuf, o.nfull), (v.qraw_v, o.qraw), (v.heads_v, o.heads))
+
+    def join():
+        x, normed = normed_of()
         swap.wait()
-        x, normed = normed_of()
-        att = o.acc[mine, :] + o.ygot[...].astype(F32)
-        o.att_v[...] = att
-        lraw = o.lraw_v[...]
+        att = v.acc[mine, :] + v.ygot[...].astype(F32)
+        v.att_v[...] = att
+        lraw = v.lraw_v[...]
         comb = (x + att * rms_of(att) * gain(1) + normed + lraw * rms_of(lraw) * gain(2)) * RH
-        o.comb_v[...] = comb
-        o.xbuf[p.b, rows_of(p.a, r), :] = (comb * rms_of(comb) * gain(3)).astype(BF)
+        v.comb_v[...] = comb
+        v.xbuf[p.b, rows_of(p.a, r), :] = (comb * rms_of(comb) * gain(3)).astype(BF)
+        line.begin()
+        stash((v.att_v, o.att), (v.comb_v, o.comb))
+
+    def hidden_part(col):
+        @tiles(hb2, min(256, hb2))
+        def _(at):
+            gate = nn(v.xbuf[col], o.gw_v[:, at])
+            up = nn(v.xbuf[col], o.uw_v[:, at])
+            v.gate_v[col, :, at] = gate.astype(BF)
+            v.up_v[col, :, at] = up.astype(BF)
+            v.geglu_v[col, :, at] = (gelu(gate) * up).astype(BF)
+
+    def down_part(col, dest, h):
+        start, size = c.halves[h]
+
+        @tiles(size, 256)
+        def _(at):
+            at = pl.ds(pl.multiple_of(start + at.start, 256), 256)
+            dest[:, at] = nt(v.geglu_v[col], o.dw_v[at, :]).astype(dest.dtype)
+
+    def ready(i):
+        if i == 0:
+            w.gw()
+            w.uw()
+        else:
+            w.dw()
+
+    line = line_stages(c, p, v, hidden_part, down_part, ready)
+
+    def rest():
+        line.rest()
+        stash((v.xbuf, o.pfull), (v.gate_v, o.gate), (v.up_v, o.up), (v.geglu_v, o.geglu))
+
+    def tail():
+        line.total()
+        down = v.down_v[...]
+        v.resid_v[...] = v.comb_v[...] + down * rms_of(down) * gain(4)
+        graw = nn(v.resid_v[...].astype(BF), o.sm_v[cols_of(LG)])
+        v.graw_v[...] = graw
+        v.lv_wait()
+        v.llow_v[...] = (gelu(graw) * v.lv[...].astype(F32)).astype(BF)
+        proj = nt(v.llow_v[...], o.sm_v[cols_of(LP)])
+        v.proj_v[...] = proj
+        v.act_v[...] = (v.resid_v[...] + proj * rms_of(proj) * gain(5)).astype(BF)
+
+        @pl.when(p.s == 0)
+        def _():
+            if m == 0:
+                pl.semaphore_wait(o.ready, 1)
+            hand.start()
+
+        stash((v.down_v, o.down), (v.resid_v, o.resid), (v.graw_v, o.graw), (v.llow_v, o.llow), (v.proj_v, o.proj))
+        stash((v.act_v, o.act))
+
+    def end():
         send.wait_send()
-
-        arrive, gathered = line_gather(p, o.xbuf, r, (o.gzs, o.gzr, o.gxs, o.gxr))
-        w.gw.wait()
-        w.uw.wait()
-
-        def hidden_part(col):
-            @tiles(hb2, min(256, hb2))
-            def _(at):
-                gate = nn(o.xbuf[col], o.gw_v[:, at])
-                up = nn(o.xbuf[col], o.uw_v[:, at])
-                o.gate_v[col, :, at] = gate
-                o.up_v[col, :, at] = up
-                o.geglu_v[col, :, at] = (gelu(gate) * up).astype(BF)
-
-        def down_part(col, dest, h):
-            start, size = c.halves[h]
-
-            @tiles(size, 256)
-            def _(at):
-                at = pl.ds(pl.multiple_of(start + at.start, 256), 256)
-                dest[:, at] = nt(o.geglu_v[col], o.dw_v[at, :]).astype(dest.dtype)
-
-        hidden_part(p.b)
-        arrive()
-        hidden_part(1 - p.b)
-        w.dw.wait()
-        start, carry, collect, finish = line_scatter(
-            p, o.acc, o.other, o.got, o.step_got, r, c.halves, (o.rxs, o.rxr, o.rzs, o.rzr), o.down_v
-        )
-        for h in range(HALVES):
-            down_part(1 - p.b, o.other, h)
-            start(h)
-        for h in range(HALVES):
-            down_part(p.b, o.acc, h)
-            carry(h)
-        for h in range(HALVES):
-            collect(h)
-        down = o.down_v[...]
-        resid = o.comb_v[...] + down * rms_of(down) * gain(4)
-        o.resid_v[...] = resid
-        graw = nn(resid.astype(BF), o.sm_v[cols_of(LG)])
-        o.graw_v[...] = graw
-        lv_copy.wait()
-        o.llow_v[...] = (gelu(graw) * o.lv[...].astype(F32)).astype(BF)
-        proj = nt(o.llow_v[...], o.sm_v[cols_of(LP)])
-        o.proj_v[...] = proj
-        o.act_v[...] = (o.resid_v[...] + proj * rms_of(proj) * gain(5)).astype(BF)
-        out = [
-            local(o.hid, o.xlow.at[m]),
-            local(o.nbuf, o.nfull.at[m]),
-            local(o.qraw_v, o.qraw.at[m]),
-            local(o.heads_v, o.heads.at[m]),
-            local(o.att_v, o.att.at[m]),
-            local(o.lmid_v, o.lmid.at[m]),
-            local(o.lraw_v, o.lraw.at[m]),
-            local(o.comb_v, o.comb.at[m]),
-            local(o.xbuf, o.pfull.at[m]),
-            local(o.gate_v, o.gate.at[m]),
-            local(o.up_v, o.up.at[m]),
-            local(o.geglu_v, o.geglu.at[m]),
-            local(o.down_v, o.down.at[m]),
-            local(o.resid_v, o.resid.at[m]),
-            local(o.graw_v, o.graw.at[m]),
-            local(o.llow_v, o.llow.at[m]),
-            local(o.proj_v, o.proj.at[m]),
-            local(o.act_v, o.act.at[m]),
-        ]
-        gathered()
-        for h in range(HALVES):
-            finish(h)
-        for copy in out:
+        line.end()
+        pl.when(p.s == 0)(hand.wait_send)
+        for copy in keep:
             copy.wait()
 
-    if k >= 1:
-        pl.when(p.s == 0)(hand.wait_send)
+    return {
+        FIRST: begin, PROJ: proj, JOIN: join, GIVE: line.give, OWN: line.own, REST: rest, SUMS: line.sums,
+        TAIL_STAGE: tail, LAST: end,
+    }
+
+
+FORWARD_ORDER = (
+    (FIRST, 0), (PROJ, 0), (JOIN, 0), (FIRST, 1), (PROJ, 1), (GIVE, 0), (JOIN, 1), (OWN, 0), (GIVE, 1), (REST, 0),
+    (OWN, 1), (SUMS, 0), (REST, 1), (TAIL_STAGE, 0), (SUMS, 1), (TAIL_STAGE, 1),
+)
+
+
+def waits_of(c, o, local):
+    got = load_weights(c, o, local)
+    return SimpleNamespace(**{name: once(copy) for name, copy in vars(got).items()})
+
+
+def forward_kernel(c, o):
+    p = place(c.n)
+    local = Local(o.lsem)
+    w = waits_of(c, o, local)
+    enter(p, o, 0)
+    views = [view(c, o, m, forward_buffers(c), stage_sems(c) | dict(hid=None)) for m in range(2)]
+    stages = [forward_stages(c, p, o, views[m], m, w, local) for m in range(2)]
+    run_stages(c, p, FORWARD_ORDER, stages)
 
 
 def stash_shapes(c):
@@ -665,8 +756,8 @@
         lraw=((m, r, w), F32),
         comb=((m, r, w), F32),
         pfull=((m, 2, ar, w), BF),
-        gate=((m, 2, ar, hb2), F32),
-        up=((m, 2, ar, hb2), F32),
+        gate=((m, 2, ar, hb2), BF),
+        up=((m, 2, ar, hb2), BF),
         geglu=((m, 2, ar, hb2), BF),
         down=((m, r, w), F32),
         resid=((m, r, w), F32),
@@ -683,7 +774,7 @@
     return {name + TAIL: pltpu.VMEM(shape[1:], kind) for name, (shape, kind) in shapes.items()}
 
 
-def line_scratch(c):
+def line_buffers(c):
     ar = c.n // 2 * c.r
     return dict(
         xbuf=pltpu.VMEM((2, ar, c.width), BF),
@@ -693,151 +784,157 @@
         step_got=pltpu.VMEM((ar, c.width), BF),
         ysend=pltpu.VMEM((c.r, c.width), BF),
         ygot=pltpu.VMEM((c.r, c.width), BF),
-        lsem=dma(40),
-        fsem=dma(1),
-        hs=dma(1),
-        hr=dma(1),
-        ys=dma(2),
-        yr=dma(2),
-        **gather_sems(c.n // 2),
-        **scatter_sems(c.n // 2, HALVES),
-    )
-
-
-def forward_tick(c, k, weights, data, tables, stash):
+        lv=pltpu.VMEM((c.r, c.per), BF),
+    )
+
+
+def stage_sems(c):
+    return dict(
+        fsem=dma(1), hs=dma(1), hr=dma(1), ys=dma(2), yr=dma(2), **gather_sems(c.n // 2), **scatter_sems(c.n // 2, HALVES)
+    )
+
+
+def forward_buffers(c):
     shapes = stash_shapes(c)
     own = {name: shapes[name] for name in shapes if name not in ("xlow", "nfull", "pfull")}
+    return dict(nbuf=pltpu.VMEM((2 * c.r, c.width), BF), **scratch_of(own), **line_buffers(c))
+
+
+def shared_scratch(c):
+    return dict(**weight_scratch(c), lsem=dma(80), ready=pltpu.SemaphoreType.REGULAR)
+
+
+def forward_pass(c, weights, data, tables):
     scratch = dict(
-        hid=pltpu.VMEM((c.r, c.width), BF),
-        nbuf=pltpu.VMEM((2 * c.r, c.width), BF),
-        lv=pltpu.VMEM((c.r, c.per), BF),
-        **scratch_of(own),
-        **weight_scratch(c),
-        **line_scratch(c),
+        **twice(c, forward_buffers(c), stage_sems(c) | dict(hid=pltpu.VMEM((c.r, c.width), BF))), **shared_scratch(c)
     )
     return launch(
-        lambda o: forward_kernel(c, k, o),
-        k,
+        lambda o: forward_kernel(c, o),
+        0,
         dict(**weights, hidden=data.hidden, lin=data.lin),
         tables,
-        shapes,
+        stash_shapes(c),
         scratch,
-        stash,
-    )
-
-
-def backward_kernel(c, k, o):
-    p = place(c.n)
+    )
+
+
+def backward_stages(c, p, o, v, m, w, local):
     r, width, hb2 = c.r, c.width, 2 * c.hb
-    A = p.A
-    m = jnp.clip(2 - k - p.s, 0, 1)
-    active = (2 - k - p.s >= 0) & (2 - k - p.s <= 1)
-    local = Local(o.lsem)
     pair = (p.s, p.d, 1 - p.t)
-
-    greet(p, active, k >= 1)
-    hand = k and rcopy(o.ilow.at[min(max(2 - k, 0), 1)], o.hid, o.hs.at[0], o.hr.at[0], (1 - p.s, p.d, p.t))
-    if k >= 1:
-        pl.when(p.s == 1)(hand.start)
-
-    @pl.when(active)
-    def _():
-        mine, theirs = rows_of(p.t, r), rows_of(1 - p.t, r)
-        gain = lambda i: o.gains[i : i + 1, :]
-        first = pltpu.make_async_copy(o.cot.at[m], o.hid, o.fsem.at[0])
-        pl.when(p.s == 1)(first.start)
-        need = {}
-        need[0] = [local(o.proj.at[m], o.proj_v), local(o.graw.at[m], o.graw_v), local(o.lin.at[m], o.lv)]
-        need[1] = [local(o.down.at[m], o.down_v)]
-        w = load_weights(c, o, local)
-        need[2] = [local(o.gate.at[m], o.gate_v), local(o.up.at[m], o.up_v)]
-        need[3] = [local(o.comb.at[m], o.comb_v), local(o.att.at[m], o.att_v), local(o.lraw.at[m], o.lraw_v)]
-        need[4] = [local(o.xlow.at[m], o.xlow_v), local(o.qraw.at[m], o.qraw_v)]
-
-        def have(i):
-            for copy in need[i]:
-                copy.wait()
-
-        pl.when(p.s == 1)(first.wait)
-        if k >= 1:
-            pl.when(p.s == 0)(hand.wait_recv)
+    mine, theirs = rows_of(p.t, r), rows_of(1 - p.t, r)
+    gain = lambda i: o.gains[i : i + 1, :]
+    hand = rcopy(v.hid, v.hid, v.hs.at[0], v.hr.at[0], (1 - p.s, p.d, p.t))
+    first = pltpu.make_async_copy(o.cot.at[m], v.hid, v.fsem.at[0])
+    send = rcopy(v.abuf.at[mine], v.abuf.at[mine], v.ys.at[0], v.yr.at[0], pair)
+    swap = rcopy(v.ysend, v.ygot, v.ys.at[1], v.yr.at[1], pair)
+    keep, need = [], {}
+
+    def stash(*pairs):
+        keep.extend(local(src, dst.at[m]) for src, dst in pairs)
+
+    def fetch():
+        loads = (
+            ((o.proj, v.proj_v), (o.graw, v.graw_v), (o.lin, v.lv)),
+            ((o.down, v.down_v),),
+            ((o.gate, v.gate_v), (o.up, v.up_v)),
+            ((o.comb, v.comb_v), (o.att, v.att_v), (o.lraw, v.lraw_v)),
+            ((o.xlow, v.xlow_v), (o.qraw, v.qraw_v)),
+        )
+        for i, group in enumerate(loads):
+            need[i] = [local(src.at[m], dst) for src, dst in group]
+
+    def have(i):
+        for copy in need[i]:
+            copy.wait()
+
+    def begin():
+        if c.slots == 1:
+            fetch()
+
+        @pl.when(p.s == 1)
+        def _():
+            first.start()
+            first.wait()
+
+        pl.when(p.s == 0)(hand.wait_recv)
         have(0)
-        o.ggr_v[...] = jnp.zeros_like(o.ggr_v)
-        dres = o.hid[...].astype(F32)
-        dproj, o.ggr_v[5:6, :] = rms_back(o.proj_v[...], gain(5), dres)
-        o.plow_v[...] = dproj.astype(BF)
-        w.sm.wait()
-        dmid = nn(o.plow_v[...], o.sm_v[cols_of(LP)])
-        value, slope = gelu_both(o.graw_v[...])
-        o.lgrad_v[...] = value * dmid
-        o.grlow_v[...] = (dmid * o.lv[...].astype(F32) * slope).astype(BF)
-        dres = o.hid[...].astype(F32) + nt(o.grlow_v[...], o.sm_v[cols_of(LG)])
-        o.dcomb_v[...] = dres
+        v.ggr_v[...] = jnp.zeros_like(v.ggr_v)
+        dproj, v.ggr_v[5:6, :] = rms_back(v.proj_v[...], gain(5), v.hid[...].astype(F32))
+        v.plow_v[...] = dproj.astype(BF)
+        w.sm()
+        dmid = nn(v.plow_v[...], o.sm_v[cols_of(LP)])
+        value, slope = gelu_both(v.graw_v[...])
+        v.lgrad_v[...] = value * dmid
+        v.grlow_v[...] = (dmid * v.lv[...].astype(F32) * slope).astype(BF)
+        dres = v.hid[...].astype(F32) + nt(v.grlow_v[...], o.sm_v[cols_of(LG)])
+        v.igrad_v[...] = dres
         have(1)
-        ddown, o.ggr_v[4:5, :] = rms_back(o.down_v[...], gain(4), dres)
-        o.xbuf[p.b, rows_of(p.a, r), :] = ddown.astype(BF)
-        arrive, gathered = line_gather(p, o.xbuf, r, (o.gzs, o.gzr, o.gxs, o.gxr))
-        w.dw.wait()
-        have(2)
-
-        def hidden_part(col):
-            @tiles(hb2, min(256, hb2))
-            def _(at):
-                dgeglu = nn(o.xbuf[col], o.dw_v[:, at])
-                value, slope = gelu_both(o.gate_v[col, :, at])
-                o.dul_v[col, :, at] = (dgeglu * value).astype(BF)
-                o.dgl_v[col, :, at] = (dgeglu * o.up_v[col, :, at] * slope).astype(BF)
-
-        def down_part(col, dest, h):
-            start, size = c.halves[h]
-
-            @tiles(size, 256)
-            def _(at):
-                at = pl.ds(pl.multiple_of(start + at.start, 256), 256)
-                part = nt(o.dgl_v[col], o.gw_v[at, :]) + nt(o.dul_v[col], o.uw_v[at, :])
-                dest[:, at] = part.astype(dest.dtype)
-
-        hidden_part(p.b)
-        arrive()
-        hidden_part(1 - p.b)
-        w.gw.wait()
-        w.uw.wait()
-        start, carry, collect, finish = line_scatter(
-            p, o.acc, o.other, o.got, o.step_got, r, c.halves, (o.rxs, o.rxr, o.rzs, o.rzr), o.down_v
-        )
-        for h in range(HALVES):
-            down_part(1 - p.b, o.other, h)
-            start(h)
-        for h in range(HALVES):
-            down_part(p.b, o.acc, h)
-            carry(h)
-        for h in range(HALVES):
-            collect(h)
+        ddown, v.ggr_v[4:5, :] = rms_back(v.down_v[...], gain(4), dres)
+        v.xbuf[p.b, rows_of(p.a, r), :] = ddown.astype(BF)
+        line.begin()
+        stash((v.lgrad_v, o.lgrad), (v.plow_v, o.plow), (v.grlow_v, o.grlow))
+
+    def hidden_part(col):
+        @tiles(hb2, min(256, hb2))
+        def _(at):
+            dgeglu = nn(v.xbuf[col], o.dw_v[:, at])
+            value, slope = gelu_both(v.gate_v[col, :, at].astype(F32))
+            up = v.up_v[col, :, at].astype(F32)
+            v.up_v[col, :, at] = (dgeglu * value).astype(BF)
+            v.gate_v[col, :, at] = (dgeglu * up * slope).astype(BF)
+
+    def down_part(col, dest, h):
+        start, size = c.halves[h]
+
+        @tiles(size, 256)
+        def _(at):
+            at = pl.ds(pl.multiple_of(start + at.start, 256), 256)
+            part = nt(v.gate_v[col], o.gw_v[at, :]) + nt(v.up_v[col], o.uw_v[at, :])
+            dest[:, at] = part.astype(dest.dtype)
+
+    def ready(i):
+        if i == 0:
+            w.dw()
+            have(2)
+        else:
+            w.gw()
+            w.uw()
+
+    line = line_stages(c, p, v, hidden_part, down_part, ready)
+
+    def rest():
+        line.rest()
+        stash((v.xbuf, o.dfull), (v.gate_v, o.dgl), (v.up_v, o.dul))
+
+    def middle():
+        line.total()
         have(3)
-        dcomb, o.ggr_v[3:4, :] = rms_back(o.comb_v[...], gain(3), o.down_v[...])
-        even = (o.dcomb_v[...] + dcomb) * RH
-        o.dcomb_v[...] = even
-        datt, o.ggr_v[1:2, :] = rms_back(o.att_v[...], gain(1), even)
-        o.abuf[mine, :] = datt.astype(BF)
-        send = rcopy(o.abuf.at[mine], o.abuf.at[mine], o.ys.at[0], o.yr.at[0], pair)
+        dcomb, v.ggr_v[3:4, :] = rms_back(v.comb_v[...], gain(3), v.down_v[...])
+        even = (v.igrad_v[...] + dcomb) * RH
+        v.igrad_v[...] = even
+        datt, v.ggr_v[1:2, :] = rms_back(v.att_v[...], gain(1), even)
+        v.abuf[mine, :] = datt.astype(BF)
         send.start()
-        dlraw, o.ggr_v[2:3, :] = rms_back(o.lraw_v[...], gain(2), o.dcomb_v[...])
-        o.lrlow_v[...] = dlraw.astype(BF)
-        o.lmg_v[...] = nn(o.lrlow_v[...], o.sm_v[cols_of(LR)]).astype(BF)
-        o.proj_v[...] = o.dcomb_v[...] + nt(o.lmg_v[...], o.sm_v[cols_of(LL)])
-        w.ot.wait()
-        rcopy(o.abuf.at[theirs], o.abuf.at[theirs], o.ys.at[0], o.yr.at[0], pair).wait_recv()
+        dlraw, v.ggr_v[2:3, :] = rms_back(v.lraw_v[...], gain(2), v.igrad_v[...])
+        v.lrlow_v[...] = dlraw.astype(BF)
+        v.lmg_v[...] = nn(v.lrlow_v[...], o.sm_v[cols_of(LR)]).astype(BF)
+        v.proj_v[...] = v.igrad_v[...] + nt(v.lmg_v[...], o.sm_v[cols_of(LL)])
+        stash((v.lrlow_v, o.lrlow), (v.lmg_v, o.lmg))
+
+    def heads():
+        w.ot()
+        rcopy(v.abuf.at[theirs], v.abuf.at[theirs], v.ys.at[0], v.yr.at[0], pair).wait_recv()
 
         @tiles(c.heads, 256)
         def _(at):
-            o.hgrad_v[:, at] = nn(o.abuf[...], o.ot_v[:, at]).astype(BF)
+            v.hgrad_v[:, at] = nn(v.abuf[...], o.ot_v[:, at]).astype(BF)
 
         have(4)
         cos, sin = o.cos[...], o.sin[...]
         q_gain, k_gain = o.gains[6:7, 0:HEAD], o.gains[7:8, 0:HEAD]
         allowed = o.allowed[m] > 0.5
         k_at, v_at = pl.ds(c.heads, HEAD), pl.ds(c.heads + HEAD, HEAD)
-        kraw, vraw = o.qraw_v[:, k_at], o.qraw_v[:, v_at]
+        kraw, vraw = v.qraw_v[:, k_at], v.qraw_v[:, v_at]
         key = rotate(kraw * rms_of(kraw) * k_gain, cos, sin).astype(BF)
         value = (vraw * rms_of(vraw)).astype(BF)
         dkey = jnp.zeros(kraw.shape, F32)
@@ -845,12 +942,12 @@
         dq_gain = jnp.zeros((1, HEAD), F32)
         for h in range(c.heads // HEAD):
             at = pl.ds(h * HEAD, HEAD)
-            raw = o.qraw_v[:, at]
+            raw = v.qraw_v[:, at]
             query = rotate(raw * rms_of(raw) * q_gain, cos, sin).astype(BF)
             scores = jnp.where(allowed, nt(query, key) * HEAD**-0.5, NEG)
             shifted = jnp.exp(scores - jnp.max(scores, axis=-1, keepdims=True))
             prob = shifted / jnp.sum(shifted, axis=-1, keepdims=True)
-            hgrad = o.hgrad_v[:, at]
+            hgrad = v.hgrad_v[:, at]
             dprob = nt(hgrad, value)
             dvalue = dvalue + tn(prob.astype(BF), hgrad)
             inner = jnp.sum(prob * dprob, axis=-1, keepdims=True)
@@ -859,51 +956,71 @@
             dkey = dkey + tn(dscore, query) * HEAD**-0.5
             draw, dg = rms_back(raw, q_gain, rotate_back(dquery, cos, sin))
             dq_gain = dq_gain + dg
-            o.dqkv_v[:, at] = draw.astype(BF)
+            v.dqkv_v[:, at] = draw.astype(BF)
         draw, dk_gain = rms_back(kraw, k_gain, rotate_back(dkey, cos, sin))
-        o.dqkv_v[:, k_at] = draw.astype(BF)
-        o.dqkv_v[:, v_at] = plain_back(vraw, dvalue).astype(BF)
-        o.ggr_v[6:7, 0:HEAD] = dq_gain
-        o.ggr_v[7:8, 0:HEAD] = dk_gain
-        w.qkv.wait()
+        v.dqkv_v[:, k_at] = draw.astype(BF)
+        v.dqkv_v[:, v_at] = plain_back(vraw, dvalue).astype(BF)
+        v.ggr_v[6:7, 0:HEAD] = dq_gain
+        v.ggr_v[7:8, 0:HEAD] = dk_gain
+        w.qkv()
 
         @tiles(width, 256)
         def _(at):
-            o.acc[0 : 2 * r, at] = nt(o.dqkv_v[...], o.qkv_v[at, :])
-
-        o.ysend[...] = o.acc[theirs, :].astype(BF)
-        swap = rcopy(o.ysend, o.ygot, o.ys.at[1], o.yr.at[1], pair)
+            v.acc[0 : 2 * r, at] = nt(v.dqkv_v[...], o.qkv_v[at, :])
+
+        v.ysend[...] = v.acc[theirs, :].astype(BF)
         swap.start()
+        stash((v.abuf, o.afull), (v.dqkv_v, o.dqkv))
+
+    def entry():
         swap.wait()
-        dnorm = o.proj_v[...] + o.acc[mine, :] + o.ygot[...].astype(F32)
-        dx, o.ggr_v[0:1, :] = rms_back(o.xlow_v[...].astype(F32), gain(0), dnorm)
-        dx = dx + o.dcomb_v[...]
-        o.igrad_v[...] = dx
-        o.ilow_v[...] = dx.astype(BF)
+        dnorm = v.proj_v[...] + v.acc[mine, :] + v.ygot[...].astype(F32)
+        dx, v.ggr_v[0:1, :] = rms_back(v.xlow_v[...].astype(F32), gain(0), dnorm)
+        dx = dx + v.igrad_v[...]
+        v.igrad_v[...] = dx
+
+        @pl.when(p.s == 1)
+        def _():
+            v.hid[...] = dx.astype(BF)
+            if m == 0:
+                pl.semaphore_wait(o.ready, 1)
+            hand.start()
+
+        stash((v.igrad_v, o.igrad), (v.ggr_v, o.ggr))
+
+    def end():
         send.wait_send()
-        out = [
-            local(o.igrad_v, o.igrad.at[m]),
-            local(o.ilow_v, o.ilow.at[m]),
-            local(o.lgrad_v, o.lgrad.at[m]),
-            local(o.plow_v, o.plow.at[m]),
-            local(o.grlow_v, o.grlow.at[m]),
-            local(o.xbuf, o.dfull.at[m]),
-            local(o.dgl_v, o.dgl.at[m]),
-            local(o.dul_v, o.dul.at[m]),
-            local(o.lrlow_v, o.lrlow.at[m]),
-            local(o.lmg_v, o.lmg.at[m]),
-            local(o.abuf, o.afull.at[m]),
-            local(o.dqkv_v, o.dqkv.at[m]),
-            local(o.ggr_v, o.ggr.at[m]),
-        ]
-        gathered()
-        for h in range(HALVES):
-            finish(h)
-        for copy in out:
+        line.end()
+        pl.when(p.s == 1)(hand.wait_send)
+        for copy in keep:
             copy.wait()
 
-    if k >= 1:
-        pl.when(p.s == 1)(hand.wait_send)
+    return {
+        FIRST: begin, GIVE: line.give, OWN: line.own, REST: rest, SUMS: line.sums, MIDDLE: middle, HEADS_STAGE: heads,
+        ENTRY: entry, LAST: end, BEGIN: fetch,
+    }
+
+
+BACKWARD_ORDER = (
+    (FIRST, 0), (GIVE, 0), (OWN, 0), (FIRST, 1), (REST, 0), (GIVE, 1), (OWN, 1), (SUMS, 0), (REST, 1), (MIDDLE, 0),
+    (HEADS_STAGE, 0), (SUMS, 1), (ENTRY, 0), (MIDDLE, 1), (HEADS_STAGE, 1), (ENTRY, 1),
+)
+
+
+def backward_kernel(c, o):
+    p = place(c.n)
+    local = Local(o.lsem)
+    views = [view(c, o, m, backward_buffers(c), stage_sems(c) | dict(hid=None)) for m in range(2)]
+    late = {}
+    w = SimpleNamespace(**{name: (lambda name=name: late[name]()) for name in ("sm", "qkv", "ot", "gw", "uw", "dw")})
+    stages = [backward_stages(c, p, o, views[m], m, w, local) for m in range(2)]
+    if c.slots == 2:
+        stages[0][BEGIN]()
+    late.update(vars(waits_of(c, o, local)))
+    if c.slots == 2:
+        stages[1][BEGIN]()
+    enter(p, o, 1)
+    run_stages(c, p, BACKWARD_ORDER, stages)
 
 
 def grad_shapes(c):
@@ -911,7 +1028,6 @@
     ar, hb2 = c.n // 2 * c.r, 2 * c.hb
     return dict(
         igrad=((m, r, w), F32),
-        ilow=((m, r, w), BF),
         lgrad=((m, r, c.per), F32),
         plow=((m, r, w), BF),
         grlow=((m, r, c.per), BF),
@@ -929,29 +1045,29 @@
 READ = ("proj", "graw", "down", "gate", "up", "comb", "att", "lraw", "xlow", "qraw")
 
 
-def backward_tick(c, k, weights, data, tables, stash, grads):
-    shapes = grad_shapes(c)
-    kept_shapes = stash_shapes(c)
-    own = {name: shapes[name] for name in shapes if name not in ("dfull", "afull")}
-    scratch = dict(
-        hid=pltpu.VMEM((c.r, c.width), BF),
+def backward_buffers(c):
+    shapes, kept = grad_shapes(c), stash_shapes(c)
+    own = {name: shapes[name] for name in shapes if name not in ("dfull", "afull", "dgl", "dul")}
+    return dict(
         abuf=pltpu.VMEM((2 * c.r, c.width), BF),
-        lv=pltpu.VMEM((c.r, c.per), BF),
-        dcomb_v=pltpu.VMEM((c.r, c.width), F32),
         hgrad_v=pltpu.VMEM((2 * c.r, c.heads), BF),
         **scratch_of(own),
-        **scratch_of({name: kept_shapes[name] for name in READ}),
-        **weight_scratch(c),
-        **line_scratch(c),
+        **scratch_of({name: kept[name] for name in READ}),
+        **line_buffers(c),
+    )
+
+
+def backward_pass(c, weights, data, tables, stash):
+    scratch = dict(
+        **twice(c, backward_buffers(c), stage_sems(c) | dict(hid=pltpu.VMEM((c.r, c.width), BF))), **shared_scratch(c)
     )
     return launch(
-        lambda o: backward_kernel(c, k, o),
-        3 + k,
+        lambda o: backward_kernel(c, o),
+        3,
         dict(**weights, cot=data.cot, lin=data.lin, **{name: stash[name] for name in READ}),
         tables,
-        shapes,
+        grad_shapes(c),
         scratch,
-        grads,
     )
 
 
@@ -1189,7 +1305,7 @@
         total=qkv + heads + small, hb=gate_weight.shape[2] // n,
         cuts=((0, qkv), (qkv, heads), (qkv + heads, small)),
         parts=(*((i, 512) for i in range(0, qkv + heads, 512)), (base, small - per), (base + small - per, per)),
-        ag=(12.0, 6.0, 12.0), tr=(1.0, 2.5, 30.0, 3.0), by_matrix=True, kg=(6.0, 2.9, 2.0, 20.0, 12.0, 12.0),
+        slots=2 if n <= 8 else 1, ag=(12.0, 6.0, 12.0), tr=(1.0, 2.5, 30.0, 3.0), by_matrix=True, kg=(6.0, 2.9, 2.0, 20.0, 12.0, 12.0),
         halves=tuple((h * width // HALVES, width // HALVES) for h in range(HALVES)),
     )
     gains = jnp.stack(
@@ -1225,11 +1341,8 @@
     tables = dict(gains=gain_rows, cos=jnp.cos(angles), sin=jnp.sin(angles), allowed=allowed.astype(F32))
     data = SimpleNamespace(hidden=hidden[:, 0], lin=layer_inputs[0, :, 0], cot=cotangent[:, 0])
 
-    stash, grads = None, None
-    for k in range(3):
-        stash = forward_tick(c, k, weights, data, tables, stash)
-    for k in range(3):
-        grads = backward_tick(c, k, weights, data, tables, stash, grads)
+    stash = forward_pass(c, weights, data, tables)
+    grads = backward_pass(c, weights, data, tables, stash)
     f, g = SimpleNamespace(**stash), SimpleNamespace(**grads)
 
     def pair_grad(inputs, outs):

time: 942 us -> 836 us (0.89)
  Pallas kernels: 869 us -> 759 us
    pallas_call x9 -> x5, Pallas kernels: 869 us -> 759 us  [launch(): pl.pallas_call(run, out_shape=[jax.ShapeDtypeStruct(*spec) for spec in ou...]
where the time goes in v2:
time: 836 us; the launch traced here: 825 us
  Pallas kernels  759 us (91%)
  local copies, waits for them, and re-layouts  36.4 us (4%)
  matrix products  20.9 us (2%)
    pallas_call x5, Pallas kernels, launch(): pl.pallas_call(run, out_shape=[jax.ShapeDtypeStruct(*spec) for spec in ou...  759 us
    unnamed x56, local copies, waits for them, and re-layouts  23.3 us
    dot_general x3, matrix products, tn(): lax.dot_general(x, w, (((0,), (0,)), ((), ())), preferred_element_type=F32)  20.9 us

profile of v2, /device:TPU:0, one launch (start us, length us, event | category | flops | bytes accessed | tf_op | source)
XLA Modules:
  0.0 824.7 jit_solution(3848172460946422971)
XLA Ops:
  3.7 0.8 copy.103
  4.6 0.8 copy.104
  5.4 0.9 copy.102
  6.3 0.9 copy.111
  7.1 0.8 copy.105
  8.0 0.8 copy.106
  8.8 0.8 copy.107
  9.6 0.8 copy.108
  11.4 0.9 fusion
  12.3 1.0 copy.112
  13.9 4.6 copy.113
  18.5 146.0 %shard_map.393 = (bf16[2048,3328]{1,0:T(8,128)(2,1)}, bf16[2048,1024]{1,0:T(8,128)(2,1)}, bf16[2048,1024]{1,0:T(8,128)(2,1)}, bf16[2048,1024]{1,0:T(8,128)(2,1)}, f32[8,2048]{1,0:T(8,128)}) custom-call(bf16[256,3328]{1,0:T(8,128)(2,1)} %copy-done, bf16[256,4096]{1,0:T(8,128)(2,1)} %bitcast.104, bf16[256,4096]{1,0:T(8,128)(2,1)} %bitcast.105, ...), custom_call_target="tpu_custom_call" | custom-call | tf_op jit(solution)/shard_map/pallas_call | solution.py:306
  164.5 0.8 slice.63
  165.4 1.5 select_maximum_fusion.refs_6_.refs_16_
  166.9 147.2 %shard_map.394 = (bf16[2,64,2048]{2,1,0:T(8,128)(2,1)}, bf16[2,64,2048]{2,1,0:T(8,128)(2,1)}, bf16[2,128,2048]{2,1,0:T(8,128)(2,1)}, f32[2,128,1536]{2,1,0:T(8,1...) custom-call(bf16[2048,3328]{1,0:T(8,128)(2,1)} %get-tuple-element.70, ...), custom_call_target="tpu_custom_call" | custom-call | tf_op jit(solution)/shard_map/pallas_call | solution.py:306
  314.1 292.2 %shard_map.395 = (f32[2,64,2048]{2,1,0:T(8,128)}, f32[2,64,256]{2,1,0:T(8,128)}, bf16[2,64,2048]{2,1,0:T(8,128)(2,1)}, bf16[2,64,256]{2,1,0:T(8,128)(2,1)}, bf16...) custom-call(bf16[2048,3328]{1,0:T(8,128)(2,1)} %get-tuple-element.70, ...), custom_call_target="tpu_custom_call" | custom-call | tf_op jit(solution)/shard_map/pallas_call | solution.py:306
  606.4 1.0 fusion.10
  607.4 0.9 add_convert_fusion
  608.7 1.0 pad.35.refs_11_
  609.8 8.5 %bitcast_convert_fusion.refs_14_ = bf16[2048,1024]{1,0:T(8,128)(2,1)} fusion(bf16[2,2,256,2048]{3,2,1,0:T(8,128)(2,1)} %get-tuple-element.103, bf16[2,2,256,1024]{3,2,1,0:T(8,128)(2,1)S(1)} %copy-done.10), kind=kOutput, calls=%fused_computation | convolution fusion | flops 4297064448 | bytes 10485760 | tf_op jit(solution)/shard_map/dot_general | solution.py:78
  618.2 6.2 bitcast_convert_fusion.2.refs_12_
  624.5 6.2 bitcast_convert_fusion.1.refs_13_
  630.7 165.7 %shard_map.396 = (f32[256,3328]{1,0:T(8,128)}, bf16[256,4096]{1,0:T(8,128)(2,1)}, bf16[256,4096]{1,0:T(8,128)(2,1)}, bf16[256,4096]{1,0:T(8,128)(2,1)}) custom-call(bf16[2,128,2048]{2,1,0:T(8,128)(2,1)} %get-tuple-element.88.refs_0_, bf16[2,128,1536]{2,1,0:T(8,128)(2,1)} %get-tuple-element.89.refs_1_, bf16[2,128,2048]{2,1,0:T(8,128)(2,1)} %get-tuple-element.90.refs_2_, ...), custom_call_target="tpu_custom_call" | custom-call | tf_op jit(solution)/shard_map/pallas_call | solution.py:306
  796.4 0.9 slice_bitcast_fusion.1
  798.0 1.0 slice_bitcast_fusion
  799.0 0.8 copy.131
  799.8 8.3 %shard_map.397 = (f32[256,1024]{1,0:T(8,128)}, f32[256,256]{1,0:T(8,128)}, f32[256,256]{1,0:T(8,128)}, f32[256,128]{1,0:T(8,128)}, f32[256,256]{1,0:T(8,128)}, /...) custom-call(f32[256,3328]{1,0:T(8,128)} %get-tuple-element.105.refs_0_, ...), custom_call_target="tpu_custom_call" | custom-call | tf_op jit(solution)/shard_map/pallas_call | solution.py:306
  808.2 1.0 slice_bitcast_fusion.3
  809.2 0.9 slice_bitcast_fusion.2
  816.2 5.7 copy.129
  821.9 0.8 copy.153
  822.7 1.0 copy.154
  (68 shorter events, 12.4 us)
Async XLA Ops:
  0.7 12.7 %copy-start.2 = (bf16[1,1024,256]{2,1,0:T(8,128)(2,1)S(1)}, bf16[1,1024,256]{2,1,0:T(8,128)(2,1)}, u32[]{:S(2)}) copy-start(bf16[1,1024,256]{2,1,0:T(8,128)(2,1)} %param.33) | copy-start | bytes 1572868
  0.7 13.0 %copy-start.5 = (bf16[1,256,256]{2,1,0:T(8,128)(2,1)S(1)}, bf16[1,256,256]{2,1,0:T(8,128)(2,1)}, u32[]{:S(2)}) copy-start(bf16[1,256,256]{2,1,0:T(8,128)(2,1)} %param.29) | copy-start | bytes 393220
  0.7 12.9 %copy-start.3 = (bf16[1,256,1024]{2,1,0:T(8,128)(2,1)S(1)}, bf16[1,256,1024]{2,1,0:T(8,128)(2,1)}, u32[]{:S(2)}) copy-start(bf16[1,256,1024]{2,1,0:T(8,128)(2,1)} %param.28) | copy-start | bytes 1572868
  3.6 10.0 %copy-start.6 = (bf16[1,256,256]{2,1,0:T(8,128)(2,1)S(1)}, bf16[1,256,256]{2,1,0:T(8,128)(2,1)}, u32[]{:S(2)}) copy-start(bf16[1,256,256]{2,1,0:T(8,128)(2,1)} %param.30) | copy-start | bytes 393220
  12.3 1.5 copy-start.7
  13.9 4.6 copy-start
  606.4 3.4 copy-start.10
  609.8 8.5 %copy-start.9 = (bf16[2,2,256,2048]{3,2,1,0:T(8,128)(2,1)S(1)}, bf16[2,2,256,2048]{3,2,1,0:T(8,128)(2,1)}, u32[]{:S(2)}) copy-start(bf16[2,2,256,2048]{3,2,1,0:T(8,128)(2,1)} %get-tuple-element.100) | copy-start | bytes 12582916
  609.8 8.5 %copy-start.12 = (bf16[2,2,256,1024]{3,2,1,0:T(8,128)(2,1)S(1)}, bf16[2,2,256,1024]{3,2,1,0:T(8,128)(2,1)}, u32[]{:S(2)}) copy-start(bf16[2,2,256,1024]{3,2,1,0:T(8,128)(2,1)} %get-tuple-element.101) | copy-start | bytes 6291460
  618.2 6.2 copy-start.11
  816.2 5.7 copy-start.4
  816.2 6.5 copy-start.1
  821.9 1.8 copy-start.8

commit v3 on v2

--- a/solution.py
+++ b/solution.py
@@ -19,9 +19,11 @@
 LANES = 128
 GELU_C = math.sqrt(2.0 / math.pi)
 GELU_K = 0.044715
-VMEM_LIMIT = 60 << 20
+VMEM_LIMIT = 61 << 20
 HALVES = 2
 GATHER_PARTS = 2
+GO_AT = 60.0
+KG = (2.5, 3.0, (2.1, 3.2, 4.3), 0.6, 2.6)
 
 
 def rms_of(v):
@@ -271,7 +273,7 @@
         for below in range(lowest(0, n)):
             message(h, 1 << below).wait_recv()
             total = total + got[pl.ds(((1 << below) - 1) * size, size), cols(h)].astype(F32)
-        out[:, cols(h)] = total
+        out[:, cols(h)] = total.astype(BF)
 
     def finish(h):
         for mask in range(1, n):
@@ -297,23 +299,24 @@
 VM = pl.BlockSpec(memory_space=pltpu.VMEM)
 
 
-def launch(kernel, cid, hbm_in, vmem_in, outs, scratch):
-    everything = [*hbm_in, *vmem_in, *outs, *scratch]
+def launch(kernel, cid, hbm_in, vmem_in, outs, scratch, small=None):
+    small = small or {}
+    everything = [*hbm_in, *vmem_in, *outs, *small, *scratch]
 
     def run(*refs):
         kernel(SimpleNamespace(**dict(zip(everything, refs))))
 
     results = pl.pallas_call(
         run,
-        out_shape=[jax.ShapeDtypeStruct(*spec) for spec in outs.values()],
+        out_shape=[jax.ShapeDtypeStruct(*spec) for spec in (*outs.values(), *small.values())],
         in_specs=[HBM] * len(hbm_in) + [VM] * len(vmem_in),
-        out_specs=[HBM] * len(outs),
+        out_specs=[HBM] * len(outs) + [VM] * len(small),
         scratch_shapes=list(scratch.values()),
         compiler_params=pltpu.CompilerParams(
             collective_id=cid, has_side_effects=cid is not None, vmem_limit_bytes=VMEM_LIMIT
         ),
     )(*hbm_in.values(), *vmem_in.values())
-    return dict(zip(outs, results))
+    return dict(zip((*outs, *small), results))
 
 
 def fetch_kernel(c, o):
@@ -343,7 +346,7 @@
 
     def give(mask, bit, q):
         rows, cs = rows_of(flip(p.d, mask), R), pl.ds(*cuts[q])
-        src = o.pk.at[rows, cs] if mask else o.pack.at[:, cs]
+        src = o.pk.at[rows, cs] if mask else o.pack_v.at[:, cs]
         far = mask | 1 << bit
         return rcopy(src, o.pk.at[rows, cs], o.gs.at[far, q], o.gr.at[far, q], (p.s, flip(p.d, 1 << bit), p.t))
 
@@ -357,7 +360,7 @@
         for bit in reversed(range(lowest(mask, n))):
             give(mask, bit, q).start()
 
-    ffn = ((o.gate, o.gw), (o.up, o.uw), (o.down, o.dw))
+    ffn = ((o.gate, o.gw), (o.up, o.uw), (o.down_t, o.dw))
 
     def block(m, source, half):
         return ffn[m][1].at[rows_of(source, R), rows_of(half, hb)]
@@ -379,23 +382,69 @@
         src = ffn[m][0].at[:, rows_of(p.d, hb)] if k == 0 else block(m, source, half)
         return rcopy(src, block(m, source, half), o.ys.at[k, m], o.yr.at[k, m], pair)
 
-    bounce = [local(o.pack, o.pack_v)]
-    for m in range(3):
-        bounce.append(local(ffn[m][0].at[:, rows_of(p.d, hb)], o.block_v.at[m]))
+    qkv, base, rank = c.qkv, c.qkv + c.heads, c.rank
+    first = [
+        local(o.query, o.pack_v.at[:, pl.ds(0, c.heads)]),
+        local(o.key, o.pack_v.at[:, pl.ds(c.heads, HEAD)]),
+        local(o.value, o.pack_v.at[:, pl.ds(c.heads + HEAD, HEAD)]),
+    ]
+    second = [local(o.out, o.out_v)]
+    third = [local(o.lg, o.pack_v.at[:, pl.ds(base + 2 * LANES, c.per)]), local(o.lp, o.lp_v), local(o.lr, o.lr_v)]
+    fourth = [local(o.down, o.down_v)]
+    bounce = [local(ffn[m][0].at[:, rows_of(p.d, hb)], o.block_v.at[m]) for m in range(2)]
+
+    def turned(x):
+        return x.astype(F32).T.astype(BF)
+
+    def prepare(q):
+        if q == 0:
+            for copy in first:
+                copy.wait()
+        elif q == 1:
+            for copy in second:
+                copy.wait()
+            for i in range(0, c.heads, HEAD):
+                o.pack_v[:, pl.ds(qkv + i, HEAD)] = turned(o.out_v[pl.ds(i, HEAD), :])
+        else:
+            for copy in third:
+                copy.wait()
+            o.rows_v[...] = jnp.zeros_like(o.rows_v)
+            for i, gain in enumerate((o.g0, o.g1, o.g2, o.g3, o.g4, o.g5, o.g6, o.g7)):
+                o.rows_v[rank + i : rank + i + 1, 0 : gain.shape[1]] = gain[...].astype(F32)
+            left = o.rows_v[...].T
+            o.pack_v[:, pl.ds(base, LANES)] = left.astype(BF)
+            o.pack_v[:, pl.ds(base, rank)] = o.ll[...]
+            o.rows_v[...] = jnp.zeros_like(o.rows_v)
+            o.rows_v[0:rank, :] = o.lr_v[...].astype(F32)
+            o.pack_v[:, pl.ds(base + LANES, LANES)] = o.rows_v[...].T.astype(BF)
+            o.pack_v[:, pl.ds(base + 2 * LANES + c.per, c.per)] = turned(o.lp_v[...])
+
+    def prepare_down():
+        for copy in fourth:
+            copy.wait()
+        for k in range(n):
+            o.down_t[:, pl.ds(k * hb, hb)] = turned(o.down_v[pl.ds(k * hb, hb), :])
+        bounce.append(local(o.down_t.at[:, rows_of(p.d, hb)], o.block_v.at[2]))
+
     events = []
     inner = sorted((mask for mask in range(2, n, 2)), key=lambda mask: (-lowest(mask, n), mask))
     for q in range(len(cuts)):
-        events.append((0.0 + 0.1 * q, lambda q=q: pass_on(0, q)))
+        events.append((0.0 + 0.1 * q, lambda q=q: (prepare(q), pass_on(0, q))))
         for i, mask in enumerate(inner):
             events.append((c.ag[0] + c.ag[1] * q + c.ag[2] * i, lambda q=q, mask=mask: pass_on(mask, q)))
+    events.append((c.tr[0] + c.tr[1] * (2 * n - 2), prepare_down))
     for k in range(n):
         for m in range(3):
-            at = m * n + k if c.by_matrix else k * 3 + m
+            at = m * n + k
             if k:
                 events.append((c.tr[0] + c.tr[1] * at, lambda m=m, k=k: trade(m, k).start()))
                 events.append((c.tr[2] + c.tr[3] * at, lambda m=m, k=k: (came(m, k).wait_recv(), share(m, k, p.t).start())))
             else:
                 events.append((c.tr[0] + c.tr[1] * at, lambda m=m: share(m, 0, p.t).start()))
+    def release():
+        pl.semaphore_signal(o.go, inc=1, device_id=(1 - p.s, p.d, p.t), device_id_type=MESH)
+
+    events.append((c.go_at, lambda: pl.when(p.s == 0)(release)))
     for _, run in sorted(events, key=lambda e: e[0]):
         run()
     for copy in bounce:
@@ -403,10 +452,6 @@
     waits.append(local(o.pack_v, o.pk.at[rows_of(p.d, R)]))
     for m in range(3):
         waits.append(local(o.block_v.at[m], block(m, p.d, p.t)))
-
-    @pl.when(p.s == 0)
-    def _():
-        pl.semaphore_signal(o.go, inc=1, device_id=(1 - p.s, p.d, p.t), device_id_type=MESH)
 
     for q in range(len(cuts)):
         for mask in range(1, n, 2):
@@ -690,14 +735,16 @@
     def tail():
         line.total()
         down = v.down_v[...]
-        v.resid_v[...] = v.comb_v[...] + down * rms_of(down) * gain(4)
-        graw = nn(v.resid_v[...].astype(BF), o.sm_v[cols_of(LG)])
+        resid = v.comb_v[...] + down * rms_of(down) * gain(4)
+        v.rf_v[...] = resid
+        v.resid_v[...] = resid.astype(BF)
+        graw = nn(v.resid_v[...], o.sm_v[cols_of(LG)])
         v.graw_v[...] = graw
         v.lv_wait()
         v.llow_v[...] = (gelu(graw) * v.lv[...].astype(F32)).astype(BF)
         proj = nt(v.llow_v[...], o.sm_v[cols_of(LP)])
         v.proj_v[...] = proj
-        v.act_v[...] = (v.resid_v[...] + proj * rms_of(proj) * gain(5)).astype(BF)
+        v.act_v[...] = (v.rf_v[...] + proj * rms_of(proj) * gain(5)).astype(BF)
 
         @pl.when(p.s == 0)
         def _():
@@ -760,7 +807,7 @@
         up=((m, 2, ar, hb2), BF),
         geglu=((m, 2, ar, hb2), BF),
         down=((m, r, w), F32),
-        resid=((m, r, w), F32),
+        resid=((m, r, w), BF),
         graw=((m, r, c.per), F32),
         llow=((m, r, c.per), BF),
         proj=((m, r, w), F32),
@@ -768,6 +815,7 @@
 
 
 TAIL = "_v"
+GROW = "grow"
 
 
 def scratch_of(shapes):
@@ -797,7 +845,7 @@
 def forward_buffers(c):
     shapes = stash_shapes(c)
     own = {name: shapes[name] for name in shapes if name not in ("xlow", "nfull", "pfull")}
-    return dict(nbuf=pltpu.VMEM((2 * c.r, c.width), BF), **scratch_of(own), **line_buffers(c))
+    return dict(nbuf=pltpu.VMEM((2 * c.r, c.width), BF), rf_v=pltpu.VMEM((c.r, c.width), F32), **scratch_of(own), **line_buffers(c))
 
 
 def shared_scratch(c):
@@ -1086,17 +1134,11 @@
     signal(pair)
     pl.semaphore_wait(barrier, n)
     local = Local(o.lsem)
-    ffn = (o.dg, o.du, o.dd)
+    outs = ((o.pfull, o.dgl), (o.pfull, o.dul), (o.dfull, o.geglu))
 
     def swap(m, k):
-        dest = lax.rem(p.d + k, n)
-        return rcopy(
-            ffn[m].at[rows_of(dest, R), rows_of(1 - p.t, hb)],
-            o.fgot.at[m, rows_of(dest, R)],
-            o.ys.at[m, k],
-            o.yr.at[m, k],
-            pair,
-        )
+        at = rows_of(lax.rem(p.d + k, n), R)
+        return rcopy(o.fsend.at[m, at], o.fgot.at[m, at], o.ys.at[m, k], o.yr.at[m, k], pair)
 
     def ffn_out(m, source):
         return (o.gg, o.gu, o.gd)[m].at[:, rows_of(source, hb)]
@@ -1111,11 +1153,30 @@
         source = lax.rem(p.d + n - k, n)
         return rcopy(o.fown.at[m, rows_of(p.d, R)], ffn_out(m, source), o.ts.at[m, k], o.tr.at[m, k], side)
 
-    owns = [local(ffn[m].at[:, rows_of(p.t, hb)], o.fown.at[m]) for m in range(3)]
     order = [*range(1, n), 0]
-    for m in range(3):
+    inputs = {0: [local(outs[0][0], o.x_v), local(outs[0][1], o.y_v.at[0])], 1: [local(outs[1][1], o.y_v.at[1])]}
+
+    def ffn_grad(m):
+        for copy in inputs[m]:
+            copy.wait()
+        y = o.y_v.at[m % 2]
+        tokens = 4 * y.shape[1]
+
+        @tiles(c.width, 256)
+        def _(rows):
+            x = o.x_v[:, :, :, rows].reshape(-1, 256)
+            mine = y[:, :, :, rows_of(p.t, hb)].reshape(-1, hb)
+            o.fown[m, rows, :] = tn(x, mine).astype(BF)
+            theirs = y[:, :, :, rows_of(1 - p.t, hb)].reshape(-1, hb)
+            o.fsend[m, rows, :] = tn(x, theirs).astype(BF)
+
         for k in order:
             swap(m, k).start()
+        if m == 0:
+            inputs[2] = [local(outs[2][1], o.y_v.at[0])]
+        if m == 1:
+            inputs[2].append(local(outs[2][0], o.x_v))
+
     need = [
         local(getattr(o, name), getattr(o, name + TAIL))
         for name in ("nfull", "dqkv", "afull", "heads", "lrlow", "lmid", "resid", "grlow", "plow", "llow", "lmg", "gcol")
@@ -1133,8 +1194,6 @@
 
     def ffn_block(m, k):
         rows = rows_of(lax.rem(p.d + k, n), R)
-        if k == order[0]:
-            owns[m].wait()
         swap(m, k).wait_recv()
         total = o.fown[m, rows, :].astype(F32) + o.fgot[m, rows, :].astype(F32)
         o.fown[m, rows, :] = total.astype(BF)
@@ -1161,30 +1220,32 @@
                 o.acc[rows, pl.ds(begin, LANES)] = jnp.where(lane < c.rank, left, gains).astype(BF)
 
             grad(o.lrlow_v, o.lmid_v, pl.ds(begin + LANES, LANES))
-            o.rlow_v[...] = o.resid_v[...].astype(BF)
-            grad(o.rlow_v, o.grlow_v, pl.ds(begin + 2 * LANES, c.per))
+            grad(o.resid_v, o.grlow_v, pl.ds(begin + 2 * LANES, c.per))
         else:
             grad(o.plow_v, o.llow_v, pl.ds(begin, c.per))
 
-    for copy in need:
-        copy.wait()
-    events = []
+    def attn_ready():
+        for copy in need:
+            copy.wait()
+
+    r0, per, lag, g1, g2 = c.kg
+    top = lowest(0, n)
+    events = [(-3.0, lambda: ffn_grad(0)), (-2.0, attn_ready), (g1, lambda: ffn_grad(1)), (g2, lambda: ffn_grad(2))]
     for m in range(3):
         for i, k in enumerate(order):
-            events.append((c.kg[0] + c.kg[1] * (m * n + i), lambda m=m, k=k: ffn_block(m, k)))
+            events.append((r0 + (m * n + i) * 8 / (n * per), lambda m=m, k=k: ffn_block(m, k)))
     for h in range(len(c.parts)):
-        events.append((c.kg[2] * h, lambda h=h: (part_grad(h), stage(h, 0))))
-        for bit in range(1, lowest(0, n)):
-            events.append((c.kg[3] + c.kg[4] * h + c.kg[5] * (bit - 1), lambda h=h, bit=bit: stage(h, bit)))
-        events.append((c.kg[3] + c.kg[4] * h + c.kg[5] * (lowest(0, n) - 1), lambda h=h: last(h)))
+        events.append((h, lambda h=h: (part_grad(h), stage(h, 0))))
+        for bit in range(1, top):
+            events.append((h + lag[min(bit, len(lag)) - 1], lambda h=h, bit=bit: stage(h, bit)))
+        events.append((h + lag[-1] + 0.01, lambda h=h: last(h)))
     for _, run in sorted(events, key=lambda e: e[0]):
         run()
     shared = pl.ds(c.qkv + c.heads, c.small)
-    o.ssend[...] = o.gp_v[:, shared].astype(BF)
-    rest = rcopy(o.ssend, o.sgot, o.ss.at[0], o.sr.at[0], pair)
+    rest = rcopy(o.gp_v.at[:, shared], o.sgot, o.ss.at[0], o.sr.at[0], pair)
     rest.start()
     rest.wait()
-    o.gp_v[:, shared] += o.sgot[...].astype(F32)
+    o.gp_v[:, shared] = (o.gp_v[:, shared].astype(F32) + o.sgot[...].astype(F32)).astype(BF)
     out = local(o.gp_v, o.gp)
     for m in range(3):
         for k in range(n):
@@ -1198,8 +1259,8 @@
         copy.wait()
 
 
-def fetch_weights(c, pack, gate, up, down):
-    n, A, q = c.n, c.n // 2, len(c.cuts)
+def fetch_weights(c, arrays, gains):
+    n, q = c.n, len(c.cuts)
     outs = dict(
         pk=((c.width, c.total), BF),
         gw=((c.width, 2 * c.hb), BF),
@@ -1209,23 +1270,26 @@
     )
     scratch = dict(
         gcol=pltpu.VMEM((c.width, LANES), BF),
+        grow_v=pltpu.VMEM((8, c.width), F32),
         pack_v=pltpu.VMEM((c.R, c.total), BF),
+        out_v=pltpu.VMEM((c.heads, c.R), BF),
+        lp_v=pltpu.VMEM((c.per, c.R), BF),
+        lr_v=pltpu.VMEM((c.rank, c.R), BF),
+        rows_v=pltpu.VMEM((LANES, c.R), F32),
+        down_v=pltpu.VMEM((n * c.hb, c.R), BF),
+        down_t=pltpu.VMEM((c.R, n * c.hb), BF),
         block_v=pltpu.VMEM((3, c.R, c.hb), BF),
-        grow_v=pltpu.VMEM((8, c.width), F32),
-        gs=dma(n, q), gr=dma(n, q),
-        ts=dma(n, 3), tr=dma(n, 3), ys=dma(n, 3), yr=dma(n, 3), lsem=dma(12),
+        gs=dma(n, q), gr=dma(n, q), ts=dma(n, 3), tr=dma(n, 3), ys=dma(n, 3), yr=dma(n, 3), lsem=dma(24),
         go=pltpu.SemaphoreType.REGULAR,
     )
-    return launch(
-        lambda o: fetch_kernel(c, o), 6, dict(pack=pack, gate=gate, up=up, down=down), {}, outs, scratch
-    )
-
-
-def return_grads(c, f, g, gcol, dg, du, dd):
-    n, A = c.n, c.n // 2
+    return launch(lambda o: fetch_kernel(c, o), 6, arrays, gains, outs, scratch)
+
+
+def return_grads(c, f, g, gcol):
+    n = c.n
     R = c.R
     flat = ((R, n * c.hb), BF)
-    outs = dict(gp=((R, c.total), F32), gg=flat, gu=flat, gd=flat)
+    outs = dict(gp=((R, c.total), BF), gg=flat, gu=flat, gd=flat)
     arrays = dict(
         nfull=f.nfull, dqkv=g.dqkv, afull=g.afull, heads=f.heads, lrlow=g.lrlow, lmid=f.lmid, resid=f.resid,
         grlow=g.grlow, plow=g.plow, llow=f.llow, lmg=g.lmg, gcol=gcol,
@@ -1233,37 +1297,52 @@
     scratch = dict(
         acc=pltpu.VMEM((c.width, c.total), BF),
         got=pltpu.VMEM(((n - 1) * R, c.total), BF),
-        gp_v=pltpu.VMEM((R, c.total), F32),
+        gp_v=pltpu.VMEM((R, c.total), BF),
         fown=pltpu.VMEM((3, c.width, c.hb), BF),
         fgot=pltpu.VMEM((3, c.width, c.hb), BF),
-        ssend=pltpu.VMEM((R, c.small), BF),
+        fsend=pltpu.VMEM((3, c.width, c.hb), BF),
+        x_v=pltpu.VMEM(f.pfull.shape, BF),
+        y_v=pltpu.VMEM((2, *g.dgl.shape), BF),
         sgot=pltpu.VMEM((R, c.small), BF),
-        rlow_v=pltpu.VMEM(f.resid.shape, BF),
         ys=dma(3, n), yr=dma(3, n), ts=dma(3, n), tr=dma(3, n), ss=dma(1), sr=dma(1), lsem=dma(24),
+        rs=dma(len(c.parts), n), rr=dma(len(c.parts), n),
         **{name + TAIL: pltpu.VMEM(v.shape, v.dtype) for name, v in arrays.items()},
-        rs=dma(len(c.parts), n), rr=dma(len(c.parts), n),
-    )
-    return launch(lambda o: return_kernel(c, o), 7, dict(**arrays, dg=dg, du=du, dd=dd), {}, outs, scratch)
+    )
+    big = dict(pfull=f.pfull, dgl=g.dgl, dul=g.dul, dfull=g.dfull, geglu=f.geglu)
+    return launch(lambda o: return_kernel(c, o), 7, dict(**arrays, **big), {}, outs, scratch)
 
 
 def widen_kernel(c, o):
     local = Local(o.lsem)
-    loads = [local(o.gp, o.gp_v), local(o.gg, o.g_v.at[0]), local(o.gu, o.g_v.at[1]), local(o.gd, o.g_v.at[2])]
+    hb, R, rank = c.hb, c.R, c.rank
+    loads = [local(o.gp, o.gp_v), local(o.gd, o.g_v.at[2]), local(o.gg, o.g_v.at[0]), local(o.gu, o.g_v.at[1])]
     base = c.qkv + c.heads
     loads[0].wait()
+    o.f_v[...] = o.gp_v[:, pl.ds(0, c.qkv)].astype(F32)
     out = [
-        local(o.gp_v.at[:, pl.ds(0, c.heads)], o.q),
-        local(o.gp_v.at[:, pl.ds(c.heads, HEAD)], o.k),
-        local(o.gp_v.at[:, pl.ds(c.heads + HEAD, HEAD)], o.v),
-        local(o.gp_v.at[:, pl.ds(base, LANES)], o.left),
-        local(o.gp_v.at[:, pl.ds(base + 2 * LANES, c.per)], o.lg),
+        local(o.f_v.at[:, pl.ds(0, c.heads)], o.q),
+        local(o.f_v.at[:, pl.ds(c.heads, HEAD)], o.k),
+        local(o.f_v.at[:, pl.ds(c.heads + HEAD, HEAD)], o.v),
     ]
-    o.t_v[...] = o.gp_v[:, pl.ds(c.qkv, c.heads)].T
+    for i, (g, w) in enumerate(((0, o.wg), (1, o.wu))):
+        loads[2 + i].wait()
+        o.w_v[i] = o.g_v[g].astype(F32)
+        out.append(local(o.w_v.at[i], w))
+    loads[1].wait()
+    for k in range(c.n):
+        o.d_v[pl.ds(k * hb, hb), :] = o.g_v[2, :, pl.ds(k * hb, hb)].astype(F32).T
+    out.append(local(o.d_v, o.wd))
+    for i in range(0, c.heads, HEAD):
+        o.t_v[pl.ds(i, HEAD), :] = o.gp_v[:, pl.ds(c.qkv + i, HEAD)].astype(F32).T
     out.append(local(o.t_v, o.out))
-    for m in range(3):
-        loads[1 + m].wait()
-        o.w_v[m] = o.g_v[m].astype(F32)
-        out.append(local(o.w_v.at[m], (o.wg, o.wu, o.wd)[m]))
+    left = o.gp_v[:, pl.ds(base, LANES)].astype(F32)
+    o.ll[...] = left[:, :rank]
+    rows = left.T
+    for i, gain in enumerate((o.g0, o.g1, o.g2, o.g3, o.g4, o.g5, o.g6, o.g7)):
+        gain[...] = rows[rank + i : rank + i + 1, 0 : gain.shape[1]]
+    o.lr[...] = o.gp_v[:, pl.ds(base + LANES, LANES)].astype(F32).T[:rank]
+    o.lg[...] = o.gp_v[:, pl.ds(base + 2 * LANES, c.per)].astype(F32)
+    o.lp[...] = o.gp_v[:, pl.ds(base + 2 * LANES + c.per, c.per)].astype(F32).T
     for copy in out:
         copy.wait()
 
@@ -1271,18 +1350,20 @@
 def widen(c, done):
     R, wide = c.R, c.n * c.hb
     outs = dict(
-        q=((R, c.heads), F32), k=((R, HEAD), F32), v=((R, HEAD), F32), left=((R, LANES), F32), lg=((R, c.per), F32),
-        out=((c.heads, R), F32), wg=((R, wide), F32), wu=((R, wide), F32), wd=((R, wide), F32),
+        q=((R, c.heads), F32), k=((R, HEAD), F32), v=((R, HEAD), F32),
+        out=((c.heads, R), F32), wg=((R, wide), F32), wu=((R, wide), F32), wd=((wide, R), F32),
+    )
+    row, head = ((1, R), F32), ((1, HEAD // c.n), F32)
+    small = dict(
+        ll=((R, c.rank), F32), lr=((c.rank, R), F32), lg=((R, c.per), F32), lp=((c.per, R), F32),
+        g0=row, g1=row, g2=row, g3=row, g4=row, g5=row, g6=head, g7=head,
     )
     scratch = dict(
-        gp_v=pltpu.VMEM((R, c.total), F32), t_v=pltpu.VMEM((c.heads, R), F32),
-        g_v=pltpu.VMEM((3, R, wide), BF), w_v=pltpu.VMEM((3, R, wide), F32), lsem=dma(16),
-    )
-    return launch(lambda o: widen_kernel(c, o), None, done, {}, outs, scratch)
-
-
-def spread(gain, n, rows):
-    return jnp.pad(gain, (0, rows - gain.shape[0]))
+        gp_v=pltpu.VMEM((R, c.total), BF), f_v=pltpu.VMEM((R, c.qkv), F32), t_v=pltpu.VMEM((c.heads, R), F32),
+        g_v=pltpu.VMEM((3, R, wide), BF), w_v=pltpu.VMEM((2, R, wide), F32), d_v=pltpu.VMEM((wide, R), F32),
+        lsem=dma(16),
+    )
+    return launch(lambda o: widen_kernel(c, o), None, done, {}, outs, scratch, small)
 
 
 def body(
@@ -1305,27 +1386,22 @@
         total=qkv + heads + small, hb=gate_weight.shape[2] // n,
         cuts=((0, qkv), (qkv, heads), (qkv + heads, small)),
         parts=(*((i, 512) for i in range(0, qkv + heads, 512)), (base, small - per), (base + small - per, per)),
-        slots=2 if n <= 8 else 1, ag=(12.0, 6.0, 12.0), tr=(1.0, 2.5, 30.0, 3.0), by_matrix=True, kg=(6.0, 2.9, 2.0, 20.0, 12.0, 12.0),
+        slots=2 if n <= 8 else 1, ag=(12.0, 6.0, 12.0), tr=(1.0, 2.5, 30.0, 3.0), by_matrix=True, go_at=GO_AT, kg=KG,
         halves=tuple((h * width // HALVES, width // HALVES) for h in range(HALVES)),
     )
-    gains = jnp.stack(
-        [
-            input_gain[0], attention_gain[0], laurel_gain[0], prefeed_gain[0], postfeed_gain[0], layer_gain[0],
-            spread(query_gain[0], n, R), spread(key_norm_gain[0], n, R),
-        ],
-        axis=1,
-    )
-    pad = lambda v, k: jnp.pad(v, ((0, 0), (0, LANES - k)))
-    pack = jnp.concatenate(
-        [
-            query_weight[0], key_projection[0], value_projection[0], output_weight[0].T,
-            pad(jnp.concatenate([laurel_left[0], gains], axis=1), rank + 8), pad(laurel_right[0].T, rank),
-            layer_gate[0], layer_project[0].T,
-        ],
-        axis=1,
-    )
-    weights = fetch_weights(c, pack, gate_weight[0], up_weight[0], down_weight[0].T)
-    columns = weights.pop("grow")
+    weights = fetch_weights(
+        c,
+        dict(
+            query=query_weight[0], key=key_projection[0], value=value_projection[0], out=output_weight[0],
+            lr=laurel_right[0], lg=layer_gate[0], lp=layer_project[0],
+            gate=gate_weight[0], up=up_weight[0], down=down_weight[0],
+        ),
+        dict(
+            ll=laurel_left[0], g0=input_gain, g1=attention_gain, g2=laurel_gain, g3=prefeed_gain, g4=postfeed_gain,
+            g5=layer_gain, g6=query_gain, g7=key_norm_gain,
+        ),
+    )
+    columns = weights.pop(GROW)
     short = HEAD // n
     head_gains = columns[6:].reshape(2, n, R)[:, :, :short].reshape(2, HEAD)
     gain_rows = jnp.concatenate([columns[:6], jnp.pad(head_gains, ((0, 0), (0, width - HEAD)))], axis=0)
@@ -1345,45 +1421,34 @@
     grads = backward_pass(c, weights, data, tables, stash)
     f, g = SimpleNamespace(**stash), SimpleNamespace(**grads)
 
-    def pair_grad(inputs, outs):
-        inputs = inputs.reshape(-1, inputs.shape[-1])
-        return tn(inputs, outs.reshape(-1, outs.shape[-1])).astype(BF)
-
     sums = g.ggr[0] + g.ggr[1]
     head_sums = jnp.pad(sums[6:, :HEAD].reshape(2, n, short), ((0, 0), (0, 0), (0, R - short))).reshape(2, width)
     gain_cols = jnp.concatenate([sums[:6], head_sums], axis=0).T
     gcol = jnp.pad(gain_cols, ((0, 0), (rank, LANES - rank - 8))).astype(BF)
-    done = return_grads(
-        c, f, g, gcol, pair_grad(f.pfull, g.dgl), pair_grad(f.pfull, g.dul), pair_grad(g.dfull, f.geglu)
-    )
-    w = SimpleNamespace(**widen(c, done))
-    gp = done["gp"]
-    base = qkv + heads
-    gain_out = w.left[:, rank : rank + 8].T
-    one = lambda i: gain_out[i][None]
+    w = SimpleNamespace(**widen(c, return_grads(c, f, g, gcol)))
     return (
         f.act[None, :, None],
         g.igrad[None, :, None],
         g.lgrad[None, :, None],
-        one(0),
+        w.g0,
         w.q[None],
         w.k[None],
         w.v[None],
-        gain_out[6, :short][None],
-        gain_out[7, :short][None],
+        w.g6,
+        w.g7,
         w.out[None],
-        one(1),
-        w.left[:, :rank][None],
-        gp[:, base + LANES : base + LANES + rank].T[None],
-        one(2),
-        one(3),
+        w.g1,
+        w.ll[None],
+        w.lr[None],
+        w.g2,
+        w.g3,
         w.wg[None],
         w.wu[None],
-        w.wd.T[None],
-        one(4),
+        w.wd[None],
+        w.g4,
         w.lg[None],
-        gp[:, base + 2 * LANES + per :].T[None],
-        one(5),
+        w.lp[None],
+        w.g5,
     )
 
 

time: 836 us -> 803 us (0.961)
  local copies, waits for them, and re-layouts: 36.4 us -> 7.91 us
  matrix products: 20.9 us -> 0 us
  Pallas kernels: 759 us -> 774 us
    dot_general x3 -> x0, matrix products: 20.9 us -> none  [tn(): lax.dot_general(x, w, (((0,), (0,)), ((), ())), preferred_element_type=F32)]
    unnamed x56 -> x14, local copies, waits for them, and re-layouts: 23.3 us -> 5.6 us
    pallas_call x5, Pallas kernels: 759 us -> 774 us  [launch(): pl.pallas_call(run, out_shape=[jax.ShapeDtypeStruct(*spec) for spec in (*...]
where the time goes in v3:
time: 803 us; the launch traced here: 790 us
  Pallas kernels  774 us (96%)
    pallas_call x5, Pallas kernels, launch(): pl.pallas_call(run, out_shape=[jax.ShapeDtypeStruct(*spec) for spec in (*...  774 us

profile of v3, /device:TPU:0, one launch (start us, length us, event | category | flops | bytes accessed | tf_op | source)
XLA Modules:
  0.0 789.9 jit_solution(18288949165387662242)
XLA Ops:
  0.7 0.7 add_bitcast_fusion
  1.3 0.7 compare_and_fusion
  2.1 1.5 copy.51
  3.6 0.8 or_convert_fusion.refs_9_.refs_19_
  4.3 0.9 fusion
  5.2 168.1 %shard_map.393 = (bf16[2048,3328]{1,0:T(8,128)(2,1)}, bf16[2048,1024]{1,0:T(8,128)(2,1)}, bf16[2048,1024]{1,0:T(8,128)(2,1)}, bf16[2048,1024]{1,0:T(8,128)(2,1)}, f32[8,2048]{1,0:T(8,128)}) custom-call(bf16[256,1024]{1,0:T(8,128)(2,1)} %bitcast.56, bf16[256,256]{1,0:T(8,128)(2,1)} %bitcast.63, bf16[256,256]{1,0:T(8,128)(2,1)} %bitcast.64, ...), custom_call_target="tpu_custom_call" | custom-call | tf_op jit(solution)/shard_map/pallas_call | solution.py:309
  173.4 0.8 slice.27
  174.3 0.1 reshape.162
  174.3 1.5 select_maximum_fusion.refs_6_.refs_16_
  175.8 124.6 %shard_map.394 = (bf16[2,64,2048]{2,1,0:T(8,128)(2,1)}, bf16[2,64,2048]{2,1,0:T(8,128)(2,1)}, bf16[2,128,2048]{2,1,0:T(8,128)(2,1)}, f32[2,128,1536]{2,1,0:T(8,1...) custom-call(bf16[2048,3328]{1,0:T(8,128)(2,1)} %get-tuple-element.80, ...), custom_call_target="tpu_custom_call" | custom-call | tf_op jit(solution)/shard_map/pallas_call | solution.py:309
  300.4 302.1 %shard_map.395 = (f32[2,64,2048]{2,1,0:T(8,128)}, f32[2,64,256]{2,1,0:T(8,128)}, bf16[2,64,2048]{2,1,0:T(8,128)(2,1)}, bf16[2,64,256]{2,1,0:T(8,128)(2,1)}, bf16...) custom-call(bf16[2048,3328]{1,0:T(8,128)(2,1)} %get-tuple-element.80, ...), custom_call_target="tpu_custom_call" | custom-call | tf_op jit(solution)/shard_map/pallas_call | solution.py:309
  602.5 0.9 fusion.2
  603.4 0.9 add_convert_fusion
  604.3 0.1 reshape.163
  604.4 0.3 copy.52
  604.7 1.0 pad.16.refs_11_
  605.7 170.1 %shard_map.396 = (bf16[256,3328]{1,0:T(8,128)(2,1)}, bf16[256,4096]{1,0:T(8,128)(2,1)}, bf16[256,4096]{1,0:T(8,128)(2,1)}, bf16[256,4096]{1,0:T(8,128)(2,1)}) custom-call(bf16[2,128,2048]{2,1,0:T(8,128)(2,1)} %get-tuple-element.98.refs_0_, bf16[2,128,1536]{2,1,0:T(8,128)(2,1)} %get-tuple-element.99.refs_1_, ...), custom_call_target="tpu_custom_call" | custom-call | tf_op jit(solution)/shard_map/pallas_call | solution.py:309
  775.8 0.0 copy-start.1
  775.8 0.0 copy-start
  775.8 9.5 %shard_map.397 = (f32[256,1024]{1,0:T(8,128)}, f32[256,256]{1,0:T(8,128)}, f32[256,256]{1,0:T(8,128)}, f32[1024,256]{1,0:T(8,128)}, f32[256,4096]{1,0:T(8,128)},...) custom-call(bf16[256,3328]{1,0:T(8,128)(2,1)} %get-tuple-element.115, ...), custom_call_target="tpu_custom_call" | custom-call | tf_op jit(solution)/shard_map/pallas_call | solution.py:309
  785.3 0.0 copy-start.2
  785.3 1.7 copy.56
  787.0 0.0 copy-done.1
  787.0 0.8 copy.64
  787.8 0.0 copy-done
  787.8 1.0 copy.65
  788.8 0.0 copy-done.2
  788.8 0.7 copy.66
  (9 shorter events, 0.1 us)
Async XLA Ops:
  775.8 11.2 %copy-start.1 = (bf16[2,64,2048]{2,1,0:T(8,128)(2,1)S(1)}, bf16[2,64,2048]{2,1,0:T(8,128)(2,1)}, u32[]{:S(2)}) copy-start(bf16[2,64,2048]{2,1,0:T(8,128)(2,1)} %get-tuple-element.85) | copy-start | bytes 1572868
  775.8 11.9 %copy-start = (f32[2,64,2048]{2,1,0:T(8,128)S(1)}, f32[2,64,2048]{2,1,0:T(8,128)}, u32[]{:S(2)}) copy-start(f32[2,64,2048]{2,1,0:T(8,128)} %get-tuple-element.96) | copy-start | bytes 3145732
  785.3 3.4 copy-start.2

commit v4 on v3

--- a/solution.py
+++ b/solution.py
@@ -23,6 +23,7 @@
 HALVES = 2
 GATHER_PARTS = 2
 GO_AT = 60.0
+SHARED = 1
 KG = (2.5, 3.0, (2.1, 3.2, 4.3), 0.6, 2.6)
 
 
@@ -234,12 +235,9 @@
     return result
 
 
-def cube_scatter(p, acc, got, size, cuts, sems, out):
+def cube_scatter(p, acc, got, size, cols, slots, sems, out):
     send, recv = sems
     n = p.n
-
-    def cols(h):
-        return pl.ds(cuts[h][0], cuts[h][1])
 
     def block(mask):
         return rows_of(flip(p.d, mask), size)
@@ -248,7 +246,7 @@
         bit = lowest(mask, n)
         return rcopy(
             acc.at[block(mask), cols(h)],
-            got.at[pl.ds((mask - 1) * size, size), cols(h)],
+            got.at[pl.ds((mask - 1) * size, size), slots(h)],
             send.at[h, mask],
             recv.at[h, mask],
             (p.s, flip(p.d, 1 << bit), p.t),
@@ -262,7 +260,7 @@
                 for below in range(bit):
                     came = mask | 1 << below
                     message(h, came).wait_recv()
-                    term = got[pl.ds((came - 1) * size, size), cols(h)].astype(F32)
+                    term = got[pl.ds((came - 1) * size, size), slots(h)].astype(F32)
                     total = term if total is None else total + term
                 if total is not None:
                     acc[at] = (acc[at].astype(F32) + total).astype(BF)
@@ -272,7 +270,7 @@
         total = acc[block(0), cols(h)].astype(F32)
         for below in range(lowest(0, n)):
             message(h, 1 << below).wait_recv()
-            total = total + got[pl.ds(((1 << below) - 1) * size, size), cols(h)].astype(F32)
+            total = total + got[pl.ds(((1 << below) - 1) * size, size), slots(h)].astype(F32)
         out[:, cols(h)] = total.astype(BF)
 
     def finish(h):
@@ -344,14 +342,25 @@
     local = Local(o.lsem)
     waits = []
 
+    def half(t):
+        size = c.small // 2
+        return pl.ds(pl.multiple_of(c.qkv + c.heads + t * size, LANES), size)
+
+    def cols(q):
+        return half(p.t) if q == SHARED else pl.ds(*cuts[q])
+
+    def mirror(mask, t):
+        at = (rows_of(flip(p.d, mask), R), half(t))
+        return rcopy(o.pk.at[at], o.pk.at[at], o.ms.at[mask], o.mr.at[mask], pair)
+
     def give(mask, bit, q):
-        rows, cs = rows_of(flip(p.d, mask), R), pl.ds(*cuts[q])
+        rows, cs = rows_of(flip(p.d, mask), R), cols(q)
         src = o.pk.at[rows, cs] if mask else o.pack_v.at[:, cs]
         far = mask | 1 << bit
         return rcopy(src, o.pk.at[rows, cs], o.gs.at[far, q], o.gr.at[far, q], (p.s, flip(p.d, 1 << bit), p.t))
 
     def taken(mask, q):
-        at = (rows_of(flip(p.d, mask), R), pl.ds(*cuts[q]))
+        at = (rows_of(flip(p.d, mask), R), cols(q))
         return rcopy(o.pk.at[at], o.pk.at[at], o.gs.at[mask, q], o.gr.at[mask, q], side)
 
     def pass_on(mask, q):
@@ -359,6 +368,8 @@
             taken(mask, q).wait_recv()
         for bit in reversed(range(lowest(mask, n))):
             give(mask, bit, q).start()
+        if mask and q == SHARED:
+            mirror(mask, p.t).start()
 
     ffn = ((o.gate, o.gw), (o.up, o.uw), (o.down_t, o.dw))
 
@@ -400,7 +411,7 @@
         if q == 0:
             for copy in first:
                 copy.wait()
-        elif q == 1:
+        elif q == 2:
             for copy in second:
                 copy.wait()
             for i in range(0, c.heads, HEAD):
@@ -453,9 +464,16 @@
     for m in range(3):
         waits.append(local(o.block_v.at[m], block(m, p.d, p.t)))
 
+    for mask in range(1, n, 2):
+        taken(mask, SHARED).wait_recv()
+        mirror(mask, p.t).start()
     for q in range(len(cuts)):
         for mask in range(1, n, 2):
-            taken(mask, q).wait_recv()
+            if q != SHARED:
+                taken(mask, q).wait_recv()
+    for mask in range(1, n):
+        mirror(mask, 1 - p.t).wait_recv()
+        mirror(mask, p.t).wait_send()
     for k in range(n):
         for m in range(3):
             share(m, k, 1 - p.t).wait_recv()
@@ -1181,7 +1199,20 @@
         local(getattr(o, name), getattr(o, name + TAIL))
         for name in ("nfull", "dqkv", "afull", "heads", "lrlow", "lmid", "resid", "grlow", "plow", "llow", "lmg", "gcol")
     ]
-    stage, last, finish = cube_scatter(p, o.acc, o.got, R, c.parts, (o.rs, o.rr), o.gp_v)
+    base = c.qkv + c.heads
+
+    def half(t):
+        size = c.small // 2
+        return pl.ds(pl.multiple_of(base + t * size, LANES), size)
+
+    def slots(h):
+        return pl.ds(*c.parts[h])
+
+    def cols(h):
+        return half(p.t) if c.parts[h][0] == base else slots(h)
+
+    stage, last, finish = cube_scatter(p, o.acc, o.got, R, cols, slots, (o.rs, o.rr), o.gp_v)
+    merge = rcopy(o.acc.at[:, half(1 - p.t)], o.sgot, o.ss.at[0], o.sr.at[0], pair)
     mine_copies = []
 
     def grad(x, y, at, block=512):
@@ -1204,25 +1235,32 @@
 
     def part_grad(h):
         begin, size = c.parts[h]
-        base = c.qkv + c.heads
         if begin < c.qkv:
             grad(o.nfull_v, o.dqkv_v.at[:, :, pl.ds(begin, size)], pl.ds(begin, size))
         elif begin < base:
             grad(o.afull_v, o.heads_v.at[:, :, pl.ds(begin - c.qkv, size)], pl.ds(begin, size))
-        elif begin == base:
-            mine = rows_of(p.t, c.r)
-            lane = lax.broadcasted_iota(jnp.int32, (512, LANES), 1)
+        else:
+            merge.wait()
 
             @tiles(c.width, 512)
             def _(rows):
-                left = tn(o.nfull_v[0, mine, rows], o.lmg_v[0]) + tn(o.nfull_v[1, mine, rows], o.lmg_v[1])
-                gains = o.gcol_v[rows, :].astype(F32)
-                o.acc[rows, pl.ds(begin, LANES)] = jnp.where(lane < c.rank, left, gains).astype(BF)
-
-            grad(o.lrlow_v, o.lmid_v, pl.ds(begin + LANES, LANES))
-            grad(o.resid_v, o.grlow_v, pl.ds(begin + 2 * LANES, c.per))
-        else:
-            grad(o.plow_v, o.llow_v, pl.ds(begin, c.per))
+                at = (rows, half(p.t))
+                o.acc[at] = (o.acc[at].astype(F32) + o.sgot[rows, :].astype(F32)).astype(BF)
+
+    def shared_grad():
+        mine = rows_of(p.t, c.r)
+        lane = lax.broadcasted_iota(jnp.int32, (512, LANES), 1)
+
+        @tiles(c.width, 512)
+        def _(rows):
+            left = tn(o.nfull_v[0, mine, rows], o.lmg_v[0]) + tn(o.nfull_v[1, mine, rows], o.lmg_v[1])
+            gains = o.gcol_v[rows, :].astype(F32)
+            o.acc[rows, pl.ds(base, LANES)] = jnp.where(lane < c.rank, left, gains).astype(BF)
+
+        grad(o.lrlow_v, o.lmid_v, pl.ds(base + LANES, LANES))
+        grad(o.resid_v, o.grlow_v, pl.ds(base + 2 * LANES, c.per))
+        grad(o.plow_v, o.llow_v, pl.ds(base + 2 * LANES + c.per, c.per))
+        merge.start()
 
     def attn_ready():
         for copy in need:
@@ -1230,7 +1268,7 @@
 
     r0, per, lag, g1, g2 = c.kg
     top = lowest(0, n)
-    events = [(-3.0, lambda: ffn_grad(0)), (-2.0, attn_ready), (g1, lambda: ffn_grad(1)), (g2, lambda: ffn_grad(2))]
+    events = [(-3.0, lambda: ffn_grad(0)), (-2.0, attn_ready), (1.3, shared_grad), (g1, lambda: ffn_grad(1)), (g2, lambda: ffn_grad(2))]
     for m in range(3):
         for i, k in enumerate(order):
             events.append((r0 + (m * n + i) * 8 / (n * per), lambda m=m, k=k: ffn_block(m, k)))
@@ -1241,11 +1279,11 @@
         events.append((h + lag[-1] + 0.01, lambda h=h: last(h)))
     for _, run in sorted(events, key=lambda e: e[0]):
         run()
-    shared = pl.ds(c.qkv + c.heads, c.small)
-    rest = rcopy(o.gp_v.at[:, shared], o.sgot, o.ss.at[0], o.sr.at[0], pair)
+    rest = rcopy(o.gp_v.at[:, half(p.t)], o.gp_v.at[:, half(p.t)], o.ss.at[1], o.sr.at[1], pair)
     rest.start()
-    rest.wait()
-    o.gp_v[:, shared] = (o.gp_v[:, shared].astype(F32) + o.sgot[...].astype(F32)).astype(BF)
+    rest.wait_send()
+    theirs = o.gp_v.at[:, half(1 - p.t)]
+    rcopy(theirs, theirs, o.ss.at[1], o.sr.at[1], pair).wait_recv()
     out = local(o.gp_v, o.gp)
     for m in range(3):
         for k in range(n):
@@ -1279,7 +1317,7 @@
         down_v=pltpu.VMEM((n * c.hb, c.R), BF),
         down_t=pltpu.VMEM((c.R, n * c.hb), BF),
         block_v=pltpu.VMEM((3, c.R, c.hb), BF),
-        gs=dma(n, q), gr=dma(n, q), ts=dma(n, 3), tr=dma(n, 3), ys=dma(n, 3), yr=dma(n, 3), lsem=dma(24),
+        ms=dma(n), mr=dma(n), gs=dma(n, q), gr=dma(n, q), ts=dma(n, 3), tr=dma(n, 3), ys=dma(n, 3), yr=dma(n, 3), lsem=dma(24),
         go=pltpu.SemaphoreType.REGULAR,
     )
     return launch(lambda o: fetch_kernel(c, o), 6, arrays, gains, outs, scratch)
@@ -1296,15 +1334,15 @@
     )
     scratch = dict(
         acc=pltpu.VMEM((c.width, c.total), BF),
-        got=pltpu.VMEM(((n - 1) * R, c.total), BF),
+        got=pltpu.VMEM(((n - 1) * R, c.total - c.small // 2), BF),
         gp_v=pltpu.VMEM((R, c.total), BF),
         fown=pltpu.VMEM((3, c.width, c.hb), BF),
         fgot=pltpu.VMEM((3, c.width, c.hb), BF),
         fsend=pltpu.VMEM((3, c.width, c.hb), BF),
         x_v=pltpu.VMEM(f.pfull.shape, BF),
         y_v=pltpu.VMEM((2, *g.dgl.shape), BF),
-        sgot=pltpu.VMEM((R, c.small), BF),
-        ys=dma(3, n), yr=dma(3, n), ts=dma(3, n), tr=dma(3, n), ss=dma(1), sr=dma(1), lsem=dma(24),
+        sgot=pltpu.VMEM((c.width, c.small // 2), BF),
+        ys=dma(3, n), yr=dma(3, n), ts=dma(3, n), tr=dma(3, n), ss=dma(2), sr=dma(2), lsem=dma(24),
         rs=dma(len(c.parts), n), rr=dma(len(c.parts), n),
         **{name + TAIL: pltpu.VMEM(v.shape, v.dtype) for name, v in arrays.items()},
     )
@@ -1384,8 +1422,8 @@
     c = SimpleNamespace(
         n=n, R=R, r=hidden.shape[2], width=width, heads=heads, qkv=qkv, per=per, small=small, rank=rank,
         total=qkv + heads + small, hb=gate_weight.shape[2] // n,
-        cuts=((0, qkv), (qkv, heads), (qkv + heads, small)),
-        parts=(*((i, 512) for i in range(0, qkv + heads, 512)), (base, small - per), (base + small - per, per)),
+        cuts=((0, qkv), (base, small), (qkv, heads)),
+        parts=(*((i, 512) for i in range(0, base, 512)), (base, small // 2)),
         slots=2 if n <= 8 else 1, ag=(12.0, 6.0, 12.0), tr=(1.0, 2.5, 30.0, 3.0), by_matrix=True, go_at=GO_AT, kg=KG,
         halves=tuple((h * width // HALVES, width // HALVES) for h in range(HALVES)),
     )

time: 803 us -> 784 us (0.976)
  Pallas kernels: 774 us -> 760 us
    pallas_call x5, Pallas kernels: 774 us -> 760 us  [launch(): pl.pallas_call(run, out_shape=[jax.ShapeDtypeStruct(*spec) for spec in (*...]
where the time goes in v4:
time: 784 us; the launch traced here: 775 us
  Pallas kernels  760 us (97%)
  local copies, waits for them, and re-layouts  7.91 us (1%)
    pallas_call x5, Pallas kernels, launch(): pl.pallas_call(run, out_shape=[jax.ShapeDtypeStruct(*spec) for spec in (*...  760 us

profile of v4, /device:TPU:0, one launch (start us, length us, event | category | flops | bytes accessed | tf_op | source)
XLA Modules:
  0.0 775.4 jit_solution(4311298075790231978)
XLA Ops:
  0.7 0.7 add_bitcast_fusion
  1.3 0.7 compare_and_fusion
  2.1 1.5 copy.51
  3.6 0.8 or_convert_fusion.refs_9_.refs_19_
  4.3 0.9 fusion
  5.2 168.1 %shard_map.393 = (bf16[2048,3328]{1,0:T(8,128)(2,1)}, bf16[2048,1024]{1,0:T(8,128)(2,1)}, bf16[2048,1024]{1,0:T(8,128)(2,1)}, bf16[2048,1024]{1,0:T(8,128)(2,1)}, f32[8,2048]{1,0:T(8,128)}) custom-call(bf16[256,1024]{1,0:T(8,128)(2,1)} %bitcast.56, bf16[256,256]{1,0:T(8,128)(2,1)} %bitcast.63, bf16[256,256]{1,0:T(8,128)(2,1)} %bitcast.64, ...), custom_call_target="tpu_custom_call" | custom-call | tf_op jit(solution)/shard_map/pallas_call | solution.py:307
  173.4 0.8 slice.27
  174.2 0.1 reshape.162
  174.3 1.5 select_maximum_fusion.refs_6_.refs_16_
  175.8 112.9 %shard_map.394 = (bf16[2,64,2048]{2,1,0:T(8,128)(2,1)}, bf16[2,64,2048]{2,1,0:T(8,128)(2,1)}, bf16[2,128,2048]{2,1,0:T(8,128)(2,1)}, f32[2,128,1536]{2,1,0:T(8,1...) custom-call(bf16[2048,3328]{1,0:T(8,128)(2,1)} %get-tuple-element.80, ...), custom_call_target="tpu_custom_call" | custom-call | tf_op jit(solution)/shard_map/pallas_call | solution.py:307
  288.7 305.8 %shard_map.395 = (f32[2,64,2048]{2,1,0:T(8,128)}, f32[2,64,256]{2,1,0:T(8,128)}, bf16[2,64,2048]{2,1,0:T(8,128)(2,1)}, bf16[2,64,256]{2,1,0:T(8,128)(2,1)}, bf16...) custom-call(bf16[2048,3328]{1,0:T(8,128)(2,1)} %get-tuple-element.80, ...), custom_call_target="tpu_custom_call" | custom-call | tf_op jit(solution)/shard_map/pallas_call | solution.py:307
  594.5 0.9 fusion.2
  595.4 0.9 add_convert_fusion
  596.3 0.1 reshape.163
  596.4 0.3 copy.52
  596.7 1.0 pad.16.refs_11_
  597.7 163.7 %shard_map.396 = (bf16[256,3328]{1,0:T(8,128)(2,1)}, bf16[256,4096]{1,0:T(8,128)(2,1)}, bf16[256,4096]{1,0:T(8,128)(2,1)}, bf16[256,4096]{1,0:T(8,128)(2,1)}) custom-call(bf16[2,128,2048]{2,1,0:T(8,128)(2,1)} %get-tuple-element.98.refs_0_, bf16[2,128,1536]{2,1,0:T(8,128)(2,1)} %get-tuple-element.99.refs_1_, ...), custom_call_target="tpu_custom_call" | custom-call | tf_op jit(solution)/shard_map/pallas_call | solution.py:307
  761.4 0.0 copy-start.1
  761.4 0.0 copy-start
  761.4 9.5 %shard_map.397 = (f32[256,1024]{1,0:T(8,128)}, f32[256,256]{1,0:T(8,128)}, f32[256,256]{1,0:T(8,128)}, f32[1024,256]{1,0:T(8,128)}, f32[256,4096]{1,0:T(8,128)},...) custom-call(bf16[256,3328]{1,0:T(8,128)(2,1)} %get-tuple-element.115, ...), custom_call_target="tpu_custom_call" | custom-call | tf_op jit(solution)/shard_map/pallas_call | solution.py:307
  770.9 0.0 copy-start.2
  770.9 1.7 copy.56
  772.6 0.0 copy-done.1
  772.6 0.8 copy.64
  773.4 0.0 copy-done
  773.4 1.0 copy.65
  774.3 0.0 copy-done.2
  774.3 0.7 copy.66
  (9 shorter events, 0.1 us)
Async XLA Ops:
  761.4 11.2 %copy-start.1 = (bf16[2,64,2048]{2,1,0:T(8,128)(2,1)S(1)}, bf16[2,64,2048]{2,1,0:T(8,128)(2,1)}, u32[]{:S(2)}) copy-start(bf16[2,64,2048]{2,1,0:T(8,128)(2,1)} %get-tuple-element.85) | copy-start | bytes 1572868
  761.4 11.9 %copy-start = (f32[2,64,2048]{2,1,0:T(8,128)S(1)}, f32[2,64,2048]{2,1,0:T(8,128)}, u32[]{:S(2)}) copy-start(f32[2,64,2048]{2,1,0:T(8,128)} %get-tuple-element.96) | copy-start | bytes 3145732
  770.9 3.4 copy-start.2

commit v5 on v4

--- a/solution.py
+++ b/solution.py
@@ -1069,7 +1069,7 @@
 
 BACKWARD_ORDER = (
     (FIRST, 0), (GIVE, 0), (OWN, 0), (FIRST, 1), (REST, 0), (GIVE, 1), (OWN, 1), (SUMS, 0), (REST, 1), (MIDDLE, 0),
-    (HEADS_STAGE, 0), (SUMS, 1), (ENTRY, 0), (MIDDLE, 1), (HEADS_STAGE, 1), (ENTRY, 1),
+    (SUMS, 1), (HEADS_STAGE, 0), (ENTRY, 0), (MIDDLE, 1), (HEADS_STAGE, 1), (ENTRY, 1),
 )
 
 

time: 784 us -> 771 us (0.983)
  Pallas kernels: 760 us -> 746 us
    pallas_call x5, Pallas kernels: 760 us -> 746 us  [launch(): pl.pallas_call(run, out_shape=[jax.ShapeDtypeStruct(*spec) for spec in (*...]
where the time goes in v5:
time: 771 us; the launch traced here: 762 us
  Pallas kernels  746 us (97%)
  local copies, waits for them, and re-layouts  7.91 us (1%)
    pallas_call x5, Pallas kernels, launch(): pl.pallas_call(run, out_shape=[jax.ShapeDtypeStruct(*spec) for spec in (*...  746 us

profile of v5, /device:TPU:0, one launch (start us, length us, event | category | flops | bytes accessed | tf_op | source)
XLA Modules:
  0.0 761.5 jit_solution(8106605691690693241)
XLA Ops:
  0.7 0.7 add_bitcast_fusion
  1.3 0.7 compare_and_fusion
  2.1 1.5 copy.51
  3.6 0.8 or_convert_fusion.refs_9_.refs_19_
  4.3 0.9 fusion
  5.2 168.1 %shard_map.393 = (bf16[2048,3328]{1,0:T(8,128)(2,1)}, bf16[2048,1024]{1,0:T(8,128)(2,1)}, bf16[2048,1024]{1,0:T(8,128)(2,1)}, bf16[2048,1024]{1,0:T(8,128)(2,1)}, f32[8,2048]{1,0:T(8,128)}) custom-call(bf16[256,1024]{1,0:T(8,128)(2,1)} %bitcast.56, bf16[256,256]{1,0:T(8,128)(2,1)} %bitcast.63, bf16[256,256]{1,0:T(8,128)(2,1)} %bitcast.64, ...), custom_call_target="tpu_custom_call" | custom-call | tf_op jit(solution)/shard_map/pallas_call | solution.py:307
  173.4 0.8 slice.27
  174.2 0.1 reshape.162
  174.3 1.5 select_maximum_fusion.refs_6_.refs_16_
  175.8 112.9 %shard_map.394 = (bf16[2,64,2048]{2,1,0:T(8,128)(2,1)}, bf16[2,64,2048]{2,1,0:T(8,128)(2,1)}, bf16[2,128,2048]{2,1,0:T(8,128)(2,1)}, f32[2,128,1536]{2,1,0:T(8,1...) custom-call(bf16[2048,3328]{1,0:T(8,128)(2,1)} %get-tuple-element.80, ...), custom_call_target="tpu_custom_call" | custom-call | tf_op jit(solution)/shard_map/pallas_call | solution.py:307
  288.7 289.1 %shard_map.395 = (f32[2,64,2048]{2,1,0:T(8,128)}, f32[2,64,256]{2,1,0:T(8,128)}, bf16[2,64,2048]{2,1,0:T(8,128)(2,1)}, bf16[2,64,256]{2,1,0:T(8,128)(2,1)}, bf16...) custom-call(bf16[2048,3328]{1,0:T(8,128)(2,1)} %get-tuple-element.80, ...), custom_call_target="tpu_custom_call" | custom-call | tf_op jit(solution)/shard_map/pallas_call | solution.py:307
  577.8 0.9 fusion.2
  578.6 0.9 add_convert_fusion
  579.6 0.1 reshape.163
  579.7 0.3 copy.52
  580.0 1.0 pad.16.refs_11_
  581.0 166.5 %shard_map.396 = (bf16[256,3328]{1,0:T(8,128)(2,1)}, bf16[256,4096]{1,0:T(8,128)(2,1)}, bf16[256,4096]{1,0:T(8,128)(2,1)}, bf16[256,4096]{1,0:T(8,128)(2,1)}) custom-call(bf16[2,128,2048]{2,1,0:T(8,128)(2,1)} %get-tuple-element.98.refs_0_, bf16[2,128,1536]{2,1,0:T(8,128)(2,1)} %get-tuple-element.99.refs_1_, ...), custom_call_target="tpu_custom_call" | custom-call | tf_op jit(solution)/shard_map/pallas_call | solution.py:307
  747.5 0.0 copy-start.1
  747.5 0.0 copy-start
  747.5 9.5 %shard_map.397 = (f32[256,1024]{1,0:T(8,128)}, f32[256,256]{1,0:T(8,128)}, f32[256,256]{1,0:T(8,128)}, f32[1024,256]{1,0:T(8,128)}, f32[256,4096]{1,0:T(8,128)},...) custom-call(bf16[256,3328]{1,0:T(8,128)(2,1)} %get-tuple-element.115, ...), custom_call_target="tpu_custom_call" | custom-call | tf_op jit(solution)/shard_map/pallas_call | solution.py:307
  757.0 0.0 copy-start.2
  757.0 1.7 copy.56
  758.7 0.0 copy-done.1
  758.7 0.8 copy.64
  759.5 0.0 copy-done
  759.5 1.0 copy.65
  760.4 0.0 copy-done.2
  760.4 0.7 copy.66
  (9 shorter events, 0.1 us)
Async XLA Ops:
  747.5 11.2 %copy-start.1 = (bf16[2,64,2048]{2,1,0:T(8,128)(2,1)S(1)}, bf16[2,64,2048]{2,1,0:T(8,128)(2,1)}, u32[]{:S(2)}) copy-start(bf16[2,64,2048]{2,1,0:T(8,128)(2,1)} %get-tuple-element.85) | copy-start | bytes 1572868
  747.5 11.9 %copy-start = (f32[2,64,2048]{2,1,0:T(8,128)S(1)}, f32[2,64,2048]{2,1,0:T(8,128)}, u32[]{:S(2)}) copy-start(f32[2,64,2048]{2,1,0:T(8,128)} %get-tuple-element.96) | copy-start | bytes 3145732
  757.0 3.4 copy-start.2
